TPU v7x, 32 devices: a whole 2x2x4 slice. The times are simulated.
32 devices in a mesh: groups: 2 (over y), queue: 4 (over z), heads: 2 (over x), seq: 2 (over core).
Axes of the slice: x: 2, y: 2, z: 4, core: 2. Of those that a mesh axis runs over, the one named last changes fastest.
Arguments:
- latent: bfloat16 [32, 128, 5120], P(('groups', 'queue', 'seq'), None, 'heads'), parts along dimension 0, may hold values from -6 to 6
- projections: bfloat16 [3, 32, 128, 3072], P(None, ('groups', 'queue', 'seq'), None, 'heads'), parts along dimension 1, may hold values from -32 to 32
- frame_times: int32 [32], P(('groups', 'queue', 'seq')), parts along dimension 0, may hold values from 1 to 112, as said below
- levels: int32 [8], P(('groups', 'queue')), parts along dimension 0, may hold values from 0 to 49
- gates: bfloat16 [50, 5120], P(None, 'heads'), may hold values from -6 to 6
- out_weight: bfloat16 [3072, 5120], P('heads', 'queue'), may hold values from -0.109375 to 0.109375
- incoming_latent: bfloat16 [4, 128, 5120], P('groups', None, 'heads'), parts along dimension 0, may hold values from -6 to 6
- incoming_proj: bfloat16 [4, 3, 128, 3072], P('groups', None, None, 'heads'), parts along dimension 0, may hold values from -32 to 32
- incoming_times: int32 [4], P('groups'), parts along dimension 0, may hold values from 115 to 118, as said below
Outputs:
- advanced_latent: bfloat16 [32, 128, 5120], P(('groups', 'queue', 'seq'), None, 'heads'), parts along dimension 0
There are 2 independent parts, one for each index of `groups`. A program takes and returns all parts, laid end to end along the dimension named above; an argument that names none is the same for every part. Nothing has to cross between parts.
Inputs may be any that keep to these rules, and one draw needn't show every extreme that they name: `frame_times`: rise strictly from frame to frame. `incoming_times`: rise strictly and all exceed the last of frame_times.
All inputs are finite; a program needn't handle non-finite values.
Results may differ from a plain program's by a relative error of at most 0.011.
Values may be sent and summed in bfloat16 or wider, within the bound.
No kernel may reach another device: no remote copies, remote signals or barrier semaphores. Data moves between devices by JAX's collectives and lax.ppermute only.
A program may use at most 128 MiB of HBM per device.

v0:
```python
import math

import jax
import jax.numpy as jnp
from jax import lax
from jax.sharding import PartitionSpec as P

HD = 128
ADV = 2


def shifted(array, axis, by):
    count = lax.axis_size(axis)
    pairs = [(i, i + by) for i in range(count) if 0 <= i + by < count]
    return lax.ppermute(array, axis, pairs)


def padded_2(block, sides, width):
    for axis, dim in sides:
        count = lax.axis_size(axis)
        forward = [(i, i + 1) for i in range(count - 1)]
        backward = [(target, source) for source, target in forward]
        low = lax.ppermute(
            lax.slice_in_dim(block, block.shape[dim] - width, None, axis=dim), axis, forward
        )
        high = lax.ppermute(lax.slice_in_dim(block, 0, width, axis=dim), axis, backward)
        block = jnp.concatenate([low, block, high], axis=dim)
    return block


def rotate_pairs(block_in, times_in, head_dim):
    frames, tokens, channels = block_in.shape
    half_dim = head_dim // 2
    pair_index = jnp.arange(half_dim, dtype=jnp.float32)
    frequency = jnp.power(jnp.float32(10000.0), -pair_index / half_dim)
    angles = times_in.astype(jnp.float32)[:, None] * frequency[None, :]
    cosine = jnp.cos(angles)[:, None, None, :]
    sine_term = jnp.sin(angles)[:, None, None, :]
    head_view = block_in.astype(jnp.float32).reshape(frames, tokens, channels // head_dim, head_dim)
    first_half = head_view[..., :half_dim]
    second_half = head_view[..., half_dim:]
    turned = jnp.concatenate(
        [
            first_half * cosine - second_half * sine_term,
            second_half * cosine + first_half * sine_term,
        ],
        axis=-1,
    )
    return turned.reshape(frames, tokens, channels).astype(jnp.bfloat16)


def rotate_all(projection, times_in, head_dim):
    return jnp.stack(
        [
            rotate_pairs(projection[0], times_in, head_dim),
            rotate_pairs(projection[1], times_in, head_dim),
            projection[2],
        ]
    )


def attend(queries, key_rows, value_rows, usable, head_dim):
    row_count, channels = queries.shape
    head_count = channels // head_dim
    query_heads = queries.reshape(row_count, head_count, head_dim)
    key_heads = key_rows.reshape(-1, head_count, head_dim)
    value_heads = value_rows.reshape(-1, head_count, head_dim)
    scores = jnp.einsum(
        "rhd,khd->hrk", query_heads, key_heads, preferred_element_type=jnp.float32
    ) * (1.0 / math.sqrt(head_dim))
    scores = jnp.where(usable[None, None, :], scores, -1e30)
    row_top = jnp.max(scores, axis=-1, keepdims=True)
    weights = jnp.exp(scores - row_top)
    weights = (weights / jnp.sum(weights, axis=-1, keepdims=True)).astype(jnp.bfloat16)
    mixture = jnp.einsum("hrk,khd->rhd", weights, value_heads, preferred_element_type=jnp.float32)
    return mixture.reshape(row_count, channels).astype(jnp.bfloat16)


def local(
    latent,
    projections,
    frame_times,
    levels,
    gates,
    out_weight,
    incoming_latent,
    incoming_proj,
    incoming_times,
):
    queue_pos = lax.axis_index("queue")
    queue_count = lax.axis_size("queue")
    seq_pos = lax.axis_index("seq")
    seq_count = lax.axis_size("seq")
    last_core = jnp.logical_and(queue_pos == queue_count - 1, seq_pos == seq_count - 1)
    before_ok = queue_pos > 0
    after_ok = queue_pos < queue_count - 1
    level_row = (jnp.arange(gates.shape[0], dtype=jnp.int32) == levels[0]).astype(jnp.bfloat16)
    gate_row = jnp.dot(level_row[None, :], gates, preferred_element_type=jnp.float32)[0]
    frames = latent.shape[0]
    tokens = latent.shape[1]
    carried = rotate_all(projections, frame_times, HD)
    fresh_proj = rotate_all(jnp.transpose(incoming_proj, (1, 0, 2, 3)), incoming_times, HD)
    channels = carried.shape[-1]
    for advance in range(ADV):
        arrived_latent, arrived_proj = shifted((latent[0], carried[:, 0]), ("queue", "seq"), -1)
        arrived_latent = jnp.where(last_core, incoming_latent[advance], arrived_latent)
        arrived_proj = jnp.where(last_core, fresh_proj[:, advance], arrived_proj)
        latent = jnp.concatenate([latent[1:], arrived_latent[None]], axis=0)
        carried = jnp.concatenate([carried[:, 1:], arrived_proj[:, None]], axis=1)
        local_kv = carried[1:]
        window = lax.all_gather(local_kv, "seq", axis=1, tiled=True)
        padded = padded_2(window, (("queue", 1),), 1)
        key_rows = padded[0].reshape(-1, channels)
        value_rows = padded[1].reshape(-1, channels)
        inner_count = (padded.shape[1] - 2) * tokens
        usable = jnp.concatenate(
            [
                jnp.full((tokens,), before_ok),
                jnp.ones((inner_count,), dtype=bool),
                jnp.full((tokens,), after_ok),
            ]
        )
        mixture = attend(
            carried[0].reshape(frames * tokens, channels), key_rows, value_rows, usable, HD
        )
        partial_value = jnp.dot(
            mixture,
            lax.all_gather(out_weight, "queue", axis=1, tiled=True),
            preferred_element_type=jnp.float32,
        )
        update = lax.psum_scatter(
            partial_value.astype(jnp.bfloat16), "heads", scatter_dimension=1, tiled=True
        ).astype(jnp.float32)
        latent = (
            latent.astype(jnp.float32)
            + gate_row[None, None, :] * update.reshape(frames, tokens, -1)
        ).astype(jnp.bfloat16)
    return latent


def solution(mesh):
    return jax.shard_map(
        local,
        mesh=mesh,
        in_specs=(
            P(("groups", "queue", "seq"), None, "heads"),
            P(None, ("groups", "queue", "seq"), None, "heads"),
            P(("groups", "queue", "seq")),
            P(("groups", "queue")),
            P(None, "heads"),
            P("heads", "queue"),
            P("groups", None, "heads"),
            P("groups", None, None, "heads"),
            P("groups"),
        ),
        out_specs=P(("groups", "queue", "seq"), None, "heads"),
        check_vma=False,
    )
```

profile of v0, /device:TPU:9, one launch (start us, length us, event | category | flops | bytes accessed | tf_op | source)
XLA Modules:
  0.0 487.2 jit_solution(18271272105420340738)
XLA Ops:
  21.4 3.0 copy.36
  27.8 7.0 %collective-permute-done.1 = bf16[3,128,1536]{1,2,0:T(8,128)(2,1)} collective-permute-done((bf16[3,128,1536]{1,2,0:T(8,128)(2,1)}, bf16[3,128,1536]{1,2,0:T(8,128)(2,1)}, u32[]{:S(2)}, u32[]{:S(2)}) %collective-permute-start.1) | collective-permute-done | bytes 1179680 | tf_op jit(solution)/shard_map/ppermute | solution.py:15
  34.8 12.6 %collective-permute-done.5 = bf16[3,128,1536]{1,2,0:T(8,128)(2,1)} collective-permute-done((bf16[3,128,1536]{1,2,0:T(8,128)(2,1)}, bf16[3,128,1536]{1,2,0:T(8,128)(2,1)}, u32[]{:S(2)}, u32[]{:S(2)}) %collective-permute-start.5) | collective-permute-done | bytes 1179680 | tf_op jit(solution)/shard_map/ppermute | solution.py:15
  51.3 2.6 copy.39
  57.5 9.1 %all-gather.4.cloned.1.call-done = bf16[2,4,128,1536]{3,2,0,1:T(8,128)(2,1)} async-done(((bf16[2,2,128,1536]{3,2,0,1:T(8,128)(2,1)}), bf16[2,4,128,1536]{3,2,0,1:T(8,128)(2,1)}) %all-gather.4.cloned.1.call-update) | async-done | bytes 3145744 | tf_op jit(solution)/shard_map/all_gather | solution.py:111
  66.6 2.8 fusion.46
  69.4 3.3 collective-permute-start.2
  72.9 6.5 %copy.45 = bf16[1,2,128,1536]{2,1,3,0:T(2,128)(2,1)S(1)} copy(bf16[1,2,128,1536]{2,3,0,1:T(8,128)(2,1)S(1)} %get-tuple-element.39) | data formatting | bytes 1572864 | tf_op jit(solution)/shard_map/slice | solution.py:124
  80.8 6.5 %copy.40 = bf16[1,2,128,1536]{2,1,3,0:T(2,128)(2,1)S(1)} copy(bf16[1,2,128,1536]{2,3,0,1:T(8,128)(2,1)S(1)} %get-tuple-element.38) | data formatting | bytes 1572864 | tf_op jit(solution)/shard_map/slice | solution.py:124
  88.7 3.3 collective-permute-start.3
  92.0 2.9 fusion.47
  97.1 4.2 collective-permute-start.7
  102.9 28.6 %collective-permute-done.3 = bf16[2,1,128,1536]{3,2,0,1:T(8,128)(2,1)} collective-permute-done((bf16[2,1,128,1536]{3,2,0,1:T(8,128)(2,1)}, bf16[2,1,128,1536]{3,2,0,1:T(8,128)(2,1)}, u32[]{:S(2)}, u32[]{:S(2)}) %collective-permute-start.3) | collective-permute-done | bytes 786464 | tf_op jit(solution)/shard_map/ppermute | solution.py:26
  132.7 2.7 fusion.44
  135.4 4.2 reshape_reshape_squeeze.20
  139.5 5.5 %reshape_reshape_squeeze.18 = bf16[768,12,128]{2,1,0:T(8,128)(2,1)} reshape(bf16[1,6,128,1536]{3,2,0,1:T(8,128)(2,1)} %get-tuple-element.5) | data formatting | bytes 4718592 | tf_op jit(solution)/shard_map/reshape;reshape;squeeze | solution.py:67
  145.0 3.0 fusion.20
  148.0 5.5 %fusion.53 = (f32[12,256]{1,0:T(8,128)S(1)}, f32[12,256,768]{2,1,0:T(8,128)}) fusion(f32[12,256,768]{2,1,0:T(8,128)S(1)} %fusion.20, pred[768]{0:T(1024)(128)(4,1)S(1)} %pad_add_fusion), kind=kOutput, calls=%fused_computation.101 | output fusion | flops 14156543 | bytes 18887424 | tf_op jit(solution)/shard_map/sub | solution.py:73
  153.4 5.8 %fusion.27 = bf16[12,128,256]{2,1,0:T(8,128)(2,1)S(1)} fusion(f32[12,256,768]{2,1,0:T(8,128)} %get-tuple-element.53, f32[12,256]{1,0:T(8,128)S(1)} %get-tuple-element.52, bf16[768,12,128]{2,1,0:T(8,128)(2,1)S(1)} %copy-done.7), kind=kOutput, calls=%fused_computation.41 | convolution fusion | flops 609091584 | bytes 12595200 | tf_op jit(solution)/shard_map/hrk,khd->rhd/dot_general | solution.py:75
  159.2 212.1 %all-gather.6.cloned.1.call-done = bf16[1536,5120]{1,0:T(8,128)(2,1)} async-done(((bf16[1536,1280]{1,0:T(8,128)(2,1)}), bf16[1536,5120]{1,0:T(8,128)(2,1)}) %all-gather.6.cloned.1.call-update) | async-done | bytes 15728656 | tf_op jit(solution)/shard_map/all_gather | solution.py:128
  371.4 11.1 %convolution_convert_fusion.1 = bf16[256,5120]{1,0:T(8,128)(2,1)} fusion(bf16[256,1536]{0,1:T(8,128)(2,1)S(1)} %bitcast.111, bf16[1536,5120]{1,0:T(8,128)(2,1)} %all-gather.6.cloned.1.call-done), kind=kOutput, calls=%fused_computation.11 | convolution fusion | flops 4027842560 | bytes 19136512 | tf_op jit(solution)/shard_map/dot_general | solution.py:126
  386.1 2.7 fusion.45
  388.8 4.2 reshape_reshape_squeeze.23
  393.0 5.4 %reshape_reshape_squeeze.21 = bf16[768,12,128]{2,1,0:T(8,128)(2,1)} reshape(bf16[1,6,128,1536]{3,2,0,1:T(8,128)(2,1)} %get-tuple-element.7) | data formatting | bytes 4718592 | tf_op jit(solution)/shard_map/reshape;reshape;squeeze | solution.py:67
  398.4 6.7 %fusion.17 = f32[12,256,768]{2,1,0:T(8,128)} fusion(bf16[256,12,128]{0,2,1:T(8,128)(2,1)} %reshape_reshape_squeeze.22, bf16[768,12,128]{2,1,0:T(8,128)(2,1)S(1)} %reshape_reshape_squeeze.23), kind=kOutput, calls=%fused_computation.33 | convolution fusion | flops 603979776 | bytes 12582912 | tf_op jit(solution)/shard_map/rhd,khd->hrk/dot_general | solution.py:68
  405.1 13.3 %fusion.52 = (f32[12,256]{1,0:T(8,128)S(1)}, f32[12,256,768]{2,1,0:T(8,128)}) fusion(f32[12,256,768]{2,1,0:T(8,128)} %fusion.17, pred[768]{0:T(1024)(128)(4,1)S(1)} %pad_add_fusion), kind=kOutput, calls=%fused_computation.100 | output fusion | flops 14156543 | bytes 18887424 | tf_op jit(solution)/shard_map/sub | solution.py:73
  418.4 6.0 %fusion.24 = bf16[12,128,256]{2,1,0:T(8,128)(2,1)S(1)} fusion(f32[12,256,768]{2,1,0:T(8,128)} %get-tuple-element.51, f32[12,256]{1,0:T(8,128)S(1)} %get-tuple-element.50, bf16[768,12,128]{2,1,0:T(8,128)(2,1)S(1)} %copy-done.6), kind=kOutput, calls=%fused_computation.40 | convolution fusion | flops 609091584 | bytes 12595200 | tf_op jit(solution)/shard_map/hrk,khd->rhd/dot_general | solution.py:75
  424.7 5.8 %convolution_convert_fusion = bf16[256,5120]{1,0:T(8,128)(2,1)} fusion(bf16[256,1536]{0,1:T(8,128)(2,1)S(1)} %bitcast.112, bf16[1536,5120]{1,0:T(8,128)(2,1)S(1)} %bitcast.99), kind=kOutput, calls=%fused_computation.10 | convolution fusion | flops 4027842560 | bytes 19136512 | tf_op jit(solution)/shard_map/dot_general | solution.py:126
  435.2 18.5 %collective-permute-done = bf16[128,2560]{1,0:T(8,128)(2,1)S(1)} collective-permute-done((bf16[128,2560]{1,0:T(8,128)(2,1)S(1)}, bf16[128,2560]{1,0:T(8,128)(2,1)S(1)}, u32[]{:S(2)}, u32[]{:S(2)}) %collective-permute-start) | collective-permute-done | bytes 655392 | tf_op jit(solution)/shard_map/ppermute | solution.py:15
  457.8 10.4 %collective-permute-done.4 = bf16[128,2560]{1,0:T(8,128)(2,1)S(1)} collective-permute-done((bf16[128,2560]{1,0:T(8,128)(2,1)S(1)}, bf16[128,2560]{1,0:T(8,128)(2,1)S(1)}, u32[]{:S(2)}, u32[]{:S(2)}) %collective-permute-start.4) | collective-permute-done | bytes 655392 | tf_op jit(solution)/shard_map/ppermute | solution.py:15
  468.3 9.2 %reduce-scatter.5.cloned.1.call-done = bf16[256,2560]{1,0:T(8,128)(2,1)} async-done(((bf16[256,5120]{1,0:T(8,128)(2,1)}), bf16[256,2560]{1,0:T(8,128)(2,1)}) %reduce-scatter.5.cloned.1.call-update) | async-done | bytes 1310736 | tf_op jit(solution)/shard_map/reduce_scatter | solution.py:131
  477.4 2.8 fusion.13
  (97 shorter events, 45.3 us)
Async XLA Ops:
  6.5 428.5 %copy-start = (bf16[50,2560]{1,0:T(8,128)(2,1)S(1)}, bf16[50,2560]{1,0:T(8,128)(2,1)}, u32[]{:S(2)}) copy-start(bf16[50,2560]{1,0:T(8,128)(2,1)} %param.13) | copy-start | bytes 768004
  6.5 60.1 %all-gather.4.cloned.1.call-start = ((), (), s32[]{:S(2)}) async-start(), calls=%async_computation.2 | async-start | bytes 4718592 | tf_op jit(solution)/shard_map/all_gather | solution.py:111
  8.7 2.5 copy-start.11
  8.8 2.5 copy-start.12
  16.9 17.9 %collective-permute-start.1 = (bf16[3,128,1536]{1,2,0:T(8,128)(2,1)}, bf16[3,128,1536]{1,2,0:T(8,128)(2,1)}, u32[]{:S(2)}, u32[]{:S(2)}) collective-permute-start(bf16[3,128,1536]{1,2,0:T(8,128)(2,1)} %get-tuple-element.15), channel_id=1, source_target_pairs={{1,0},{4,1},{5,4},{8,5},{9,8},{12,9},{13,12},{3,2},{6,3},{7,6},{10... | collective-permute-start | bytes 3538952 | tf_op jit(solution)/shard_map/ppermute | solution.py:15
  19.4 28.0 %collective-permute-start.5 = (bf16[3,128,1536]{1,2,0:T(8,128)(2,1)}, bf16[3,128,1536]{1,2,0:T(8,128)(2,1)}, u32[]{:S(2)}, u32[]{:S(2)}) collective-permute-start(bf16[3,128,1536]{1,2,0:T(8,128)(2,1)} %get-tuple-element.14), channel_id=1, source_target_pairs={{1,0},{4,1},{5,4},{8,5},{9,8},{12,9},{13,12},{3,2},{6,3},{7,6},{10... | collective-permute-start | bytes 3538952 | tf_op jit(solution)/shard_map/ppermute | solution.py:15
  26.4 1.1 copy-start.5
  27.8 21.8 %copy-start.1 = (bf16[3,1,128,1536]{2,3,0,1:T(8,128)(2,1)S(1)}, bf16[3,1,128,1536]{2,3,0,1:T(8,128)(2,1)}, u32[]{:S(2)}) copy-start(bf16[3,1,128,1536]{2,3,0,1:T(8,128)(2,1)} %get-tuple-element.13) | copy-start | bytes 3538948
  54.0 38.0 %all-gather.8.cloned.1.call-start = ((), (), s32[]{:S(2)}) async-start(), calls=%async_computation.5 | async-start | bytes 4718592 | tf_op jit(solution)/shard_map/all_gather | solution.py:111
  56.6 314.7 %all-gather.6.cloned.1.call-start = ((), (), s32[]{:S(2)}) async-start(), calls=%async_computation.3 | async-start | bytes 19660800 | tf_op jit(solution)/shard_map/all_gather | solution.py:128
  57.4 396.5 %reduce-scatter.3.cloned.1.call-start = ((), (), s32[]{:S(2)}) async-start(), calls=%async_computation.4 | async-start | bytes 3932160 | tf_op jit(solution)/shard_map/reduce_scatter | solution.py:131
  66.6 6.1 %copy-start.2 = (bf16[3,1,128,1536]{2,3,0,1:T(8,128)(2,1)S(1)}, bf16[3,1,128,1536]{2,3,0,1:T(8,128)(2,1)}, u32[]{:S(2)}) copy-start(bf16[3,1,128,1536]{2,3,0,1:T(8,128)(2,1)} %get-tuple-element.13) | copy-start | bytes 3538948
  69.4 31.9 %collective-permute-start.2 = (bf16[2,1,128,1536]{3,2,0,1:T(8,128)(2,1)}, bf16[2,1,128,1536]{3,2,0,1:T(8,128)(2,1)}, u32[]{:S(2)}, u32[]{:S(2)}) collective-permute-start(bf16[2,1,128,1536]{3,2,0,1:T(8,128)(2,1)} %get-tuple-element.10), channel_id=1, source_target_pairs={{0,4},{4,8},{8,12},{1,5},{5,9},{9,13},{2,6},{6,10},{10,14},{3,7},{... | collective-permute-start | bytes 2359304 | tf_op jit(solution)/shard_map/ppermute | solution.py:23
  88.7 13.9 %copy-start.4 = (bf16[2,4,128,1536]{3,2,0,1:T(8,128)(2,1)S(1)}, bf16[2,4,128,1536]{3,2,0,1:T(8,128)(2,1)}, u32[]{:S(2)}) copy-start(bf16[2,4,128,1536]{3,2,0,1:T(8,128)(2,1)} %all-gather.4.cloned.1.call-done) | copy-start | bytes 9437188
  88.7 42.9 %collective-permute-start.3 = (bf16[2,1,128,1536]{3,2,0,1:T(8,128)(2,1)}, bf16[2,1,128,1536]{3,2,0,1:T(8,128)(2,1)}, u32[]{:S(2)}, u32[]{:S(2)}) collective-permute-start(bf16[2,1,128,1536]{3,2,0,1:T(8,128)(2,1)} %get-tuple-element.9), channel_id=1, source_target_pairs={{4,0},{8,4},{12,8},{5,1},{9,5},{13,9},{6,2},{10,6},{14,10},{7,3},{... | collective-permute-start | bytes 2359304 | tf_op jit(solution)/shard_map/ppermute | solution.py:26
  94.9 288.0 %collective-permute-start.6 = (bf16[2,1,128,1536]{3,2,0,1:T(8,128)(2,1)}, bf16[2,1,128,1536]{3,2,0,1:T(8,128)(2,1)}, u32[]{:S(2)}, u32[]{:S(2)}) collective-permute-start(bf16[2,1,128,1536]{3,2,0,1:T(8,128)(2,1)} %get-tuple-element.12), channel_id=1, source_target_pairs={{0,4},{4,8},{8,12},{1,5},{5,9},{9,13},{2,6},{6,10},{10,14},{3,7},{... | collective-permute-start | bytes 2359304 | tf_op jit(solution)/shard_map/ppermute | solution.py:23
  97.1 287.9 %collective-permute-start.7 = (bf16[2,1,128,1536]{3,2,0,1:T(8,128)(2,1)}, bf16[2,1,128,1536]{3,2,0,1:T(8,128)(2,1)}, u32[]{:S(2)}, u32[]{:S(2)}) collective-permute-start(bf16[2,1,128,1536]{3,2,0,1:T(8,128)(2,1)} %get-tuple-element.11), channel_id=1, source_target_pairs={{4,0},{8,4},{12,8},{5,1},{9,5},{13,9},{6,2},{10,6},{14,10},{7,3},{... | collective-permute-start | bytes 2359304 | tf_op jit(solution)/shard_map/ppermute | solution.py:26
  148.0 5.5 %copy-start.7 = (bf16[768,12,128]{2,1,0:T(8,128)(2,1)S(1)}, bf16[768,12,128]{2,1,0:T(8,128)(2,1)}, u32[]{:S(2)}) copy-start(bf16[768,12,128]{2,1,0:T(8,128)(2,1)} %reshape_reshape_squeeze.18) | copy-start | bytes 7077892
  382.5 2.1 copy-start.3
  382.5 94.9 %reduce-scatter.5.cloned.1.call-start = ((), (), s32[]{:S(2)}) async-start(), calls=%async_computation.6 | async-start | bytes 3932160 | tf_op jit(solution)/shard_map/reduce_scatter | solution.py:131
  405.1 13.3 %copy-start.6 = (bf16[768,12,128]{2,1,0:T(8,128)(2,1)S(1)}, bf16[768,12,128]{2,1,0:T(8,128)(2,1)}, u32[]{:S(2)}) copy-start(bf16[768,12,128]{2,1,0:T(8,128)(2,1)} %reshape_reshape_squeeze.21) | copy-start | bytes 7077892
  405.1 19.3 %slice-start = ((s8[15728640]{0:T(1024)(128)(4,1)}), s8[4194304]{0:T(1024)(128)(4,1)S(1)}, s32[]{:S(2)}) async-start(s8[15728640]{0:T(1024)(128)(4,1)} %bitcast.98), calls=%async_computation.7 | async-start | bytes 8388608
  405.1 19.3 %slice-start.1 = ((s8[15728640]{0:T(1024)(128)(4,1)}), s8[3145728]{0:T(1024)(128)(4,1)S(1)}, s32[]{:S(2)}) async-start(s8[15728640]{0:T(1024)(128)(4,1)} %bitcast.98), calls=%async_computation.8 | async-start | bytes 6291456
  418.4 6.0 %slice-start.2 = ((s8[15728640]{0:T(1024)(128)(4,1)}), s8[4194304]{0:T(1024)(128)(4,1)S(1)}, s32[]{:S(2)}) async-start(s8[15728640]{0:T(1024)(128)(4,1)} %bitcast.98), calls=%async_computation.9 | async-start | bytes 8388608
  418.4 6.3 %slice-start.3 = ((s8[15728640]{0:T(1024)(128)(4,1)}), s8[4194304]{0:T(1024)(128)(4,1)S(1)}, s32[]{:S(2)}) async-start(s8[15728640]{0:T(1024)(128)(4,1)} %bitcast.98), calls=%async_computation.10 | async-start | bytes 8388608
  430.5 1.3 copy-start.8
  431.8 22.0 %copy-start.9 = (bf16[2,128,2560]{2,1,0:T(8,128)(2,1)S(1)}, bf16[2,128,2560]{2,1,0:T(8,128)(2,1)}, u32[]{:S(2)}) copy-start(bf16[2,128,2560]{2,1,0:T(8,128)(2,1)} %param.15) | copy-start | bytes 3932164
  431.9 21.9 %collective-permute-start = (bf16[128,2560]{1,0:T(8,128)(2,1)S(1)}, bf16[128,2560]{1,0:T(8,128)(2,1)S(1)}, u32[]{:S(2)}, u32[]{:S(2)}) collective-permute-start(bf16[128,2560]{1,0:T(8,128)(2,1)S(1)} %get-tuple-element.35), channel_id=1, source_target_pairs={{1,0},{4,1},{5,4},{8,5},{9,8},{12,9},{13,12},{3,2},{6,3},{7,6},{10... | collective-permute-start | bytes 1966088 | tf_op jit(solution)/shard_map/ppermute | solution.py:15
  453.9 14.3 %copy-start.10 = (bf16[2,128,2560]{2,1,0:T(8,128)(2,1)S(1)}, bf16[2,128,2560]{2,1,0:T(8,128)(2,1)}, u32[]{:S(2)}) copy-start(bf16[2,128,2560]{2,1,0:T(8,128)(2,1)} %param.15) | copy-start | bytes 3932164
  455.9 12.3 %collective-permute-start.4 = (bf16[128,2560]{1,0:T(8,128)(2,1)S(1)}, bf16[128,2560]{1,0:T(8,128)(2,1)S(1)}, u32[]{:S(2)}, u32[]{:S(2)}) collective-permute-start(bf16[128,2560]{1,0:T(8,128)(2,1)S(1)} %get-tuple-element.33), channel_id=1, source_target_pairs={{1,0},{4,1},{5,4},{8,5},{9,8},{12,9},{13,12},{3,2},{6,3},{7,6},{10... | collective-permute-start | bytes 1966088 | tf_op jit(solution)/shard_map/ppermute | solution.py:15
Sparse Core Ops, SparseCore 0:
  54.1 12.4 all-gather.3
  68.1 13.2 all-gather.7
  83.0 288.2 all-gather.5
  382.6 46.9 reduce-scatter.2
  431.8 45.6 reduce-scatter.4
where the time goes:
time: 495 us; the launch traced here: 487 us
  waiting for transfers between devices  308 us (62%)
  local copies, waits for them, and re-layouts  70.7 us (14%)
  matrix products  38.5 us (8%)
  other arithmetic  32.6 us (7%)
  starting transfers between devices  22.3 us (5%)
  between operations  14.7 us (3%)
    all_gather x1, waiting for transfers between devices, local(): lax.all_gather(out_weight, 'queue', axis=1, tiled=True)  212 us
    ppermute x4, waiting for transfers between devices, shifted(): return lax.ppermute(array, axis, pairs)  48.6 us
    ppermute x2, waiting for transfers between devices, padded_2(): lax.ppermute(lax.slice_in_dim(block, 0, width, axis=dim), axis, backward)  28.6 us
    sub x2, other arithmetic, attend(): weights = jnp.exp(scores - row_top)  18.8 us
    dot_general x2, matrix products, local(): jnp.dot(mixture, lax.all_gather(out_weight, 'queue', axis=1, tiled=True),...  16.9 us
    unnamed x43, local copies, waits for them, and re-layouts  14.1 us
    slice x2, local copies, waits for them, and re-layouts, local(): carried[0].reshape(frames * tokens, channels)  13 us
    dot_general x2, matrix products, attend(): jnp.einsum('hrk,khd->rhd', weights, value_heads, preferred_element_type=j...  11.8 us
  transfers between devices with their start and end apart: 13, of which 8 were waited for; matrix products, arithmetic and copies ran while one was open for 24% of the time, Pallas kernels for 0%

commit v1 on v0

v1 whole, which is shorter than its diff:
```python
import functools
import math

import jax
import jax.numpy as jnp
from jax import lax
from jax.experimental import pallas as pl
from jax.experimental.pallas import tpu as pltpu
from jax.sharding import PartitionSpec as P

HD = 128
BF16 = jnp.bfloat16
F32 = jnp.float32
VMEM_LIMIT = 48 * 1024 * 1024


def params(*semantics):
    return pltpu.CompilerParams(
        dimension_semantics=semantics, vmem_limit_bytes=VMEM_LIMIT
    )


def rotation_tables(times):
    half = HD // 2
    pair_index = jnp.arange(half, dtype=F32)
    frequency = jnp.power(F32(10000.0), -pair_index / half)
    angles = times.astype(F32)[:, None] * frequency[None, :]
    cosine, sine = jnp.cos(angles), jnp.sin(angles)
    return (
        jnp.concatenate([cosine, cosine], axis=1),
        jnp.concatenate([-sine, sine], axis=1),
    )


def rotate_kernel(core_ref, cos_ref, sin_ref, own_ref, new_ref, q_ref, kv_ref, side_ref, nq_ref, nkv_ref):
    frames = own_ref.shape[1]
    heads = own_ref.shape[-1] // HD
    first_core = core_ref[0] == 0

    def turn(block, row):
        block = block.astype(F32)
        out = block * cos_ref[row : row + 1, :] + pltpu.roll(block, HD // 2, 1) * sin_ref[row : row + 1, :]
        return out.astype(BF16)

    for head in range(heads):
        at = slice(head * HD, (head + 1) * HD)
        for frame in range(frames):
            query = turn(own_ref[0, frame, :, at], frame)
            q_ref[frame, :, at] = query
            kv_ref[0, frame, :, at] = turn(own_ref[1, frame, :, at], frame)
            kv_ref[1, frame, :, at] = own_ref[2, frame, :, at]
            nq_ref[frame, :, at] = turn(new_ref[frame, 0, :, at], frames + frame)
            nkv_ref[0, frame, :, at] = turn(new_ref[frame, 1, :, at], frames + frame)
            nkv_ref[1, frame, :, at] = new_ref[frame, 2, :, at]

    @pl.when(first_core)
    def _():
        side_ref[...] = q_ref[...]

    @pl.when(jnp.logical_not(first_core))
    def _():
        side_ref[0] = kv_ref[0, 0]
        side_ref[1] = kv_ref[1, 0]


def rotate_all(core, cos, sin, own, new):
    _, frames, tokens, channels = own.shape
    wide = min(channels, 3 * HD)
    steps = channels // wide
    three = pl.BlockSpec((frames, tokens, wide), lambda i, c: (0, 0, i))
    four = pl.BlockSpec((2, frames, tokens, wide), lambda i, c: (0, 0, 0, i))
    table = pl.BlockSpec(cos.shape, lambda i, c: (0, 0))
    sq = jax.ShapeDtypeStruct((frames, tokens, channels), BF16)
    skv = jax.ShapeDtypeStruct((2, frames, tokens, channels), BF16)
    return pl.pallas_call(
        rotate_kernel,
        grid_spec=pltpu.PrefetchScalarGridSpec(
            num_scalar_prefetch=1,
            grid=(steps,),
            in_specs=[
                table,
                table,
                pl.BlockSpec((3, frames, tokens, wide), lambda i, c: (0, 0, 0, i)),
                pl.BlockSpec((frames, 3, tokens, wide), lambda i, c: (0, 0, 0, i)),
            ],
            out_specs=[three, four, three, three, four],
        ),
        out_shape=[sq, skv, sq, sq, skv],
        compiler_params=params("arbitrary"),
        cost_estimate=pl.CostEstimate(flops=10 * own.size, bytes_accessed=10 * own.size, transcendentals=0),
        name="rotate",
    )(core, cos, sin, own, new)


def attend_kernel(
    where_ref, peer_q, far_q, new_q, own_kv, peer_kv, far_kv, new_kv, far6_kv, send_ref, keep_ref, key_s, value_s
):
    tokens = peer_q.shape[1]
    core, first, last = where_ref[0], where_ref[1] == 1, where_ref[2] == 1
    second_core = core == 1
    for side, scratch in ((0, key_s), (1, value_s)):
        for frame in range(2):
            own, peer = own_kv[side, frame], peer_kv[side, frame]
            scratch[pl.ds(frame * tokens, tokens), :] = jnp.where(second_core, peer, own)
            scratch[pl.ds((2 + frame) * tokens, tokens), :] = jnp.where(second_core, own, peer)
            scratch[pl.ds((4 + frame) * tokens, tokens), :] = jnp.where(
                last, new_kv[side, frame], far_kv[side, frame]
            )
        scratch[pl.ds(6 * tokens, tokens), :] = far6_kv[side]
    q4 = jnp.where(last, new_q[0], far_q[0])
    q5 = jnp.where(last, new_q[1], far_q[1])
    qa = jnp.where(second_core, q4, peer_q[0])
    qb = peer_q[1]
    qc = jnp.where(second_core, q5, peer_q[1])
    factor = math.log2(math.e) / math.sqrt(HD)
    keys = key_s[...]
    scores = lax.dot_general(
        jnp.concatenate([qa, qb, qc], axis=0), keys, (((1,), (1,)), ((), ())), preferred_element_type=F32
    )

    def mix(rows, low):
        part = [rows[:, (low + i) * tokens : (low + i + 1) * tokens] for i in range(6)]
        part[0] = jnp.where(first, -1e30, part[0])
        part[5] = jnp.where(last, -1e30, part[5])
        rows = jnp.concatenate(part, axis=1)
        top = jnp.max(rows, axis=1, keepdims=True)
        weights = jnp.exp2((rows - top) * factor)
        total = jnp.sum(weights, axis=1, keepdims=True)
        out = jnp.dot(
            weights.astype(BF16), value_s[pl.ds(low * tokens, 6 * tokens), :], preferred_element_type=F32
        )
        return (out * (1.0 / total)).astype(BF16)

    early = mix(scores[: 2 * tokens], 0)
    late = mix(jnp.concatenate([scores[:tokens], scores[2 * tokens :]], axis=0), 1)
    keep_ref[0] = early[:tokens]
    send_ref[...] = early[tokens:]
    keep_ref[1] = late[:tokens]
    keep_ref[2] = late[tokens:]


def attend_all(where, peer_q, far_q, new_q, own_kv, peer_kv, far_kv, new_kv, far6_kv):
    _, tokens, channels = peer_q.shape
    heads = channels // HD
    three = pl.BlockSpec((2, tokens, HD), lambda i, c: (0, 0, i))
    four = pl.BlockSpec((2, 2, tokens, HD), lambda i, c: (0, 0, 0, i))
    return pl.pallas_call(
        attend_kernel,
        grid_spec=pltpu.PrefetchScalarGridSpec(
            num_scalar_prefetch=1,
            grid=(heads,),
            in_specs=[three, three, three, four, four, four, four, three],
            out_specs=[
                pl.BlockSpec((tokens, HD), lambda i, c: (0, i)),
                pl.BlockSpec((3, tokens, HD), lambda i, c: (0, 0, i)),
            ],
            scratch_shapes=[pltpu.VMEM((7 * tokens, HD), BF16), pltpu.VMEM((7 * tokens, HD), BF16)],
        ),
        out_shape=[
            jax.ShapeDtypeStruct((tokens, channels), BF16),
            jax.ShapeDtypeStruct((3, tokens, channels), BF16),
        ],
        compiler_params=params("arbitrary"),
        cost_estimate=pl.CostEstimate(
            flops=heads * 4 * 4 * 6 * tokens * tokens * HD,
            bytes_accessed=26 * tokens * channels * 2,
            transcendentals=heads * 4 * 6 * tokens * tokens,
        ),
        name="attend",
    )(where, peer_q, far_q, new_q, own_kv, peer_kv, far_kv, new_kv, far6_kv)


def project_kernel(order_ref, *refs):
    count = (len(refs) - 2) // 2
    mixes, pieces, gate_ref, out_ref = refs[:count], refs[count : 2 * count], refs[-2], refs[-1]
    total = None
    for mix, piece in zip(mixes, pieces):
        product = jnp.dot(mix[...], piece[...], preferred_element_type=F32)
        total = product if total is None else total + product
    frames, tokens = 2, out_ref.shape[0] // 2
    for frame in range(frames):
        a, b = frame * tokens, (frames + frame) * tokens
        out_ref[a : a + tokens, :] = (
            total[a : a + tokens] * gate_ref[frame : frame + 1, :]
            + total[b : b + tokens] * gate_ref[frames + frame : frames + frame + 1, :]
        ).astype(BF16)


def project(order, mix, pieces, whole, gates, wide=256):
    count = len(pieces)
    rows, channels = mix.shape
    depth = channels // count
    columns = pieces[0].shape[1]
    if depth % HD or columns % wide:
        total = 0.0
        for i, piece in enumerate(pieces):
            piece = lax.slice_in_dim(piece, i * depth, (i + 1) * depth, axis=0) if whole else piece
            part = lax.dynamic_slice_in_dim(mix, order[i] * depth, depth, axis=1)
            total = total + jnp.dot(part, piece, preferred_element_type=F32)
        total = total.reshape(4, rows // 4, columns) * gates[:, None, :]
        return (total[:2] + total[2:]).reshape(rows // 2, columns).astype(BF16)

    def mix_at(p):
        return pl.BlockSpec((rows, depth), lambda i, c: (0, c[p]))

    def piece_at(p):
        return pl.BlockSpec((depth, wide), lambda i, c: (p if whole else 0, i))

    return pl.pallas_call(
        project_kernel,
        grid_spec=pltpu.PrefetchScalarGridSpec(
            num_scalar_prefetch=1,
            grid=(columns // wide,),
            in_specs=[mix_at(p) for p in range(count)]
            + [piece_at(p) for p in range(count)]
            + [pl.BlockSpec((4, wide), lambda i, c: (0, i))],
            out_specs=pl.BlockSpec((rows // 2, wide), lambda i, c: (0, i)),
        ),
        out_shape=jax.ShapeDtypeStruct((rows // 2, columns), BF16),
        compiler_params=params("arbitrary"),
        cost_estimate=pl.CostEstimate(
            flops=2 * rows * channels * columns,
            bytes_accessed=2 * (rows * channels + channels * columns + rows * columns // 2),
            transcendentals=0,
        ),
        name="project",
    )(order, *([mix] * count), *pieces, gates)


def arrivals(count):
    table = []
    for k in range(1, count):
        row = []
        for q in range(count):
            ahead, behind = count - 1 - q, q
            if q < count // 2:
                row.append(("down", k) if k <= ahead else ("up", k - ahead))
            else:
                row.append(("up", k) if k <= behind else ("down", k - behind))
        table.append(row)
    return table


def pick(place, row, held):
    value = None
    for source in sorted(set(row)):
        here = jnp.array([r == source for r in row])[place]
        value = held[source] if value is None else jnp.where(here, held[source], value)
    return value


def local(
    latent,
    projections,
    frame_times,
    levels,
    gates,
    out_weight,
    incoming_latent,
    incoming_proj,
    incoming_times,
):
    place, count = lax.axis_index("queue"), lax.axis_size("queue")
    core, cores = lax.axis_index("seq"), lax.axis_size("seq")
    side, sides = lax.axis_index("heads"), lax.axis_size("heads")
    group, groups = lax.axis_index("groups"), lax.axis_size("groups")
    first, last = place == 0, place == count - 1
    frames, tokens, features = latent.shape
    assert cores == 2 and frames == 2 and groups == 2 and count % sides == 0

    depth = out_weight.shape[0] // 4
    mine = group * 2 + core
    quarter = lax.dynamic_slice_in_dim(out_weight, mine * depth, depth, axis=0)
    held = {}
    up = down = quarter
    for hop in range(1, count):
        up = lax.ppermute(up, "queue", [(i, i + 1) for i in range(hop - 1, count - 1)])
        down = lax.ppermute(down, "queue", [(i, i - 1) for i in range(1, count - hop + 1)])
        held["up", hop], held["down", hop] = up, down

    cos, sin = rotation_tables(jnp.concatenate([frame_times, incoming_times]))
    where = jnp.stack([core, first.astype(jnp.int32), last.astype(jnp.int32)])
    own_q, own_kv, side_out, new_q, new_kv = rotate_all(where, cos, sin, projections, incoming_proj)
    swap = [(0, 1), (1, 0)]
    pair = ("queue", "seq")
    far_kv = lax.ppermute(own_kv, pair, [(2 * i + 2, 2 * i) for i in range(count - 1)])
    side_in = lax.ppermute(
        side_out, pair, [(2 * i + 2 + s, 2 * i + 1 - s) for i in range(count - 1) for s in range(2)]
    )
    peer_q = lax.ppermute(own_q, "seq", swap)
    peer_kv = lax.ppermute(own_kv, "seq", swap)
    far_kv_1 = lax.ppermute(far_kv, "seq", [(0, 1)])
    far6_1 = lax.ppermute(side_in, "seq", [(0, 1)])
    far_kv = jnp.where(core == 0, far_kv, far_kv_1)
    far6 = jnp.where(core == 0, side_in, far6_1)

    send, keep = attend_all(where, peer_q, side_in, new_q, own_kv, peer_kv, far_kv, new_kv, far6)
    came = lax.ppermute(send, pair, [(2 * i + 3, 2 * i + 1) for i in range(count - 1)])
    mix = jnp.concatenate(
        [keep[0], jnp.where(core == 0, send, came), keep[1], keep[2]], axis=0
    )

    next_level = lax.ppermute(levels, "queue", [(i + 1, i) for i in range(count - 1)])
    chosen = jnp.concatenate([levels, next_level])
    one_hot = (jnp.arange(gates.shape[0], dtype=jnp.int32)[None, :] == chosen[:, None]).astype(BF16)
    rows = jnp.dot(one_hot, gates, preferred_element_type=F32).astype(BF16)
    rows = lax.all_gather(rows, "heads", axis=1, tiled=True).astype(F32)
    crossing = jnp.where(last, 0.0, rows[1:2])
    gate_rows = jnp.concatenate(
        [rows[:1], jnp.where(core == 0, rows[:1], crossing), rows[:1], rows[:1]], axis=0
    )

    moved = lax.ppermute(latent, pair, [(i + 1, i) for i in range(2 * count - 1)])
    moved = jnp.where(jnp.logical_and(last, core == 1), incoming_latent, moved)
    moved = moved.reshape(frames * tokens, features)

    columns = out_weight.shape[1]
    per_side = count // sides
    table = arrivals(count)
    block_of = [list(range(count))]
    for row in table:
        block_of.append([q + hops if way == "down" else q - hops for q, (way, hops) in enumerate(row)])
    flat = ("queue", "heads")
    deltas, others, blocks = [], [], []
    for k in range(count):
        block = jnp.array(block_of[k], jnp.int32)[place]
        gate = lax.dynamic_slice_in_dim(gate_rows, block * columns, columns, axis=1)
        if k == 0:
            pieces, order = [out_weight] * 4, jnp.arange(4, dtype=jnp.int32)
        else:
            a = pick(place, table[k - 1], held)
            b = lax.ppermute(a, "groups", swap)
            c = lax.ppermute(a, "seq", swap)
            d = lax.ppermute(b, "seq", swap)
            pieces = [a, b, c, d]
            order = jnp.stack([mine, mine ^ 2, mine ^ 1, mine ^ 3]).astype(jnp.int32)
        delta = project(order, mix, pieces, k == 0, gate)
        deltas.append(delta)
        blocks.append(block)
        if sides == 2:
            pairs = [
                (q * 2 + 1 - block_of[k][q] // per_side, q * 2 + block_of[k][q] // per_side)
                for q in range(count)
            ]
            others.append(lax.ppermute(delta, flat, pairs))

    if sides == 2:
        parts = []
        for b in range(per_side):
            wanted = side * per_side + b
            total = moved[:, b * columns : (b + 1) * columns].astype(F32)
            change = jnp.zeros_like(total)
            for delta, other, block in zip(deltas, others, blocks):
                change = jnp.where(block == wanted, delta.astype(F32) + other.astype(F32), change)
            parts.append(total + change)
        total = jnp.concatenate(parts, axis=1)
    else:
        change = jnp.zeros((frames * tokens, columns * count), BF16)
        for delta, block in zip(deltas, blocks):
            change = lax.dynamic_update_slice_in_dim(change, delta, block * columns, axis=1)
        change = lax.psum_scatter(change, "heads", scatter_dimension=1, tiled=True)
        total = moved.astype(F32) + change.astype(F32)
    return total.astype(BF16).reshape(frames, tokens, features)


def solution(mesh):
    return jax.shard_map(
        local,
        mesh=mesh,
        in_specs=(
            P(("groups", "queue", "seq"), None, "heads"),
            P(None, ("groups", "queue", "seq"), None, "heads"),
            P(("groups", "queue", "seq")),
            P(("groups", "queue")),
            P(None, "heads"),
            P("heads", "queue"),
            P("groups", None, "heads"),
            P("groups", None, None, "heads"),
            P("groups"),
        ),
        out_specs=P(("groups", "queue", "seq"), None, "heads"),
        check_vma=False,
    )
```

time: 495 us -> 226 us (0.46)
  the two profiles are of different devices: /device:TPU:9 before, /device:TPU:24 now
where the time goes in v1:
time: 226 us; the launch traced here: 225 us
  waiting for transfers between devices  107 us (47%)
  starting transfers between devices  41.7 us (18%)
  Pallas kernels  41 us (18%)
  other arithmetic  12.7 us (6%)
  local copies, waits for them, and re-layouts  10.7 us (5%)
  between operations  6.71 us (3%)
  blocking collectives  4.38 us (2%)
    ppermute x3, waiting for transfers between devices, local(): lax.ppermute(up, 'queue', [(i, i + 1) for i in range(hop - 1, count - 1)])  45 us
    ppermute x3, waiting for transfers between devices, local(): b = lax.ppermute(a, 'groups', swap)  33.4 us
    pallas_call x4, Pallas kernels, project(): pl.pallas_call(project_kernel, grid_spec=pltpu.PrefetchScalarGridSpec(num...  21.8 us
    ppermute x4, waiting for transfers between devices, local(): others.append(lax.ppermute(delta, flat, pairs))  15.4 us
    pallas_call x1, Pallas kernels, attend_all(): pl.pallas_call(attend_kernel, grid_spec=pltpu.PrefetchScalarGridSpec(num_...  14.4 us
    ppermute x1, waiting for transfers between devices, local(): lax.ppermute(levels, 'queue', [(i + 1, i) for i in range(count - 1)])  13.6 us
    ppermute x4, starting transfers between devices, local(): others.append(lax.ppermute(delta, flat, pairs))  10.7 us
    ppermute x3, starting transfers between devices, local(): lax.ppermute(down, 'queue', [(i, i - 1) for i in range(1, count - hop + 1)])  7.03 us
  transfers between devices with their start and end apart: 28, of which 7 were waited for; matrix products, arithmetic and copies ran while one was open for 7% of the time, Pallas kernels for 18%

profile of v1, /device:TPU:24, one launch (start us, length us, event | category | flops | bytes accessed | tf_op | source)
XLA Modules:
  0.0 224.9 jit_solution(12374809931594604825)
XLA Ops:
  0.0 2.3 %constant_dynamic-slice_fusion.4 = bf16[384,1280]{1,0:T(8,128)(2,1)} fusion(bf16[1536,1280]{1,0:T(8,128)(2,1)} %refs_7_.1, s32[]{:T(128)S(6)} %select_n.167), kind=kLoop, calls=%fused_computation.31 | loop fusion | bytes 1966084 | tf_op jit(solution)/shard_map/dynamic_slice | solution.py:273
  3.6 5.6 %collective-permute-start.11 = (bf16[384,1280]{1,0:T(8,128)(2,1)}, bf16[384,1280]{1,0:T(8,128)(2,1)}, u32[]{:S(2)}, u32[]{:S(2)}) collective-permute-start(bf16[384,1280]{1,0:T(8,128)(2,1)} %constant_dynamic-slice_fusion.4), channel_id=1, source_target_pairs={{4,0},{8,4},{12,8},{5,1},{9,5},{13,9},{6,2},{10,6},{14,10},{7,3},{... | collective-permute-start | bytes 2949128 | tf_op jit(solution)/shard_map/ppermute | solution.py:278
  9.6 4.9 %rotate.1 = (bf16[2,128,1536]{2,1,0:T(8,128)(2,1)S(1)}, bf16[2,2,128,1536]{3,2,1,0:T(8,128)(2,1)S(1)}, bf16[2,128,1536]{2,1,0:T(8,128)(2,1)S(1)}, bf16[2,128,153...) custom-call(s32[3]{0:T(128)S(1)} %pad_add_fusion.1.core_ref.where_ref, f32[4,128]{1,0:T(4,128)S(1)} %get-tuple-element.33.cos_ref, ...), custom_call_target="tpu_custom_call" | custom-call | flops 11796480 | bytes 11796480 | tf_op jit(solution)/shard_map/rotate/pallas_call | solution.py:75
  16.5 2.5 %collective-permute-start.4 = (bf16[2,2,128,1536]{3,2,1,0:T(8,128)(2,1)S(1)}, bf16[2,2,128,1536]{3,2,1,0:T(8,128)(2,1)}, u32[]{:S(2)}, u32[]{:S(2)}) collective-permute-start(bf16[2,2,128,1536]{3,2,1,0:T(8,128)(2,1)S(1)} %get-tuple-element.15.own_kv), channel_id=1, source_target_pairs={{4,0},{8,4},{12,8},{6,2},{10,6},{14,10},{20,16},{24,20},{28,24},{2... | collective-permute-start | bytes 4718600 | tf_op jit(solution)/shard_map/ppermute | solution.py:286
  19.1 2.7 %collective-permute-start.17 = (s32[1]{0:T(128)}, s32[1]{0:T(128)}, u32[]{:S(2)}, u32[]{:S(2)}) collective-permute-start(s32[1]{0:T(128)} %param.21), channel_id=1, source_target_pairs={{4,0},{8,4},{12,8},{5,1},{9,5},{13,9},{6,2},{10,6},{14,10},{7,3},{... | collective-permute-start | bytes 20 | tf_op jit(solution)/shard_map/ppermute | solution.py:303
  32.3 13.6 %collective-permute-done.17 = s32[1]{0:T(128)} collective-permute-done((s32[1]{0:T(128)}, s32[1]{0:T(128)}, u32[]{:S(2)}, u32[]{:S(2)}) %collective-permute-start.17) | collective-permute-done | bytes 36 | tf_op jit(solution)/shard_map/ppermute | solution.py:303
  45.9 1.3 collective-permute-start.2
  48.1 4.4 %all_gather.3 = bf16[2,5120]{1,0:T(2,128)(2,1)S(1)} all-gather(bf16[2,2560]{1,0:T(2,128)(2,1)S(1)} %convolution_convert_fusion), channel_id=1, replica_groups=mesh['groups'=2,'queue'=4,'heads'=2,'seq'=2] {'heads'}, dimensions={1}, use_global_device_ids=true | all-gather | bytes 30720 | tf_op jit(solution)/shard_map/all_gather | solution.py:307
  52.5 1.3 collective-permute-start.9
  54.6 25.8 %collective-permute-done.9 = bf16[384,1280]{1,0:T(8,128)(2,1)S(1)} collective-permute-done((bf16[384,1280]{1,0:T(8,128)(2,1)}, bf16[384,1280]{1,0:T(8,128)(2,1)S(1)}, u32[]{:S(2)}, u32[]{:S(2)}) %collective-permute-start.9) | collective-permute-done | bytes 983072 | tf_op jit(solution)/shard_map/ppermute | solution.py:277
  81.8 2.1 collective-permute-start.6
  83.9 1.4 collective-permute-start.5
  86.8 19.2 %collective-permute-done.10 = bf16[384,1280]{1,0:T(8,128)(2,1)S(1)} collective-permute-done((bf16[384,1280]{1,0:T(8,128)(2,1)S(1)}, bf16[384,1280]{1,0:T(8,128)(2,1)S(1)}, u32[]{:S(2)}, u32[]{:S(2)}) %collective-permute-start.10) | collective-permute-done | bytes 983072 | tf_op jit(solution)/shard_map/ppermute | solution.py:277
  106.0 1.5 collective-permute-start.19
  107.7 4.1 %broadcast_select_fusion.2 = (bf16[384,1280]{1,0:T(8,128)(2,1)S(1)}, bf16[384,1280]{1,0:T(8,128)(2,1)S(1)}) fusion(bf16[384,1280]{1,0:T(8,128)(2,1)} %collective-permute-done.8, bf16[384,1280]{1,0:T(8,128)(2,1)} %collective-permute-done.11, pred[]{:T(512)} %bitcast.16, bf16[384,1280]{1,0:T(8,128)(2,1)S(1)} %collective-permute-done.10, ...), kind=kLoop, calls=%fused_computation.12 | loop fusion | flops 1966080 | bytes 5898244 | tf_op jit(solution)/shard_map/jit(_where)/select_n | solution.py:248
  112.5 18.3 %collective-permute-done.19.refs_5_ = bf16[384,1280]{1,0:T(8,128)(2,1)S(1)} collective-permute-done((bf16[384,1280]{1,0:T(8,128)(2,1)S(1)}, bf16[384,1280]{1,0:T(8,128)(2,1)S(1)}, u32[]{:S(2)}, u32[]{:S(2)}) %collective-permute-start.19) | collective-permute-done | bytes 983072 | tf_op jit(solution)/shard_map/ppermute | solution.py:332
  130.7 1.5 collective-permute-start.14
  132.3 2.8 %broadcast_select_fusion.far_kv = bf16[2,2,128,1536]{3,2,1,0:T(8,128)(2,1)} fusion(bf16[2,2,128,1536]{3,2,1,0:T(8,128)(2,1)} %collective-permute-done.4, bf16[2,2,128,1536]{3,2,1,0:T(8,128)(2,1)S(1)} %collective-permute-done.5, pred[]{:T(512)S(6)} %eq.56), kind=kLoop, calls=%fused_computation.2 | loop fusion | flops 786432 | bytes 4718593 | tf_op jit(solution)/shard_map/jit(_where)/select_n | solution.py:294
  135.0 14.4 %attend.1 = (bf16[128,1536]{1,0:T(8,128)(2,1)S(1)}, bf16[3,128,1536]{2,1,0:T(8,128)(2,1)S(1)}) custom-call(s32[3]{0:T(128)S(1)} %pad_add_fusion.1.core_ref.where_ref, bf16[2,128,1536]{2,1,0:T(8,128)(2,1)S(1)} %collective-permute-done.1.peer_q, bf16[2,128,1536]{2,1,0:T(8,128)(2,1)S(1)} %collective-permute-done.2.far_q, bf16[2,128,1536]{2,1,0:T(8,128)(2,1)S(1)} %copy-done.5, ...), custom_call_target="tpu_custom_call" | custom-call | flops 2415919104 | bytes 10223616 | tf_op jit(solution)/shard_map/attend/pallas_call | solution.py:147
  150.2 1.9 collective-permute-start
  152.2 3.3 %collective-permute-start.24 = (bf16[384,1280]{1,0:T(8,128)(2,1)S(1)}, bf16[384,1280]{1,0:T(8,128)(2,1)S(1)}, u32[]{:S(2)}, u32[]{:S(2)}) collective-permute-start(bf16[384,1280]{1,0:T(8,128)(2,1)S(1)} %get-tuple-element.21.refs_4_), channel_id=1, source_target_pairs={{0,1},{1,0},{2,3},{3,2},{4,5},{5,4},{6,7},{7,6},{8,9},{9,8},{10,11... | collective-permute-start | bytes 2949128 | tf_op jit(solution)/shard_map/ppermute | solution.py:333
  156.0 15.2 %collective-permute-done.14.refs_5_ = bf16[384,1280]{1,0:T(8,128)(2,1)S(1)} collective-permute-done((bf16[384,1280]{1,0:T(8,128)(2,1)S(1)}, bf16[384,1280]{1,0:T(8,128)(2,1)S(1)}, u32[]{:S(2)}, u32[]{:S(2)}) %collective-permute-start.14) | collective-permute-done | bytes 983072 | tf_op jit(solution)/shard_map/ppermute | solution.py:332
  171.3 1.9 copy-done.1
  173.2 4.7 %project.7 = bf16[256,1280]{1,0:T(8,128)(2,1)S(1)} custom-call(s32[4]{0:T(128)S(1)} %iota.14.order_ref, bf16[512,1536]{1,0:T(8,128)(2,1)S(1)} %pad_maximum_fusion.refs_0_.refs_1_.refs_2_.refs_3_, bf16[512,1536]{1,0:T(8,128)(2,1)S(1)} %pad_maximum_fusion.refs_0_.refs_1_.refs_2_.refs_3_, bf16[512,1536]{1,0:T(8,128)(2,1)S(1)} %pad_maximum_fusion.refs_0_.refs_1_.refs_2_.refs_3_, ...), custom_call_target="tpu_custom_call" | custom-call | flops 2013265920 | bytes 6160384 | tf_op jit(solution)/shard_map/project/pallas_call | solution.py:209
  178.0 5.7 %project.5 = bf16[256,1280]{1,0:T(8,128)(2,1)S(1)} custom-call(s32[4]{0:T(128)S(1)} %pad_add_fusion.order_ref, bf16[512,1536]{1,0:T(8,128)(2,1)S(1)} %pad_maximum_fusion.refs_0_.refs_1_.refs_2_.refs_3_, bf16[512,1536]{1,0:T(8,128)(2,1)S(1)} %pad_maximum_fusion.refs_0_.refs_1_.refs_2_.refs_3_, ...), custom_call_target="tpu_custom_call" | custom-call | flops 2013265920 | bytes 6160384 | tf_op jit(solution)/shard_map/project/pallas_call | solution.py:209
  183.7 3.4 %collective-permute-start.27 = (bf16[256,1280]{1,0:T(8,128)(2,1)S(1)}, bf16[256,1280]{1,0:T(8,128)(2,1)S(1)}, u32[]{:S(2)}, u32[]{:S(2)}) collective-permute-start(bf16[256,1280]{1,0:T(8,128)(2,1)S(1)} %project.7), channel_id=1, source_target_pairs={{2,0},{6,4},{8,10},{12,14},{3,1},{7,5},{9,11},{13,15},{18,16},{22,... | collective-permute-start | bytes 1966088 | tf_op jit(solution)/shard_map/ppermute | solution.py:345
  188.4 5.7 %project.6 = bf16[256,1280]{1,0:T(8,128)(2,1)S(1)} custom-call(s32[4]{0:T(128)S(1)} %pad_add_fusion.order_ref, bf16[512,1536]{1,0:T(8,128)(2,1)S(1)} %pad_maximum_fusion.refs_0_.refs_1_.refs_2_.refs_3_, bf16[512,1536]{1,0:T(8,128)(2,1)S(1)} %pad_maximum_fusion.refs_0_.refs_1_.refs_2_.refs_3_, ...), custom_call_target="tpu_custom_call" | custom-call | flops 2013265920 | bytes 6160384 | tf_op jit(solution)/shard_map/project/pallas_call | solution.py:209
  194.1 4.6 %collective-permute-start.26 = (bf16[256,1280]{1,0:T(8,128)(2,1)S(1)}, bf16[256,1280]{1,0:T(8,128)(2,1)S(1)}, u32[]{:S(2)}, u32[]{:S(2)}) collective-permute-start(bf16[256,1280]{1,0:T(8,128)(2,1)S(1)} %project.6), channel_id=1, source_target_pairs={{2,0},{4,6},{10,8},{12,14},{3,1},{5,7},{11,9},{13,15},{18,16},{20,... | collective-permute-start | bytes 1966088 | tf_op jit(solution)/shard_map/ppermute | solution.py:345
  198.8 5.7 %project.4 = bf16[256,1280]{1,0:T(8,128)(2,1)S(1)} custom-call(s32[4]{0:T(128)S(1)} %pad_add_fusion.order_ref, bf16[512,1536]{1,0:T(8,128)(2,1)S(1)} %pad_maximum_fusion.refs_0_.refs_1_.refs_2_.refs_3_, bf16[512,1536]{1,0:T(8,128)(2,1)S(1)} %pad_maximum_fusion.refs_0_.refs_1_.refs_2_.refs_3_, ...), custom_call_target="tpu_custom_call" | custom-call | flops 2013265920 | bytes 6160384 | tf_op jit(solution)/shard_map/project/pallas_call | solution.py:209
  205.8 1.5 broadcast_select_fusion.1
  207.3 8.5 %collective-permute-done.26 = bf16[256,1280]{1,0:T(8,128)(2,1)S(1)} collective-permute-done((bf16[256,1280]{1,0:T(8,128)(2,1)S(1)}, bf16[256,1280]{1,0:T(8,128)(2,1)S(1)}, u32[]{:S(2)}, u32[]{:S(2)}) %collective-permute-start.26) | collective-permute-done | bytes 655392 | tf_op jit(solution)/shard_map/ppermute | solution.py:345
  215.8 6.9 %collective-permute-done.18 = bf16[256,1280]{1,0:T(8,128)(2,1)S(1)} collective-permute-done((bf16[256,1280]{1,0:T(8,128)(2,1)S(1)}, bf16[256,1280]{1,0:T(8,128)(2,1)S(1)}, u32[]{:S(2)}, u32[]{:S(2)}) %collective-permute-start.18) | collective-permute-done | bytes 655392 | tf_op jit(solution)/shard_map/ppermute | solution.py:345
  (95 shorter events, 19.6 us)
Async XLA Ops:
  0.0 47.9 %copy-start = (bf16[50,2560]{1,0:T(8,128)(2,1)S(1)}, bf16[50,2560]{1,0:T(8,128)(2,1)}, u32[]{:S(2)}) copy-start(bf16[50,2560]{1,0:T(8,128)(2,1)} %param.22) | copy-start | bytes 768004
  2.3 50.2 %collective-permute-start.8 = (bf16[384,1280]{1,0:T(8,128)(2,1)}, bf16[384,1280]{1,0:T(8,128)(2,1)}, u32[]{:S(2)}, u32[]{:S(2)}) collective-permute-start(bf16[384,1280]{1,0:T(8,128)(2,1)} %constant_dynamic-slice_fusion.4), channel_id=1, source_target_pairs={{0,4},{4,8},{8,12},{1,5},{5,9},{9,13},{2,6},{6,10},{10,14},{3,7},{... | collective-permute-start | bytes 2949128 | tf_op jit(solution)/shard_map/ppermute | solution.py:277
  3.6 50.3 %collective-permute-start.11 = (bf16[384,1280]{1,0:T(8,128)(2,1)}, bf16[384,1280]{1,0:T(8,128)(2,1)}, u32[]{:S(2)}, u32[]{:S(2)}) collective-permute-start(bf16[384,1280]{1,0:T(8,128)(2,1)} %constant_dynamic-slice_fusion.4), channel_id=1, source_target_pairs={{4,0},{8,4},{12,8},{5,1},{9,5},{13,9},{6,2},{10,6},{14,10},{7,3},{... | collective-permute-start | bytes 2949128 | tf_op jit(solution)/shard_map/ppermute | solution.py:278
  9.5 21.4 %copy-start.10 = (pred[4]{0:T(512)(128)(4,1)S(1)}, pred[4]{0:T(512)(128)(4,1)}, u32[]{:S(2)}) copy-start(pred[4]{0:T(512)(128)(4,1)} %constant.62.clone) | copy-start | bytes 16
  9.6 22.0 %copy-start.9 = (pred[4]{0:T(512)(128)(4,1)S(1)}, pred[4]{0:T(512)(128)(4,1)}, u32[]{:S(2)}) copy-start(pred[4]{0:T(512)(128)(4,1)} %constant.61.clone) | copy-start | bytes 16
  16.5 70.2 %copy-start.2 = (bf16[2,2,128,1536]{3,2,1,0:T(8,128)(2,1)}, bf16[2,2,128,1536]{3,2,1,0:T(8,128)(2,1)S(1)}, u32[]{:S(2)}) copy-start(bf16[2,2,128,1536]{3,2,1,0:T(8,128)(2,1)S(1)} %get-tuple-element.15.own_kv) | copy-start | bytes 4718596
  16.5 67.3 %collective-permute-start.4 = (bf16[2,2,128,1536]{3,2,1,0:T(8,128)(2,1)S(1)}, bf16[2,2,128,1536]{3,2,1,0:T(8,128)(2,1)}, u32[]{:S(2)}, u32[]{:S(2)}) collective-permute-start(bf16[2,2,128,1536]{3,2,1,0:T(8,128)(2,1)S(1)} %get-tuple-element.15.own_kv), channel_id=1, source_target_pairs={{4,0},{8,4},{12,8},{6,2},{10,6},{14,10},{20,16},{24,20},{28,24},{2... | collective-permute-start | bytes 4718600 | tf_op jit(solution)/shard_map/ppermute | solution.py:286
  19.1 116.0 %collective-permute-start.3 = (bf16[2,2,128,1536]{3,2,1,0:T(8,128)(2,1)S(1)}, bf16[2,2,128,1536]{3,2,1,0:T(8,128)(2,1)}, u32[]{:S(2)}, u32[]{:S(2)}) collective-permute-start(bf16[2,2,128,1536]{3,2,1,0:T(8,128)(2,1)S(1)} %get-tuple-element.15.own_kv), channel_id=1, source_target_pairs={{0,1},{1,0},{2,3},{3,2},{4,5},{5,4},{6,7},{7,6},{8,9},{9,8},{10,11... | collective-permute-start | bytes 4718600 | tf_op jit(solution)/shard_map/ppermute | solution.py:291
  19.1 26.9 %collective-permute-start.17 = (s32[1]{0:T(128)}, s32[1]{0:T(128)}, u32[]{:S(2)}, u32[]{:S(2)}) collective-permute-start(s32[1]{0:T(128)} %param.21), channel_id=1, source_target_pairs={{4,0},{8,4},{12,8},{5,1},{9,5},{13,9},{6,2},{10,6},{14,10},{7,3},{... | collective-permute-start | bytes 20 | tf_op jit(solution)/shard_map/ppermute | solution.py:303
  45.9 35.8 %collective-permute-start.2 = (bf16[2,128,1536]{2,1,0:T(8,128)(2,1)S(1)}, bf16[2,128,1536]{2,1,0:T(8,128)(2,1)S(1)}, u32[]{:S(2)}, u32[]{:S(2)}) collective-permute-start(bf16[2,128,1536]{2,1,0:T(8,128)(2,1)S(1)} %get-tuple-element.13), channel_id=1, source_target_pairs={{4,1},{5,0},{8,5},{9,4},{12,9},{13,8},{6,3},{7,2},{10,7},{11,6},{1... | collective-permute-start | bytes 2359304 | tf_op jit(solution)/shard_map/ppermute | solution.py:287
  52.5 27.9 %collective-permute-start.9 = (bf16[384,1280]{1,0:T(8,128)(2,1)}, bf16[384,1280]{1,0:T(8,128)(2,1)S(1)}, u32[]{:S(2)}, u32[]{:S(2)}) collective-permute-start(bf16[384,1280]{1,0:T(8,128)(2,1)} %collective-permute-done.8), channel_id=1, source_target_pairs={{4,8},{8,12},{5,9},{9,13},{6,10},{10,14},{7,11},{11,15},{20,24},{2... | collective-permute-start | bytes 2949128 | tf_op jit(solution)/shard_map/ppermute | solution.py:277
  53.8 31.4 %collective-permute-start.12 = (bf16[384,1280]{1,0:T(8,128)(2,1)}, bf16[384,1280]{1,0:T(8,128)(2,1)S(1)}, u32[]{:S(2)}, u32[]{:S(2)}) collective-permute-start(bf16[384,1280]{1,0:T(8,128)(2,1)} %collective-permute-done.11), channel_id=1, source_target_pairs={{4,0},{8,4},{5,1},{9,5},{6,2},{10,6},{7,3},{11,7},{20,16},{24,20},... | collective-permute-start | bytes 2949128 | tf_op jit(solution)/shard_map/ppermute | solution.py:278
  80.4 25.7 %collective-permute-start.10 = (bf16[384,1280]{1,0:T(8,128)(2,1)S(1)}, bf16[384,1280]{1,0:T(8,128)(2,1)S(1)}, u32[]{:S(2)}, u32[]{:S(2)}) collective-permute-start(bf16[384,1280]{1,0:T(8,128)(2,1)S(1)} %collective-permute-done.9), channel_id=1, source_target_pairs={{8,12},{9,13},{10,14},{11,15},{24,28},{25,29},{26,30},{27,31}} | collective-permute-start | bytes 2949128 | tf_op jit(solution)/shard_map/ppermute | solution.py:277
  81.8 5.0 %collective-permute-start.6 = (bf16[2,128,1536]{2,1,0:T(8,128)(2,1)S(1)}, bf16[2,128,1536]{2,1,0:T(8,128)(2,1)S(1)}, u32[]{:S(2)}, u32[]{:S(2)}) collective-permute-start(bf16[2,128,1536]{2,1,0:T(8,128)(2,1)S(1)} %collective-permute-done.2.far_q), channel_id=1, source_target_pairs={{0,1},{2,3},{4,5},{6,7},{8,9},{10,11},{12,13},{14,15},{16,17},{18,... | collective-permute-start | bytes 2359304 | tf_op jit(solution)/shard_map/ppermute | solution.py:293
  83.9 48.4 %collective-permute-start.5 = (bf16[2,2,128,1536]{3,2,1,0:T(8,128)(2,1)}, bf16[2,2,128,1536]{3,2,1,0:T(8,128)(2,1)S(1)}, u32[]{:S(2)}, u32[]{:S(2)}) collective-permute-start(bf16[2,2,128,1536]{3,2,1,0:T(8,128)(2,1)} %collective-permute-done.4), channel_id=1, source_target_pairs={{0,1},{2,3},{4,5},{6,7},{8,9},{10,11},{12,13},{14,15},{16,17},{18,... | collective-permute-start | bytes 4718600 | tf_op jit(solution)/shard_map/ppermute | solution.py:292
  85.3 22.4 %collective-permute-start.13 = (bf16[384,1280]{1,0:T(8,128)(2,1)S(1)}, bf16[384,1280]{1,0:T(8,128)(2,1)S(1)}, u32[]{:S(2)}, u32[]{:S(2)}) collective-permute-start(bf16[384,1280]{1,0:T(8,128)(2,1)S(1)} %collective-permute-done.12), channel_id=1, source_target_pairs={{4,0},{5,1},{6,2},{7,3},{20,16},{21,17},{22,18},{23,19}} | collective-permute-start | bytes 2949128 | tf_op jit(solution)/shard_map/ppermute | solution.py:278
  86.8 25.1 %collective-permute-start.1 = (bf16[2,128,1536]{2,1,0:T(8,128)(2,1)S(1)}, bf16[2,128,1536]{2,1,0:T(8,128)(2,1)S(1)}, u32[]{:S(2)}, u32[]{:S(2)}) collective-permute-start(bf16[2,128,1536]{2,1,0:T(8,128)(2,1)S(1)} %get-tuple-element.12), channel_id=1, source_target_pairs={{0,1},{1,0},{2,3},{3,2},{4,5},{5,4},{6,7},{7,6},{8,9},{9,8},{10,11... | collective-permute-start | bytes 2359304 | tf_op jit(solution)/shard_map/ppermute | solution.py:290
  106.0 24.7 %collective-permute-start.19 = (bf16[384,1280]{1,0:T(8,128)(2,1)S(1)}, bf16[384,1280]{1,0:T(8,128)(2,1)S(1)}, u32[]{:S(2)}, u32[]{:S(2)}) collective-permute-start(bf16[384,1280]{1,0:T(8,128)(2,1)S(1)} %broadcast_select_fusion.3.refs_4_), channel_id=1, source_target_pairs={{0,16},{16,0},{1,17},{17,1},{2,18},{18,2},{3,19},{19,3},{4,20},{20... | collective-permute-start | bytes 2949128 | tf_op jit(solution)/shard_map/ppermute | solution.py:332
  107.7 42.6 %collective-permute-start.20 = (bf16[384,1280]{1,0:T(8,128)(2,1)S(1)}, bf16[384,1280]{1,0:T(8,128)(2,1)S(1)}, u32[]{:S(2)}, u32[]{:S(2)}) collective-permute-start(bf16[384,1280]{1,0:T(8,128)(2,1)S(1)} %broadcast_select_fusion.3.refs_4_), channel_id=1, source_target_pairs={{0,1},{1,0},{2,3},{3,2},{4,5},{5,4},{6,7},{7,6},{8,9},{9,8},{10,11... | collective-permute-start | bytes 2949128 | tf_op jit(solution)/shard_map/ppermute | solution.py:333
  111.9 43.6 %collective-permute-start.23 = (bf16[384,1280]{1,0:T(8,128)(2,1)S(1)}, bf16[384,1280]{1,0:T(8,128)(2,1)S(1)}, u32[]{:S(2)}, u32[]{:S(2)}) collective-permute-start(bf16[384,1280]{1,0:T(8,128)(2,1)S(1)} %get-tuple-element.21.refs_4_), channel_id=1, source_target_pairs={{0,16},{16,0},{1,17},{17,1},{2,18},{18,2},{3,19},{19,3},{4,20},{20... | collective-permute-start | bytes 2949128 | tf_op jit(solution)/shard_map/ppermute | solution.py:332
  130.7 40.4 %collective-permute-start.14 = (bf16[384,1280]{1,0:T(8,128)(2,1)S(1)}, bf16[384,1280]{1,0:T(8,128)(2,1)S(1)}, u32[]{:S(2)}, u32[]{:S(2)}) collective-permute-start(bf16[384,1280]{1,0:T(8,128)(2,1)S(1)} %get-tuple-element.22.refs_4_), channel_id=1, source_target_pairs={{0,16},{16,0},{1,17},{17,1},{2,18},{18,2},{3,19},{19,3},{4,20},{20... | collective-permute-start | bytes 2949128 | tf_op jit(solution)/shard_map/ppermute | solution.py:332
  132.3 23.2 %collective-permute-start.21 = (bf16[384,1280]{1,0:T(8,128)(2,1)S(1)}, bf16[384,1280]{1,0:T(8,128)(2,1)}, u32[]{:S(2)}, u32[]{:S(2)}) collective-permute-start(bf16[384,1280]{1,0:T(8,128)(2,1)S(1)} %collective-permute-done.19.refs_5_), channel_id=1, source_target_pairs={{0,1},{1,0},{2,3},{3,2},{4,5},{5,4},{6,7},{7,6},{8,9},{9,8},{10,11... | collective-permute-start | bytes 2949128 | tf_op jit(solution)/shard_map/ppermute | solution.py:334
  149.4 2.7 %collective-permute-start.7 = (bf16[128,1536]{1,0:T(8,128)(2,1)S(1)}, bf16[128,1536]{1,0:T(8,128)(2,1)S(1)}, u32[]{:S(2)}, u32[]{:S(2)}) collective-permute-start(bf16[128,1536]{1,0:T(8,128)(2,1)S(1)} %get-tuple-element.18), channel_id=1, source_target_pairs={{5,1},{9,5},{13,9},{7,3},{11,7},{15,11},{21,17},{25,21},{29,25},{2... | collective-permute-start | bytes 1179656 | tf_op jit(solution)/shard_map/ppermute | solution.py:298
  150.2 55.6 %collective-permute-start = (bf16[2,128,2560]{2,1,0:T(8,128)(2,1)}, bf16[2,128,2560]{2,1,0:T(8,128)(2,1)}, u32[]{:S(2)}, u32[]{:S(2)}) collective-permute-start(bf16[2,128,2560]{2,1,0:T(8,128)(2,1)} %param.18), channel_id=1, source_target_pairs={{1,0},{4,1},{5,4},{8,5},{9,8},{12,9},{13,12},{3,2},{6,3},{7,6},{10... | collective-permute-start | bytes 3932168 | tf_op jit(solution)/shard_map/ppermute | solution.py:313
  152.2 31.5 %collective-permute-start.24 = (bf16[384,1280]{1,0:T(8,128)(2,1)S(1)}, bf16[384,1280]{1,0:T(8,128)(2,1)S(1)}, u32[]{:S(2)}, u32[]{:S(2)}) collective-permute-start(bf16[384,1280]{1,0:T(8,128)(2,1)S(1)} %get-tuple-element.21.refs_4_), channel_id=1, source_target_pairs={{0,1},{1,0},{2,3},{3,2},{4,5},{5,4},{6,7},{7,6},{8,9},{9,8},{10,11... | collective-permute-start | bytes 2949128 | tf_op jit(solution)/shard_map/ppermute | solution.py:333
  155.4 38.7 %collective-permute-start.15 = (bf16[384,1280]{1,0:T(8,128)(2,1)S(1)}, bf16[384,1280]{1,0:T(8,128)(2,1)S(1)}, u32[]{:S(2)}, u32[]{:S(2)}) collective-permute-start(bf16[384,1280]{1,0:T(8,128)(2,1)S(1)} %get-tuple-element.22.refs_4_), channel_id=1, source_target_pairs={{0,1},{1,0},{2,3},{3,2},{4,5},{5,4},{6,7},{7,6},{8,9},{9,8},{10,11... | collective-permute-start | bytes 2949128 | tf_op jit(solution)/shard_map/ppermute | solution.py:333
  155.5 31.7 %collective-permute-start.25 = (bf16[384,1280]{1,0:T(8,128)(2,1)S(1)}, bf16[384,1280]{1,0:T(8,128)(2,1)}, u32[]{:S(2)}, u32[]{:S(2)}) collective-permute-start(bf16[384,1280]{1,0:T(8,128)(2,1)S(1)} %collective-permute-done.23.refs_5_), channel_id=1, source_target_pairs={{0,1},{1,0},{2,3},{3,2},{4,5},{5,4},{6,7},{7,6},{8,9},{9,8},{10,11... | collective-permute-start | bytes 2949128 | tf_op jit(solution)/shard_map/ppermute | solution.py:334
  171.1 27.6 %collective-permute-start.16 = (bf16[384,1280]{1,0:T(8,128)(2,1)S(1)}, bf16[384,1280]{1,0:T(8,128)(2,1)}, u32[]{:S(2)}, u32[]{:S(2)}) collective-permute-start(bf16[384,1280]{1,0:T(8,128)(2,1)S(1)} %collective-permute-done.14.refs_5_), channel_id=1, source_target_pairs={{0,1},{1,0},{2,3},{3,2},{4,5},{5,4},{6,7},{7,6},{8,9},{9,8},{10,11... | collective-permute-start | bytes 2949128 | tf_op jit(solution)/shard_map/ppermute | solution.py:334
  183.7 23.6 %collective-permute-start.27 = (bf16[256,1280]{1,0:T(8,128)(2,1)S(1)}, bf16[256,1280]{1,0:T(8,128)(2,1)S(1)}, u32[]{:S(2)}, u32[]{:S(2)}) collective-permute-start(bf16[256,1280]{1,0:T(8,128)(2,1)S(1)} %project.7), channel_id=1, source_target_pairs={{2,0},{6,4},{8,10},{12,14},{3,1},{7,5},{9,11},{13,15},{18,16},{22,... | collective-permute-start | bytes 1966088 | tf_op jit(solution)/shard_map/ppermute | solution.py:345
  187.1 20.1 %collective-permute-start.22 = (bf16[256,1280]{1,0:T(8,128)(2,1)S(1)}, bf16[256,1280]{1,0:T(8,128)(2,1)S(1)}, u32[]{:S(2)}, u32[]{:S(2)}) collective-permute-start(bf16[256,1280]{1,0:T(8,128)(2,1)S(1)} %project.5), channel_id=1, source_target_pairs={{0,2},{4,6},{10,8},{14,12},{1,3},{5,7},{11,9},{15,13},{16,18},{20,... | collective-permute-start | bytes 1966088 | tf_op jit(solution)/shard_map/ppermute | solution.py:345
  194.1 21.6 %collective-permute-start.26 = (bf16[256,1280]{1,0:T(8,128)(2,1)S(1)}, bf16[256,1280]{1,0:T(8,128)(2,1)S(1)}, u32[]{:S(2)}, u32[]{:S(2)}) collective-permute-start(bf16[256,1280]{1,0:T(8,128)(2,1)S(1)} %project.6), channel_id=1, source_target_pairs={{2,0},{4,6},{10,8},{12,14},{3,1},{5,7},{11,9},{13,15},{18,16},{20,... | collective-permute-start | bytes 1966088 | tf_op jit(solution)/shard_map/ppermute | solution.py:345
  204.5 18.2 %collective-permute-start.18 = (bf16[256,1280]{1,0:T(8,128)(2,1)S(1)}, bf16[256,1280]{1,0:T(8,128)(2,1)S(1)}, u32[]{:S(2)}, u32[]{:S(2)}) collective-permute-start(bf16[256,1280]{1,0:T(8,128)(2,1)S(1)} %project.4), channel_id=1, source_target_pairs={{0,2},{6,4},{8,10},{14,12},{1,3},{7,5},{9,11},{15,13},{16,18},{22,... | collective-permute-start | bytes 1966088 | tf_op jit(solution)/shard_map/ppermute | solution.py:345
  (12 other events, 115.1 us)

commit v2 on v1

v2 whole, which is shorter than its diff:
```python
import functools
import math

import jax
import jax.numpy as jnp
from jax import lax
from jax.experimental import pallas as pl
from jax.experimental.pallas import tpu as pltpu
from jax.sharding import PartitionSpec as P

HD = 128
BF16 = jnp.bfloat16
F32 = jnp.float32
VMEM_LIMIT = 16 * 1024 * 1024


COST = pl.CostEstimate(flops=1000, bytes_accessed=1000, transcendentals=0)


def params(*semantics):
    return pltpu.CompilerParams(dimension_semantics=semantics or None, vmem_limit_bytes=VMEM_LIMIT)


def rotation_tables(times):
    half = HD // 2
    pair_index = jnp.arange(half, dtype=F32)
    frequency = jnp.power(F32(10000.0), -pair_index / half)
    angles = times.astype(F32)[:, None] * frequency[None, :]
    cosine, sine = jnp.cos(angles), jnp.sin(angles)
    return (
        jnp.concatenate([cosine, cosine], axis=1),
        jnp.concatenate([-sine, sine], axis=1),
    )


def rotate_kernel(core_ref, cos_ref, sin_ref, own_ref, new_ref, q_ref, kv_ref, side_ref, nq_ref, nkv_ref):
    frames = own_ref.shape[1]
    heads = own_ref.shape[-1] // HD
    first_core = core_ref[0] == 0

    def turn(block, row):
        block = block.astype(F32)
        out = block * cos_ref[row : row + 1, :] + pltpu.roll(block, HD // 2, 1) * sin_ref[row : row + 1, :]
        return out.astype(BF16)

    for head in range(heads):
        at = slice(head * HD, (head + 1) * HD)
        for frame in range(frames):
            query = turn(own_ref[0, frame, :, at], frame)
            q_ref[frame, :, at] = query
            kv_ref[0, frame, :, at] = turn(own_ref[1, frame, :, at], frame)
            kv_ref[1, frame, :, at] = own_ref[2, frame, :, at]
            nq_ref[frame, :, at] = turn(new_ref[frame, 0, :, at], frames + frame)
            nkv_ref[0, frame, :, at] = turn(new_ref[frame, 1, :, at], frames + frame)
            nkv_ref[1, frame, :, at] = new_ref[frame, 2, :, at]

    @pl.when(first_core)
    def _():
        side_ref[...] = q_ref[...]

    @pl.when(jnp.logical_not(first_core))
    def _():
        side_ref[0] = kv_ref[0, 0]
        side_ref[1] = kv_ref[1, 0]


def rotate_all(core, cos, sin, own, new):
    _, frames, tokens, channels = own.shape
    wide = min(channels, 3 * HD)
    steps = channels // wide
    three = pl.BlockSpec((frames, tokens, wide), lambda i, c: (0, 0, i))
    four = pl.BlockSpec((2, frames, tokens, wide), lambda i, c: (0, 0, 0, i))
    table = pl.BlockSpec(cos.shape, lambda i, c: (0, 0))
    sq = jax.ShapeDtypeStruct((frames, tokens, channels), BF16)
    skv = jax.ShapeDtypeStruct((2, frames, tokens, channels), BF16)
    return pl.pallas_call(
        rotate_kernel,
        grid_spec=pltpu.PrefetchScalarGridSpec(
            num_scalar_prefetch=1,
            grid=(steps,),
            in_specs=[
                table,
                table,
                pl.BlockSpec((3, frames, tokens, wide), lambda i, c: (0, 0, 0, i)),
                pl.BlockSpec((frames, 3, tokens, wide), lambda i, c: (0, 0, 0, i)),
            ],
            out_specs=[three, four, three, three, four],
        ),
        out_shape=[sq, skv, sq, sq, skv],
        compiler_params=params("arbitrary"),
        cost_estimate=COST,
        name="rotate",
    )(core, cos, sin, own, new)


def attend_kernel(
    where_ref, peer_q, far_q, new_q, own_kv, peer_kv, far_kv, far_kv_1, new_kv, far6_kv_1, send_ref, keep_ref
):
    tokens = peer_q.shape[1]
    heads = peer_q.shape[-1] // HD
    core, first, last = where_ref[0], where_ref[1] == 1, where_ref[2] == 1
    second_core = core == 1
    factor = math.log2(math.e) / math.sqrt(HD)

    def one(at):
        def frames_of(side):
            own = [own_kv[side, frame, :, at] for frame in range(2)]
            peer = [peer_kv[side, frame, :, at] for frame in range(2)]
            rows = [jnp.where(second_core, p, o) for o, p in zip(own, peer)]
            rows += [jnp.where(second_core, o, p) for o, p in zip(own, peer)]
            for frame in range(2):
                far = jnp.where(second_core, far_kv_1[side, frame, :, at], far_kv[side, frame, :, at])
                rows.append(jnp.where(last, new_kv[side, frame, :, at], far))
            return rows + [jnp.where(second_core, far6_kv_1[side, :, at], far_q[side, :, at])]

        keys, values = frames_of(0), frames_of(1)

        def mix(query, low):
            rows = lax.dot_general(
                query,
                jnp.concatenate(keys[low : low + 6], axis=0),
                (((1,), (1,)), ((), ())),
                preferred_element_type=F32,
            )
            part = [rows[:, i * tokens : (i + 1) * tokens] for i in range(6)]
            part[0] = jnp.where(first, -1e30, part[0])
            part[5] = jnp.where(last, -1e30, part[5])
            rows = jnp.concatenate(part, axis=1)
            top = jnp.max(rows, axis=1, keepdims=True)
            weights = jnp.exp2((rows - top) * factor)
            total = jnp.sum(weights, axis=1, keepdims=True)
            out = jnp.dot(
                weights.astype(BF16),
                jnp.concatenate(values[low : low + 6], axis=0),
                preferred_element_type=F32,
            )
            return (out * (1.0 / total)).astype(BF16)

        q4 = jnp.where(last, new_q[0, :, at], far_q[0, :, at])
        q5 = jnp.where(last, new_q[1, :, at], far_q[1, :, at])
        qa = jnp.where(second_core, q4, peer_q[0, :, at])
        qc = jnp.where(second_core, q5, peer_q[1, :, at])
        early = mix(jnp.concatenate([qa, peer_q[1, :, at]], axis=0), 0)
        late = mix(jnp.concatenate([qa, qc], axis=0), 1)
        keep_ref[0, :, at] = early[:tokens]
        send_ref[:, at] = early[tokens:]
        keep_ref[1, :, at] = late[:tokens]
        keep_ref[2, :, at] = late[tokens:]

    group = 4 if heads % 4 == 0 else 1

    @pl.loop(0, heads // group)
    def _(step):
        for head in range(group):
            one(pl.ds(pl.multiple_of((step * group + head) * HD, HD), HD))


def attend(where, *operands):
    _, tokens, channels = operands[0].shape
    return pl.pallas_call(
        attend_kernel,
        in_specs=[pl.BlockSpec(memory_space=pltpu.SMEM)] + [pl.BlockSpec(memory_space=pltpu.VMEM)] * len(operands),
        out_specs=[pl.BlockSpec(memory_space=pltpu.VMEM)] * 2,
        out_shape=[
            jax.ShapeDtypeStruct((tokens, channels), BF16),
            jax.ShapeDtypeStruct((3, tokens, channels), BF16),
        ],
        compiler_params=params(),
        cost_estimate=COST,
        name="attend",
    )(where, *operands)


def project_kernel(half, place_ref, mix_ref, gate_ref, *refs):
    pieces, out_ref = refs[:-1], refs[-1]
    group, core, gate_at = place_ref[0], place_ref[1], place_ref[2]
    channels = mix_ref.shape[1]
    tokens = mix_ref.shape[0] // 8
    depth = channels // 2
    if len(pieces) == 1:
        widths = [256] * (half // 256) + [half % 256] * (half % 256 > 0)
    else:
        widths = [piece.shape[1] for piece in pieces[::2]]
    low = 0
    for i, wide in enumerate(widths):
        if len(pieces) == 1:
            at = pl.ds(pl.multiple_of(core * half + low, HD), wide)
            total = jnp.dot(mix_ref[...], pieces[0][:, at], preferred_element_type=F32)
        else:
            near = mix_ref[:, pl.ds(pl.multiple_of(group * depth, HD), depth)]
            far = mix_ref[:, pl.ds(pl.multiple_of((1 - group) * depth, HD), depth)]
            total = jnp.dot(near, pieces[2 * i][...], preferred_element_type=F32)
            total = total + jnp.dot(far, pieces[2 * i + 1][...], preferred_element_type=F32)
        at = pl.ds(pl.multiple_of(gate_at + low, HD), wide)
        row = gate_ref[0:1, at]
        parts = [total[n * tokens : (n + 1) * tokens] for n in range(8)]
        for who in range(2):
            crossing = gate_ref[1 + who : 2 + who, at]
            p = parts[4 * who : 4 * who + 4]
            base = 2 * who * tokens
            out_ref[base : base + tokens, low : low + wide] = ((p[0] + p[2]) * row).astype(BF16)
            out_ref[base + tokens : base + 2 * tokens, low : low + wide] = (p[1] * crossing + p[3] * row).astype(BF16)
        low += wide


def project(group, core, half, gate_at, mix, pieces, gates):
    rows, channels = mix.shape
    columns = half if len(pieces) == 1 else sum(piece.shape[1] for piece in pieces[::2])
    depth = channels // 2
    if depth % HD or half % HD:
        if len(pieces) == 1:
            weights = lax.dynamic_slice_in_dim(pieces[0], core * half, half, axis=1)
        else:
            weights = [
                jnp.where(group == 0, jnp.concatenate([own, other]), jnp.concatenate([other, own]))
                for own, other in zip(pieces[::2], pieces[1::2])
            ]
            weights = jnp.concatenate(weights, axis=1)
        total = jnp.dot(mix, weights, preferred_element_type=F32).reshape(2, 4, rows // 8, columns)
        gates = lax.dynamic_slice_in_dim(gates, gate_at, columns, axis=1)
        even = (total[:, 0] + total[:, 2]) * gates[0]
        odd = total[:, 1] * gates[1:, None, :] + total[:, 3] * gates[0]
        return jnp.stack([even, odd], axis=1).reshape(rows // 2, columns).astype(BF16)

    place = jnp.stack([group, core, gate_at]).astype(jnp.int32)
    return pl.pallas_call(
        functools.partial(project_kernel, half),
        in_specs=[pl.BlockSpec(memory_space=pltpu.SMEM)]
        + [pl.BlockSpec(memory_space=pltpu.VMEM)] * (2 + len(pieces)),
        out_specs=pl.BlockSpec(memory_space=pltpu.VMEM),
        out_shape=jax.ShapeDtypeStruct((rows // 2, columns), BF16),
        compiler_params=params(),
        cost_estimate=COST,
        name="project",
    )(place, mix, gates, *pieces)


def arrivals(count):
    table = []
    for k in range(1, count):
        row = []
        for q in range(count):
            ahead, behind = count - 1 - q, q
            if q < count // 2:
                row.append(("down", k) if k <= ahead else ("up", k - ahead))
            else:
                row.append(("up", k) if k <= behind else ("down", k - behind))
        table.append(row)
    return table


def pick(place, row, held):
    value = None
    for source in sorted(set(row)):
        here = functools.reduce(jnp.logical_or, [place == q for q, r in enumerate(row) if r == source])
        value = held(source) if value is None else jnp.where(here, held(source), value)
    return value


def look_up(place, row):
    return sum(jnp.where(place == q, value, 0) for q, value in enumerate(row))


def after(value, *done):
    return lax.optimization_barrier((value, done))[0]


def local(
    latent,
    projections,
    frame_times,
    levels,
    gates,
    out_weight,
    incoming_latent,
    incoming_proj,
    incoming_times,
):
    place, count = lax.axis_index("queue"), lax.axis_size("queue")
    core, cores = lax.axis_index("seq"), lax.axis_size("seq")
    side, sides = lax.axis_index("heads"), lax.axis_size("heads")
    group, groups = lax.axis_index("groups"), lax.axis_size("groups")
    first, last = place == 0, place == count - 1
    frames, tokens, features = latent.shape
    assert cores == 2 and frames == 2 and groups == 2 and count % sides == 0
    columns = out_weight.shape[1]
    half = columns // 2
    swap = [(0, 1), (1, 0)]
    pair = ("queue", "seq")
    table = arrivals(count)
    block_of = [list(range(count))]
    for row in table:
        block_of.append([q + hops if way == "down" else q - hops for q, (way, hops) in enumerate(row)])

    next_level = lax.ppermute(levels, "queue", [(i + 1, i) for i in range(count - 1)])
    depth = out_weight.shape[0] // 2
    cuts = [0, half]
    if half % HD == 0 and half > HD:
        cuts = [0, (half // HD + 1) // 2 * HD, half]
    chunks = list(zip(cuts[:-1], cuts[1:]))
    origin = lax.dynamic_slice(out_weight, (group * depth, core * half), (depth, half))
    whole = [(0, half)]
    held = {}

    def send_weights(name, block, low, hops, ends):
        for way, part, sign in (("up", block[0], 1), ("down", block[1], -1)):
            pairs = [(i, i + hops) for i in range(count - hops) if i >= ends]
            if sign < 0:
                pairs = [(count - 1 - i, count - 1 - j) for i, j in pairs]
            held[way, name, low] = lax.ppermute(part, "queue", pairs)

    gathered = {}

    def spread(k, low, high, *done):
        sources = {key: held[key + (0,)] for key in table[k - 1]}
        if done:
            sources = after(sources, *done)
        own = pick(place, table[k - 1], lambda key: sources[key][:, low:high])
        gathered[k, low] = (own, lax.ppermute(own, "groups", swap))
        return own

    send_weights(1, (origin, origin), 0, 1, 0)
    if count > 2:
        send_weights(2, (held["up", 1, 0], held["down", 1, 0]), 0, 1, 1)

    spread(1, 0, half)

    cos, sin = rotation_tables(jnp.concatenate([frame_times, incoming_times]))
    where = jnp.stack([core, first.astype(jnp.int32), last.astype(jnp.int32)])
    own_q, own_kv, side_out, new_q, new_kv = rotate_all(where, cos, sin, projections, incoming_proj)
    peer_q = lax.ppermute(own_q, "seq", swap)
    peer_kv = lax.ppermute(own_kv, "seq", swap)
    side_in = lax.ppermute(
        side_out, pair, [(2 * i + 2 + s, 2 * i + 1 - s) for i in range(count - 1) for s in range(2)]
    )
    far_kv = lax.ppermute(own_kv, pair, [(2 * i + 2, 2 * i) for i in range(count - 1)])
    far6_1 = lax.ppermute(after(side_in, gathered[1, 0][0]), "seq", [(0, 1)])
    far_kv = after(far_kv, peer_q, peer_kv, gathered[1, 0][1], held["up", 2, 0], held["down", 2, 0])
    far_kv_1 = lax.ppermute(far_kv, "seq", [(0, 1)])
    inputs = (peer_q, side_in, new_q, own_kv, peer_kv, far_kv, far_kv_1, new_kv, far6_1)

    send, keep = attend(where, *inputs)
    came = lax.ppermute(send, pair, [(2 * i + 3, 2 * i + 1) for i in range(count - 1)])
    for hop in range(3, count):
        send_weights(hop, (held["up", hop - 1, 0], held["down", hop - 1, 0]), 0, 1, hop - 1)
        came = after(came, spread(hop - 1, 0, half))
    k = count - 1
    for low, high in chunks:
        came = after(came, spread(k, low, high, keep))
    peer_keep = lax.ppermute(keep, "seq", swap)
    second = jnp.where(core == 0, send, came)
    peer_second = lax.ppermute(second, "seq", swap)
    mix = jnp.concatenate(
        [keep[0], second, keep[1], keep[2], peer_keep[0], peer_second, peer_keep[1], peer_keep[2]], axis=0
    )

    moved = lax.ppermute(after(latent, second), pair, [(i + 1, i) for i in range(2 * count - 1)])
    moved = jnp.where(jnp.logical_and(last, core == 1), incoming_latent, moved)
    moved = moved.reshape(frames * tokens, features)

    chosen = jnp.concatenate([levels, after(next_level, far_kv)])
    one_hot = (jnp.arange(gates.shape[0], dtype=jnp.int32)[None, :] == chosen[:, None]).astype(BF16)
    rows = jnp.dot(one_hot, gates, preferred_element_type=F32).astype(BF16)
    if sides == 2:
        other = lax.ppermute(rows, "heads", swap)
        rows = jnp.concatenate(
            [jnp.where(side == 0, rows, other), jnp.where(side == 0, other, rows)], axis=1
        )
    else:
        rows = lax.all_gather(rows, "heads", axis=1, tiled=True)
    rows = rows.astype(F32)
    crossing = jnp.where(last, 0.0, rows[1:2])
    gate_rows = jnp.concatenate(
        [rows[:1], jnp.where(core == 0, rows[:1], crossing), jnp.where(core == 0, crossing, rows[:1])], axis=0
    )

    per_side = count // sides
    flat = ("queue", "heads")

    def summed(k, pieces, low, *done):
        block = look_up(place, block_of[k])
        rows = after(mix, *done) if done else mix
        delta = project(group, core, half, block * columns + core * half + low, rows, pieces, gate_rows)
        if sides != 2:
            return block, delta, None
        pairs = [
            (q * 2 + 1 - block_of[k][q] // per_side, q * 2 + block_of[k][q] // per_side) for q in range(count)
        ]
        return block, delta, lax.ppermute(delta, flat, pairs)

    results = [summed(0, [out_weight], 0)]
    for n in range(1, k):
        done = [gathered[k, low][1] for low, _ in chunks[n - 1 : n]]
        results.append(summed(n, gathered[n, 0], 0, *done))
    late = []
    for n, (low, high) in enumerate(chunks):
        own, other = gathered[k, low]
        other = after(other, *[part for part in results[0][1:] + results[min(n + 1, k - 1)][1:2] if part is not None])
        late.append((low, summed(k, [own, other], low)))
    if sides != 2:
        results += [result for _, result in late]
        change = jnp.zeros((2 * frames * tokens, count * half), BF16)
        for n, (block, delta, _) in enumerate(results):
            low = late[n - count + 1][0] if n >= count - 1 else 0
            change = lax.dynamic_update_slice_in_dim(change, delta, block * half + low, axis=1)
        early = lax.psum_scatter(change, "heads", scatter_dimension=1, tiled=True)
        late = []
    else:
        early = []
        for b in range(per_side):
            total = 0.0
            for block, delta, other in results:
                change = delta.astype(F32) + other.astype(F32)
                total = total + jnp.where(block == side * per_side + b, change, 0.0)
            early.append(total)
        early = jnp.concatenate(early, axis=1).astype(BF16)

    mine = frames * tokens
    early_back = lax.ppermute(early[mine:], "seq", swap)
    tail = []
    for low, (block, delta, other) in late:
        total = (delta.astype(F32) + other.astype(F32)).astype(BF16)
        tail.append((low, low + delta.shape[1], block, total[:mine], lax.ppermute(total[mine:], "seq", swap)))

    parts = []
    for b in range(per_side):
        for who in range(2):
            for low, high in chunks:
                at = b * half + low
                change = jnp.where(core == who, early[:mine, at : at + high - low], early_back[:, at : at + high - low])
                change = change.astype(F32)
                for start, _, block, own, back in tail:
                    if start == low:
                        last_part = jnp.where(core == who, own, back).astype(F32)
                        change = change + jnp.where(block == side * per_side + b, last_part, 0.0)
                at = b * columns + who * half + low
                parts.append((moved[:, at : at + high - low].astype(F32) + change).astype(BF16))
    return jnp.concatenate(parts, axis=1).reshape(frames, tokens, features)


def solution(mesh):
    return jax.shard_map(
        local,
        mesh=mesh,
        in_specs=(
            P(("groups", "queue", "seq"), None, "heads"),
            P(None, ("groups", "queue", "seq"), None, "heads"),
            P(("groups", "queue", "seq")),
            P(("groups", "queue")),
            P(None, "heads"),
            P("heads", "queue"),
            P("groups", None, "heads"),
            P("groups", None, None, "heads"),
            P("groups"),
        ),
        out_specs=P(("groups", "queue", "seq"), None, "heads"),
        check_vma=False,
    )
```

time: 226 us -> 182 us (0.81)
  the two profiles are of different devices: /device:TPU:24 before, /device:TPU:9 now
where the time goes in v2:
time: 182 us; the launch traced here: 180 us
  waiting for transfers between devices  66.5 us (37%)
  starting transfers between devices  55.5 us (30%)
  Pallas kernels  33.2 us (18%)
  other arithmetic  12.5 us (7%)
  local copies, waits for them, and re-layouts  10.9 us (6%)
    ppermute x6, waiting for transfers between devices, send_weights(): held[way, name, low] = lax.ppermute(part, 'queue', pairs)  25.5 us
    ppermute x6, starting transfers between devices, send_weights(): held[way, name, low] = lax.ppermute(part, 'queue', pairs)  17.3 us
    pallas_call x5, Pallas kernels, project(): pl.pallas_call(functools.partial(project_kernel, half), in_specs=[pl.Bloc...  16.5 us
    pallas_call x1, Pallas kernels, attend(): pl.pallas_call(attend_kernel, in_specs=[pl.BlockSpec(memory_space=pltpu.S...  12.9 us
    ppermute x1, waiting for transfers between devices, local(): lax.ppermute(side_out, pair, [(2 * i + 2 + s, 2 * i + 1 - s) for i in ran...  11.4 us
    ppermute x5, waiting for transfers between devices, summed(): return (block, delta, lax.ppermute(delta, flat, pairs))  10.3 us
    unnamed x50, local copies, waits for them, and re-layouts  9.49 us
    ppermute x1, starting transfers between devices, local(): peer_keep = lax.ppermute(keep, 'seq', swap)  9.39 us
  transfers between devices with their start and end apart: 30, of which 11 were waited for; matrix products, arithmetic and copies ran while one was open for 7% of the time, Pallas kernels for 18%

profile of v2, /device:TPU:9, one launch (start us, length us, event | category | flops | bytes accessed | tf_op | source)
XLA Modules:
  0.0 180.2 jit_solution(3958006864123518205)
XLA Ops:
  1.4 3.2 %collective-permute-start.4 = (bf16[768,640]{1,0:T(8,128)(2,1)S(1)}, bf16[768,640]{1,0:T(8,128)(2,1)}, u32[]{:S(2)}, u32[]{:S(2)}) collective-permute-start(bf16[768,640]{1,0:T(8,128)(2,1)S(1)} %dynamic_slice.3), channel_id=1, source_target_pairs={{0,4},{4,8},{8,12},{1,5},{5,9},{9,13},{2,6},{6,10},{10,14},{3,7},{... | collective-permute-start | bytes 2949128 | tf_op jit(solution)/shard_map/ppermute | solution.py:310
  4.6 3.0 %collective-permute-start.5 = (bf16[768,640]{1,0:T(8,128)(2,1)S(1)}, bf16[768,640]{1,0:T(8,128)(2,1)}, u32[]{:S(2)}, u32[]{:S(2)}) collective-permute-start(bf16[768,640]{1,0:T(8,128)(2,1)S(1)} %dynamic_slice.3), channel_id=1, source_target_pairs={{12,8},{8,4},{4,0},{13,9},{9,5},{5,1},{14,10},{10,6},{6,2},{15,11}... | collective-permute-start | bytes 2949128 | tf_op jit(solution)/shard_map/ppermute | solution.py:310
  8.0 1.7 copy-done.6
  9.6 1.7 copy-done.7
  11.3 3.8 %rotate.1 = (bf16[2,128,1536]{2,1,0:T(8,128)(2,1)}, bf16[2,2,128,1536]{3,2,1,0:T(8,128)(2,1)S(1)}, bf16[2,128,1536]{2,1,0:T(8,128)(2,1)}, bf16[2,128,1536]{2,1,0:T(8,128)(2,1)S(1)}, bf16[2,2,128,1536]{3,2,1,0:T(8,128)(2,1)S(1)}) custom-call(s32[3]{0:T(128)S(1)} %pad_add_fusion.core_ref.where_ref, f32[4,128]{1,0:T(4,128)S(1)} %get-tuple-element.67.cos_ref, ...), custom_call_target="tpu_custom_call" | custom-call | flops 1000 | bytes 1000 | tf_op jit(solution)/shard_map/rotate/pallas_call | solution.py:76
  18.4 1.9 %collective-permute-start.1 = (bf16[2,128,1536]{2,1,0:T(8,128)(2,1)}, bf16[2,128,1536]{2,1,0:T(8,128)(2,1)}, u32[]{:S(2)}, u32[]{:S(2)}) collective-permute-start(bf16[2,128,1536]{2,1,0:T(8,128)(2,1)} %get-tuple-element.28), channel_id=1, source_target_pairs={{4,1},{5,0},{8,5},{9,4},{12,9},{13,8},{6,3},{7,2},{10,7},{11,6},{1... | collective-permute-start | bytes 2359304 | tf_op jit(solution)/shard_map/ppermute | solution.py:333
  20.4 5.5 %collective-permute-done.4 = bf16[768,640]{1,0:T(8,128)(2,1)} collective-permute-done((bf16[768,640]{1,0:T(8,128)(2,1)S(1)}, bf16[768,640]{1,0:T(8,128)(2,1)}, u32[]{:S(2)}, u32[]{:S(2)}) %collective-permute-start.4) | collective-permute-done | bytes 983072 | tf_op jit(solution)/shard_map/ppermute | solution.py:310
  26.0 1.8 collective-permute-start.3
  31.5 4.3 %collective-permute-start.7 = (bf16[768,640]{1,0:T(8,128)(2,1)}, bf16[768,640]{1,0:T(8,128)(2,1)}, u32[]{:S(2)}, u32[]{:S(2)}) collective-permute-start(bf16[768,640]{1,0:T(8,128)(2,1)} %collective-permute-done.4), channel_id=1, source_target_pairs={{4,8},{8,12},{5,9},{9,13},{6,10},{10,14},{7,11},{11,15},{20,24},{2... | collective-permute-start | bytes 2949128 | tf_op jit(solution)/shard_map/ppermute | solution.py:310
  35.8 11.4 %collective-permute-done.1.far_q = bf16[2,128,1536]{2,1,0:T(8,128)(2,1)} collective-permute-done((bf16[2,128,1536]{2,1,0:T(8,128)(2,1)}, bf16[2,128,1536]{2,1,0:T(8,128)(2,1)}, u32[]{:S(2)}, u32[]{:S(2)}) %collective-permute-start.1) | collective-permute-done | bytes 786464 | tf_op jit(solution)/shard_map/ppermute | solution.py:333
  47.2 3.0 %collective-permute-start.8 = (bf16[768,640]{1,0:T(8,128)(2,1)}, bf16[768,640]{1,0:T(8,128)(2,1)}, u32[]{:S(2)}, u32[]{:S(2)}) collective-permute-start(bf16[768,640]{1,0:T(8,128)(2,1)} %collective-permute-done.5), channel_id=1, source_target_pairs={{8,4},{4,0},{9,5},{5,1},{10,6},{6,2},{11,7},{7,3},{24,20},{20,16},... | collective-permute-start | bytes 2949128 | tf_op jit(solution)/shard_map/ppermute | solution.py:310
  51.1 1.9 %collective-permute-start.17 = (s32[1]{0:T(128)}, s32[1]{0:T(128)}, u32[]{:S(2)}, u32[]{:S(2)}) collective-permute-start(s32[1]{0:T(128)} %param.12), channel_id=1, source_target_pairs={{4,0},{8,4},{12,8},{5,1},{9,5},{13,9},{6,2},{10,6},{14,10},{7,3},{... | collective-permute-start | bytes 20 | tf_op jit(solution)/shard_map/ppermute | solution.py:295
  54.3 18.9 %collective-permute-done.8 = bf16[768,640]{1,0:T(8,128)(2,1)} collective-permute-done((bf16[768,640]{1,0:T(8,128)(2,1)}, bf16[768,640]{1,0:T(8,128)(2,1)}, u32[]{:S(2)}, u32[]{:S(2)}) %collective-permute-start.8) | collective-permute-done | bytes 983072 | tf_op jit(solution)/shard_map/ppermute | solution.py:310
  79.4 3.1 %collective-permute-start.12 = (bf16[768,640]{1,0:T(8,128)(2,1)}, bf16[768,640]{1,0:T(8,128)(2,1)S(1)}, u32[]{:S(2)}, u32[]{:S(2)}) collective-permute-start(bf16[768,640]{1,0:T(8,128)(2,1)} %collective-permute-done.8), channel_id=1, source_target_pairs={{4,0},{5,1},{6,2},{7,3},{20,16},{21,17},{22,18},{23,19}} | collective-permute-start | bytes 2949128 | tf_op jit(solution)/shard_map/ppermute | solution.py:310
  83.4 6.5 %collective-permute-done.9.far_kv_1 = bf16[2,2,128,1536]{3,2,1,0:T(8,128)(2,1)S(1)} collective-permute-done((bf16[2,2,128,1536]{3,2,1,0:T(8,128)(2,1)}, bf16[2,2,128,1536]{3,2,1,0:T(8,128)(2,1)S(1)}, u32[]{:S(2)}, u32[]{:S(2)}) %collective-permute-start.9) | collective-permute-done | bytes 1572896 | tf_op jit(solution)/shard_map/ppermute | solution.py:339
  89.9 12.9 %attend.1 = (bf16[128,1536]{1,0:T(8,128)(2,1)S(1)}, bf16[3,128,1536]{2,1,0:T(8,128)(2,1)S(1)}) custom-call(s32[3]{0:T(128)S(1)} %pad_add_fusion.core_ref.where_ref, bf16[2,128,1536]{2,1,0:T(8,128)(2,1)} %collective-permute-done.peer_q, bf16[2,128,1536]{2,1,0:T(8,128)(2,1)} %collective-permute-done.1.far_q, bf16[2,128,1536]{2,1,0:T(8,128)(2,1)S(1)} %copy-done.13, ...), custom_call_target="tpu_custom_call" | custom-call | flops 1000 | bytes 1000 | tf_op jit(solution)/shard_map/attend/pallas_call | solution.py:160
  104.1 1.5 select_select_fusion.refs_0_
  105.6 9.4 %collective-permute-start.15 = (bf16[3,128,1536]{2,1,0:T(8,128)(2,1)S(1)}, bf16[3,128,1536]{2,1,0:T(8,128)(2,1)S(1)}, u32[]{:S(2)}, u32[]{:S(2)}) collective-permute-start(bf16[3,128,1536]{2,1,0:T(8,128)(2,1)S(1)} %get-tuple-element.36), channel_id=1, source_target_pairs={{0,1},{1,0},{2,3},{3,2},{4,5},{5,4},{6,7},{7,6},{8,9},{9,8},{10,11... | collective-permute-start | bytes 3538952 | tf_op jit(solution)/shard_map/ppermute | solution.py:350
  115.0 2.0 %collective-permute-start.11 = (bf16[128,1536]{1,0:T(8,128)(2,1)S(1)}, bf16[128,1536]{1,0:T(8,128)(2,1)S(1)}, u32[]{:S(2)}, u32[]{:S(2)}) collective-permute-start(bf16[128,1536]{1,0:T(8,128)(2,1)S(1)} %get-tuple-element.34), channel_id=1, source_target_pairs={{5,1},{9,5},{13,9},{7,3},{11,7},{15,11},{21,17},{25,21},{29,25},{2... | collective-permute-start | bytes 1179656 | tf_op jit(solution)/shard_map/ppermute | solution.py:343
  118.5 5.3 %collective-permute-done.11 = bf16[128,1536]{1,0:T(8,128)(2,1)S(1)} collective-permute-done((bf16[128,1536]{1,0:T(8,128)(2,1)S(1)}, bf16[128,1536]{1,0:T(8,128)(2,1)S(1)}, u32[]{:S(2)}, u32[]{:S(2)}) %collective-permute-start.11) | collective-permute-done | bytes 393248 | tf_op jit(solution)/shard_map/ppermute | solution.py:343
  124.1 1.6 collective-permute-done.16
  126.1 4.0 %project.5 = bf16[512,640]{1,0:T(8,128)(2,1)} custom-call(s32[3]{0:T(128)S(1)} %get-tuple-element.66.place_ref, bf16[1024,1536]{1,0:T(8,128)(2,1)S(1)} %fusion.12.mix_ref, f32[3,5120]{1,0:T(4,128)S(1)} %pad_maximum_fusion.1.gate_ref, bf16[1536,1280]{1,0:T(8,128)(2,1)S(1)} %copy-done.1), custom_call_target="tpu_custom_call" | custom-call | flops 1000 | bytes 1000 | tf_op jit(solution)/shard_map/project/pallas_call | solution.py:226
  131.5 4.0 %project.7 = bf16[512,640]{1,0:T(8,128)(2,1)} custom-call(s32[3]{0:T(128)S(1)} %get-tuple-element.64.place_ref, bf16[1024,1536]{1,0:T(8,128)(2,1)S(1)} %fusion.12.mix_ref, f32[3,5120]{1,0:T(4,128)S(1)} %pad_maximum_fusion.1.gate_ref, bf16[768,640]{1,0:T(8,128)(2,1)S(1)} %broadcast_select_fusion.1.refs_0_, bf16[768,640]{1,0:T(8,128)(2,1)S(1)} %collective-permute-done.23.refs_1_), custom_call_target="tpu_custom_call" | custom-call | flops 1000 | bytes 1000 | tf_op jit(solution)/shard_map/project/pallas_call | solution.py:226
  135.5 4.7 %collective-permute-done.20.refs_1_ = bf16[768,384]{1,0:T(8,128)(2,1)S(1)} collective-permute-done((bf16[768,384]{1,0:T(8,128)(2,1)S(1)}, bf16[768,384]{1,0:T(8,128)(2,1)S(1)}, u32[]{:S(2)}, u32[]{:S(2)}) %collective-permute-start.20) | collective-permute-done | bytes 589856 | tf_op jit(solution)/shard_map/ppermute | solution.py:319
  140.1 2.2 %collective-permute-start.24 = (bf16[512,640]{1,0:T(8,128)(2,1)}, bf16[512,640]{1,0:T(8,128)(2,1)}, u32[]{:S(2)}, u32[]{:S(2)}) collective-permute-start(bf16[512,640]{1,0:T(8,128)(2,1)} %project.7), channel_id=1, source_target_pairs={{0,2},{4,6},{10,8},{14,12},{1,3},{5,7},{11,9},{15,13},{16,18},{20,... | collective-permute-start | bytes 1966088 | tf_op jit(solution)/shard_map/ppermute | solution.py:389
  142.4 4.7 %project.6 = bf16[512,640]{1,0:T(8,128)(2,1)} custom-call(s32[3]{0:T(128)S(1)} %get-tuple-element.65.place_ref, bf16[1024,1536]{1,0:T(8,128)(2,1)S(1)} %fusion.12.mix_ref, f32[3,5120]{1,0:T(4,128)S(1)} %pad_maximum_fusion.1.gate_ref, bf16[768,640]{1,0:T(8,128)(2,1)S(1)} %copy-done.3, bf16[768,640]{1,0:T(8,128)(2,1)} %collective-permute-done.6.refs_1_), custom_call_target="tpu_custom_call" | custom-call | flops 1000 | bytes 1000 | tf_op jit(solution)/shard_map/project/pallas_call | solution.py:226
  147.0 2.1 %collective-permute-start.21 = (bf16[512,640]{1,0:T(8,128)(2,1)}, bf16[512,640]{1,0:T(8,128)(2,1)}, u32[]{:S(2)}, u32[]{:S(2)}) collective-permute-start(bf16[512,640]{1,0:T(8,128)(2,1)} %project.6), channel_id=1, source_target_pairs={{2,0},{4,6},{10,8},{12,14},{3,1},{5,7},{11,9},{13,15},{18,16},{20,... | collective-permute-start | bytes 1966088 | tf_op jit(solution)/shard_map/ppermute | solution.py:389
  149.1 2.1 %collective-permute-start.14 = (bf16[2,128,2560]{2,1,0:T(8,128)(2,1)}, bf16[2,128,2560]{2,1,0:T(8,128)(2,1)}, u32[]{:S(2)}, u32[]{:S(2)}) collective-permute-start(bf16[2,128,2560]{2,1,0:T(8,128)(2,1)} %param.9), channel_id=1, source_target_pairs={{1,0},{4,1},{5,4},{8,5},{9,8},{12,9},{13,12},{3,2},{6,3},{7,6},{10... | collective-permute-start | bytes 3932168 | tf_op jit(solution)/shard_map/ppermute | solution.py:357
  153.3 1.5 project.9
  156.1 2.3 %project.8 = bf16[512,384]{1,0:T(8,128)(2,1)S(1)} custom-call(s32[3]{0:T(128)S(1)} %get-tuple-element.63.place_ref, bf16[1024,1536]{1,0:T(8,128)(2,1)S(1)} %fusion.12.mix_ref, f32[3,5120]{1,0:T(4,128)S(1)} %pad_maximum_fusion.1.gate_ref, bf16[768,384]{1,0:T(8,128)(2,1)S(1)} %copy-done.5, bf16[768,384]{1,0:T(8,128)(2,1)S(1)} %copy-done.15), custom_call_target="tpu_custom_call" | custom-call | flops 1000 | bytes 1000 | tf_op jit(solution)/shard_map/project/pallas_call | solution.py:226
  159.8 10.3 %collective-permute-done.21 = bf16[512,640]{1,0:T(8,128)(2,1)} collective-permute-done((bf16[512,640]{1,0:T(8,128)(2,1)}, bf16[512,640]{1,0:T(8,128)(2,1)}, u32[]{:S(2)}, u32[]{:S(2)}) %collective-permute-start.21) | collective-permute-done | bytes 655392 | tf_op jit(solution)/shard_map/ppermute | solution.py:389
  170.1 2.9 %add_convert_fusion.1 = (bf16[512,640]{1,0:T(8,128)(2,1)S(1)}, bf16[512,640]{1,0:T(8,128)(2,1)S(1)}) fusion(bf16[512,640]{1,0:T(8,128)(2,1)} %collective-permute-done.19, bf16[512,640]{1,0:T(8,128)(2,1)} %project.5, bf16[512,640]{1,0:T(8,128)(2,1)} %collective-permute-done.21, bf16[512,640]{1,0:T(8,128)(2,1)} %project.6, ...), kind=kLoop, calls=%fused_computation.2 | loop fusion | flops 6881280 | bytes 5242886 | tf_op jit(solution)/shard_map/convert.2
  (120 shorter events, 33.7 us)
Async XLA Ops:
  0.0 75.2 %copy-start = (bf16[50,2560]{1,0:T(8,128)(2,1)S(1)}, bf16[50,2560]{1,0:T(8,128)(2,1)}, u32[]{:S(2)}) copy-start(bf16[50,2560]{1,0:T(8,128)(2,1)} %param.13) | copy-start | bytes 768004
  1.4 24.6 %collective-permute-start.4 = (bf16[768,640]{1,0:T(8,128)(2,1)S(1)}, bf16[768,640]{1,0:T(8,128)(2,1)}, u32[]{:S(2)}, u32[]{:S(2)}) collective-permute-start(bf16[768,640]{1,0:T(8,128)(2,1)S(1)} %dynamic_slice.3), channel_id=1, source_target_pairs={{0,4},{4,8},{8,12},{1,5},{5,9},{9,13},{2,6},{6,10},{10,14},{3,7},{... | collective-permute-start | bytes 2949128 | tf_op jit(solution)/shard_map/ppermute | solution.py:310
  4.6 24.3 %collective-permute-start.5 = (bf16[768,640]{1,0:T(8,128)(2,1)S(1)}, bf16[768,640]{1,0:T(8,128)(2,1)}, u32[]{:S(2)}, u32[]{:S(2)}) collective-permute-start(bf16[768,640]{1,0:T(8,128)(2,1)S(1)} %dynamic_slice.3), channel_id=1, source_target_pairs={{12,8},{8,4},{4,0},{13,9},{9,5},{5,1},{14,10},{10,6},{6,2},{15,11}... | collective-permute-start | bytes 2949128 | tf_op jit(solution)/shard_map/ppermute | solution.py:310
  17.2 14.3 %collective-permute-start = (bf16[2,128,1536]{2,1,0:T(8,128)(2,1)}, bf16[2,128,1536]{2,1,0:T(8,128)(2,1)}, u32[]{:S(2)}, u32[]{:S(2)}) collective-permute-start(bf16[2,128,1536]{2,1,0:T(8,128)(2,1)} %get-tuple-element.27), channel_id=1, source_target_pairs={{0,1},{1,0},{2,3},{3,2},{4,5},{5,4},{6,7},{7,6},{8,9},{9,8},{10,11... | collective-permute-start | bytes 2359304 | tf_op jit(solution)/shard_map/ppermute | solution.py:331
  18.4 28.8 %collective-permute-start.1 = (bf16[2,128,1536]{2,1,0:T(8,128)(2,1)}, bf16[2,128,1536]{2,1,0:T(8,128)(2,1)}, u32[]{:S(2)}, u32[]{:S(2)}) collective-permute-start(bf16[2,128,1536]{2,1,0:T(8,128)(2,1)} %get-tuple-element.28), channel_id=1, source_target_pairs={{4,1},{5,0},{8,5},{9,4},{12,9},{13,8},{6,3},{7,2},{10,7},{11,6},{1... | collective-permute-start | bytes 2359304 | tf_op jit(solution)/shard_map/ppermute | solution.py:333
  20.4 30.7 %collective-permute-start.2 = (bf16[2,2,128,1536]{3,2,1,0:T(8,128)(2,1)S(1)}, bf16[2,2,128,1536]{3,2,1,0:T(8,128)(2,1)}, u32[]{:S(2)}, u32[]{:S(2)}) collective-permute-start(bf16[2,2,128,1536]{3,2,1,0:T(8,128)(2,1)S(1)} %get-tuple-element.30.own_kv), channel_id=1, source_target_pairs={{0,1},{1,0},{2,3},{3,2},{4,5},{5,4},{6,7},{7,6},{8,9},{9,8},{10,11... | collective-permute-start | bytes 4718600 | tf_op jit(solution)/shard_map/ppermute | solution.py:332
  26.0 27.0 %collective-permute-start.3 = (bf16[2,2,128,1536]{3,2,1,0:T(8,128)(2,1)S(1)}, bf16[2,2,128,1536]{3,2,1,0:T(8,128)(2,1)}, u32[]{:S(2)}, u32[]{:S(2)}) collective-permute-start(bf16[2,2,128,1536]{3,2,1,0:T(8,128)(2,1)S(1)} %get-tuple-element.30.own_kv), channel_id=1, source_target_pairs={{4,0},{8,4},{12,8},{6,2},{10,6},{14,10},{20,16},{24,20},{28,24},{2... | collective-permute-start | bytes 4718600 | tf_op jit(solution)/shard_map/ppermute | solution.py:336
  30.2 47.9 %copy-start.2 = (bf16[768,640]{1,0:T(8,128)(2,1)}, bf16[768,640]{1,0:T(8,128)(2,1)S(1)}, u32[]{:S(2)}) copy-start(bf16[768,640]{1,0:T(8,128)(2,1)S(1)} %broadcast_select_fusion.2.refs_0_) | copy-start | bytes 2949124
  30.2 24.1 %collective-permute-start.6 = (bf16[768,640]{1,0:T(8,128)(2,1)S(1)}, bf16[768,640]{1,0:T(8,128)(2,1)}, u32[]{:S(2)}, u32[]{:S(2)}) collective-permute-start(bf16[768,640]{1,0:T(8,128)(2,1)S(1)} %broadcast_select_fusion.2.refs_0_), channel_id=1, source_target_pairs={{0,16},{16,0},{1,17},{17,1},{2,18},{18,2},{3,19},{19,3},{4,20},{20... | collective-permute-start | bytes 2949128 | tf_op jit(solution)/shard_map/ppermute | solution.py:319
  31.5 22.8 %collective-permute-start.7 = (bf16[768,640]{1,0:T(8,128)(2,1)}, bf16[768,640]{1,0:T(8,128)(2,1)}, u32[]{:S(2)}, u32[]{:S(2)}) collective-permute-start(bf16[768,640]{1,0:T(8,128)(2,1)} %collective-permute-done.4), channel_id=1, source_target_pairs={{4,8},{8,12},{5,9},{9,13},{6,10},{10,14},{7,11},{11,15},{20,24},{2... | collective-permute-start | bytes 2949128 | tf_op jit(solution)/shard_map/ppermute | solution.py:310
  47.2 26.0 %collective-permute-start.8 = (bf16[768,640]{1,0:T(8,128)(2,1)}, bf16[768,640]{1,0:T(8,128)(2,1)}, u32[]{:S(2)}, u32[]{:S(2)}) collective-permute-start(bf16[768,640]{1,0:T(8,128)(2,1)} %collective-permute-done.5), channel_id=1, source_target_pairs={{8,4},{4,0},{9,5},{5,1},{10,6},{6,2},{11,7},{7,3},{24,20},{20,16},... | collective-permute-start | bytes 2949128 | tf_op jit(solution)/shard_map/ppermute | solution.py:310
  51.1 23.4 %collective-permute-start.17 = (s32[1]{0:T(128)}, s32[1]{0:T(128)}, u32[]{:S(2)}, u32[]{:S(2)}) collective-permute-start(s32[1]{0:T(128)} %param.12), channel_id=1, source_target_pairs={{4,0},{8,4},{12,8},{5,1},{9,5},{13,9},{6,2},{10,6},{14,10},{7,3},{... | collective-permute-start | bytes 20 | tf_op jit(solution)/shard_map/ppermute | solution.py:295
  53.0 30.3 %collective-permute-start.10 = (bf16[2,128,1536]{2,1,0:T(8,128)(2,1)}, bf16[2,128,1536]{2,1,0:T(8,128)(2,1)S(1)}, u32[]{:S(2)}, u32[]{:S(2)}) collective-permute-start(bf16[2,128,1536]{2,1,0:T(8,128)(2,1)} %collective-permute-done.1.far_q), channel_id=1, source_target_pairs={{0,1},{2,3},{4,5},{6,7},{8,9},{10,11},{12,13},{14,15},{16,17},{18,... | collective-permute-start | bytes 2359304 | tf_op jit(solution)/shard_map/ppermute | solution.py:337
  73.2 16.7 %collective-permute-start.9 = (bf16[2,2,128,1536]{3,2,1,0:T(8,128)(2,1)}, bf16[2,2,128,1536]{3,2,1,0:T(8,128)(2,1)S(1)}, u32[]{:S(2)}, u32[]{:S(2)}) collective-permute-start(bf16[2,2,128,1536]{3,2,1,0:T(8,128)(2,1)} %collective-permute-done.3.far_kv), channel_id=1, source_target_pairs={{0,1},{2,3},{4,5},{6,7},{8,9},{10,11},{12,13},{14,15},{16,17},{18,... | collective-permute-start | bytes 4718600 | tf_op jit(solution)/shard_map/ppermute | solution.py:339
  75.5 7.0 %collective-permute-start.18 = (bf16[2,2560]{1,0:T(2,128)(2,1)S(1)}, bf16[2,2560]{1,0:T(2,128)(2,1)S(1)}, u32[]{:S(2)}, u32[]{:S(2)}) collective-permute-start(bf16[2,2560]{1,0:T(2,128)(2,1)S(1)} %convolution_convert_fusion), channel_id=1, source_target_pairs={{0,2},{2,0},{1,3},{3,1},{4,6},{6,4},{5,7},{7,5},{8,10},{10,8},{9,1... | collective-permute-start | bytes 30728 | tf_op jit(solution)/shard_map/ppermute | solution.py:365
  78.1 53.4 %collective-permute-start.23 = (bf16[768,640]{1,0:T(8,128)(2,1)S(1)}, bf16[768,640]{1,0:T(8,128)(2,1)S(1)}, u32[]{:S(2)}, u32[]{:S(2)}) collective-permute-start(bf16[768,640]{1,0:T(8,128)(2,1)S(1)} %broadcast_select_fusion.1.refs_0_), channel_id=1, source_target_pairs={{0,16},{16,0},{1,17},{17,1},{2,18},{18,2},{3,19},{19,3},{4,20},{20... | collective-permute-start | bytes 2949128 | tf_op jit(solution)/shard_map/ppermute | solution.py:319
  79.4 23.4 %collective-permute-start.12 = (bf16[768,640]{1,0:T(8,128)(2,1)}, bf16[768,640]{1,0:T(8,128)(2,1)S(1)}, u32[]{:S(2)}, u32[]{:S(2)}) collective-permute-start(bf16[768,640]{1,0:T(8,128)(2,1)} %collective-permute-done.8), channel_id=1, source_target_pairs={{4,0},{5,1},{6,2},{7,3},{20,16},{21,17},{22,18},{23,19}} | collective-permute-start | bytes 2949128 | tf_op jit(solution)/shard_map/ppermute | solution.py:310
  82.5 20.3 %collective-permute-start.13 = (bf16[768,640]{1,0:T(8,128)(2,1)}, bf16[768,640]{1,0:T(8,128)(2,1)S(1)}, u32[]{:S(2)}, u32[]{:S(2)}) collective-permute-start(bf16[768,640]{1,0:T(8,128)(2,1)} %collective-permute-done.7), channel_id=1, source_target_pairs={{8,12},{9,13},{10,14},{11,15},{24,28},{25,29},{26,30},{27,31}} | collective-permute-start | bytes 2949128 | tf_op jit(solution)/shard_map/ppermute | solution.py:310
  105.6 18.5 %collective-permute-start.15 = (bf16[3,128,1536]{2,1,0:T(8,128)(2,1)S(1)}, bf16[3,128,1536]{2,1,0:T(8,128)(2,1)S(1)}, u32[]{:S(2)}, u32[]{:S(2)}) collective-permute-start(bf16[3,128,1536]{2,1,0:T(8,128)(2,1)S(1)} %get-tuple-element.36), channel_id=1, source_target_pairs={{0,1},{1,0},{2,3},{3,2},{4,5},{5,4},{6,7},{7,6},{8,9},{9,8},{10,11... | collective-permute-start | bytes 3538952 | tf_op jit(solution)/shard_map/ppermute | solution.py:350
  115.0 8.8 %collective-permute-start.11 = (bf16[128,1536]{1,0:T(8,128)(2,1)S(1)}, bf16[128,1536]{1,0:T(8,128)(2,1)S(1)}, u32[]{:S(2)}, u32[]{:S(2)}) collective-permute-start(bf16[128,1536]{1,0:T(8,128)(2,1)S(1)} %get-tuple-element.34), channel_id=1, source_target_pairs={{5,1},{9,5},{13,9},{7,3},{11,7},{15,11},{21,17},{25,21},{29,25},{2... | collective-permute-start | bytes 1179656 | tf_op jit(solution)/shard_map/ppermute | solution.py:343
  117.0 14.4 %collective-permute-start.22 = (bf16[768,256]{1,0:T(8,128)(2,1)S(1)}, bf16[768,256]{1,0:T(8,128)(2,1)S(1)}, u32[]{:S(2)}, u32[]{:S(2)}) collective-permute-start(bf16[768,256]{1,0:T(8,128)(2,1)S(1)} %select_select_fusion.1.refs_0_), channel_id=1, source_target_pairs={{0,16},{16,0},{1,17},{17,1},{2,18},{18,2},{3,19},{19,3},{4,20},{20... | collective-permute-start | bytes 1179656 | tf_op jit(solution)/shard_map/ppermute | solution.py:319
  117.1 23.1 %collective-permute-start.20 = (bf16[768,384]{1,0:T(8,128)(2,1)S(1)}, bf16[768,384]{1,0:T(8,128)(2,1)S(1)}, u32[]{:S(2)}, u32[]{:S(2)}) collective-permute-start(bf16[768,384]{1,0:T(8,128)(2,1)S(1)} %select_select_fusion.refs_0_), channel_id=1, source_target_pairs={{0,16},{16,0},{1,17},{17,1},{2,18},{18,2},{3,19},{19,3},{4,20},{20... | collective-permute-start | bytes 1769480 | tf_op jit(solution)/shard_map/ppermute | solution.py:319
  123.9 1.8 collective-permute-start.16
  130.1 21.2 %collective-permute-start.19 = (bf16[512,640]{1,0:T(8,128)(2,1)}, bf16[512,640]{1,0:T(8,128)(2,1)}, u32[]{:S(2)}, u32[]{:S(2)}) collective-permute-start(bf16[512,640]{1,0:T(8,128)(2,1)} %project.5), channel_id=1, source_target_pairs={{2,0},{6,4},{8,10},{12,14},{3,1},{7,5},{9,11},{13,15},{18,16},{22,... | collective-permute-start | bytes 1966088 | tf_op jit(solution)/shard_map/ppermute | solution.py:389
  140.1 19.7 %collective-permute-start.24 = (bf16[512,640]{1,0:T(8,128)(2,1)}, bf16[512,640]{1,0:T(8,128)(2,1)}, u32[]{:S(2)}, u32[]{:S(2)}) collective-permute-start(bf16[512,640]{1,0:T(8,128)(2,1)} %project.7), channel_id=1, source_target_pairs={{0,2},{4,6},{10,8},{14,12},{1,3},{5,7},{11,9},{15,13},{16,18},{20,... | collective-permute-start | bytes 1966088 | tf_op jit(solution)/shard_map/ppermute | solution.py:389
  147.0 23.1 %collective-permute-start.21 = (bf16[512,640]{1,0:T(8,128)(2,1)}, bf16[512,640]{1,0:T(8,128)(2,1)}, u32[]{:S(2)}, u32[]{:S(2)}) collective-permute-start(bf16[512,640]{1,0:T(8,128)(2,1)} %project.6), channel_id=1, source_target_pairs={{2,0},{4,6},{10,8},{12,14},{3,1},{5,7},{11,9},{13,15},{18,16},{20,... | collective-permute-start | bytes 1966088 | tf_op jit(solution)/shard_map/ppermute | solution.py:389
  149.1 24.7 %collective-permute-start.14 = (bf16[2,128,2560]{2,1,0:T(8,128)(2,1)}, bf16[2,128,2560]{2,1,0:T(8,128)(2,1)}, u32[]{:S(2)}, u32[]{:S(2)}) collective-permute-start(bf16[2,128,2560]{2,1,0:T(8,128)(2,1)} %param.9), channel_id=1, source_target_pairs={{1,0},{4,1},{5,4},{8,5},{9,8},{12,9},{13,12},{3,2},{6,3},{7,6},{10... | collective-permute-start | bytes 3932168 | tf_op jit(solution)/shard_map/ppermute | solution.py:357
  154.8 21.9 %collective-permute-start.28 = (bf16[512,256]{1,0:T(8,128)(2,1)S(1)}, bf16[512,256]{1,0:T(8,128)(2,1)S(1)}, u32[]{:S(2)}, u32[]{:S(2)}) collective-permute-start(bf16[512,256]{1,0:T(8,128)(2,1)S(1)} %project.9), channel_id=1, source_target_pairs={{0,2},{6,4},{8,10},{14,12},{1,3},{7,5},{9,11},{15,13},{16,18},{22,... | collective-permute-start | bytes 786440 | tf_op jit(solution)/shard_map/ppermute | solution.py:389
  158.5 17.3 %collective-permute-start.26 = (bf16[512,384]{1,0:T(8,128)(2,1)S(1)}, bf16[512,384]{1,0:T(8,128)(2,1)S(1)}, u32[]{:S(2)}, u32[]{:S(2)}) collective-permute-start(bf16[512,384]{1,0:T(8,128)(2,1)S(1)} %project.8), channel_id=1, source_target_pairs={{0,2},{6,4},{8,10},{14,12},{1,3},{7,5},{9,11},{15,13},{16,18},{22,... | collective-permute-start | bytes 1179656 | tf_op jit(solution)/shard_map/ppermute | solution.py:389
  173.1 4.7 %collective-permute-start.25 = (bf16[256,1280]{1,0:T(8,128)(2,1)S(1)}, bf16[256,1280]{1,0:T(8,128)(2,1)S(1)}, u32[]{:S(2)}, u32[]{:S(2)}) collective-permute-start(bf16[256,1280]{1,0:T(8,128)(2,1)S(1)} %pad_maximum_fusion), channel_id=1, source_target_pairs={{0,1},{1,0},{2,3},{3,2},{4,5},{5,4},{6,7},{7,6},{8,9},{9,8},{10,11... | collective-permute-start | bytes 1966088 | tf_op jit(solution)/shard_map/ppermute | solution.py:419
  176.0 1.8 %collective-permute-start.27 = (bf16[256,384]{1,0:T(8,128)(2,1)S(1)}, bf16[256,384]{1,0:T(8,128)(2,1)S(1)}, u32[]{:S(2)}, u32[]{:S(2)}) collective-permute-start(bf16[256,384]{1,0:T(8,128)(2,1)S(1)} %slice.171), channel_id=1, source_target_pairs={{0,1},{1,0},{2,3},{3,2},{4,5},{5,4},{6,7},{7,6},{8,9},{9,8},{10,11... | collective-permute-start | bytes 589832 | tf_op jit(solution)/shard_map/ppermute | solution.py:423
  176.8 1.4 collective-permute-start.29
  (20 other events, 114.9 us)

commit v3 on v2

v3 whole, which is shorter than its diff:
```python
import functools
import math

import jax
import jax.numpy as jnp
from jax import lax
from jax.experimental import pallas as pl
from jax.experimental.pallas import tpu as pltpu
from jax.sharding import PartitionSpec as P

HD = 128
BF16 = jnp.bfloat16
F32 = jnp.float32
SPARE = 16
VMEM_LIMIT = 16 * 1024 * 1024


COST = pl.CostEstimate(flops=1000, bytes_accessed=1000, transcendentals=0)


def params(*semantics):
    return pltpu.CompilerParams(dimension_semantics=semantics or None, vmem_limit_bytes=VMEM_LIMIT)


def rotation_tables(times):
    half = HD // 2
    pair_index = jnp.arange(half, dtype=F32)
    frequency = jnp.power(F32(10000.0), -pair_index / half)
    angles = times.astype(F32)[:, None] * frequency[None, :]
    cosine, sine = jnp.cos(angles), jnp.sin(angles)
    return (
        jnp.concatenate([cosine, cosine], axis=1),
        jnp.concatenate([-sine, sine], axis=1),
    )


def rotate_kernel(core_ref, cos_ref, sin_ref, own_ref, new_ref, mine_ref, peer_ref, peer_v_ref, fresh_ref):
    _, frames, _, channels = own_ref.shape
    share = mine_ref.shape[-1]

    def turn(block, row):
        block = block.astype(F32)
        out = block * cos_ref[row : row + 1, :] + pltpu.roll(block, HD // 2, 1) * sin_ref[row : row + 1, :]
        return out.astype(BF16)

    for head in range(share // HD):
        to = slice(head * HD, (head + 1) * HD)
        for target, core in ((mine_ref, core_ref[0]), (peer_ref, 1 - core_ref[0])):
            start = core * share if share < channels else 0
            at = pl.ds(pl.multiple_of(start + head * HD, HD), HD)
            for frame in range(frames):
                target[0, frame, :, to] = turn(own_ref[0, frame, :, at], frame)
                target[1, frame, :, to] = turn(own_ref[1, frame, :, at], frame)
                if target is mine_ref:
                    target[2, frame, :, to] = own_ref[2, frame, :, at]
                else:
                    peer_v_ref[frame, :, to] = own_ref[2, frame, :, at]
        start = core_ref[0] * share if share < channels else 0
        at = pl.ds(pl.multiple_of(start + head * HD, HD), HD)
        for frame in range(frames):
            fresh_ref[0, frame, :, to] = turn(new_ref[frame, 0, :, at], frames + frame)
            fresh_ref[1, frame, :, to] = turn(new_ref[frame, 1, :, at], frames + frame)
            fresh_ref[2, frame, :, to] = new_ref[frame, 2, :, at]

def rotate_all(where, cos, sin, own, new):
    _, frames, tokens, channels = own.shape
    share = channels // 2 if channels % (2 * HD) == 0 else channels
    full = jax.ShapeDtypeStruct((3, frames, tokens, share), BF16)
    return pl.pallas_call(
        rotate_kernel,
        in_specs=[pl.BlockSpec(memory_space=pltpu.SMEM)] + [pl.BlockSpec(memory_space=pltpu.VMEM)] * 4,
        out_specs=[pl.BlockSpec(memory_space=pltpu.VMEM)] * 4,
        out_shape=[
            full,
            jax.ShapeDtypeStruct((2, frames, tokens, share), BF16),
            jax.ShapeDtypeStruct((frames, tokens, share), BF16),
            full,
        ],
        compiler_params=params(),
        cost_estimate=COST,
        name="rotate",
    )(where, cos, sin, own, new)


def bundle_kernel(where_ref, mine, got, got_v, out_ref):
    theirs = got.at[0], got.at[1], got_v
    tokens = mine.shape[2]
    second_core = where_ref[0] == 1
    for kind in range(3):
        for frame in range(2):
            at = (2 * kind + frame) * tokens
            out_ref[at : at + tokens, :] = jnp.where(second_core, theirs[kind][frame], mine[kind, frame])
    for kind in (1, 2):
        at = (5 + kind) * tokens
        out_ref[at : at + tokens, :] = jnp.where(second_core, mine[kind, 0], theirs[kind][0])
    level = jnp.full((SPARE, out_ref.shape[1]), where_ref[3].astype(F32))
    out_ref[8 * tokens :, :] = level.astype(BF16)


def bundle(where, mine, got, got_v):
    _, _, tokens, share = mine.shape
    return pl.pallas_call(
        bundle_kernel,
        in_specs=[pl.BlockSpec(memory_space=pltpu.SMEM)] + [pl.BlockSpec(memory_space=pltpu.VMEM)] * 3,
        out_specs=pl.BlockSpec(memory_space=pltpu.VMEM),
        out_shape=jax.ShapeDtypeStruct((8 * tokens + SPARE, share), BF16),
        compiler_params=params(),
        cost_estimate=COST,
        name="bundle",
    )(where, mine, got, got_v)


def attend_kernel(where_ref, mine, got, got_v, fresh, far_ref, send_ref, keep_ref):
    theirs = got.at[0], got.at[1], got_v
    tokens = mine.shape[2]
    heads = mine.shape[-1] // HD
    core, first, last = where_ref[0], where_ref[1] == 1, where_ref[2] == 1
    second_core = core == 1
    factor = math.log2(math.e) / math.sqrt(HD)

    def one(at):
        def frames_of(kind):
            own = [mine[kind, frame, :, at] for frame in range(2)]
            peer = [theirs[kind][frame, :, at] for frame in range(2)]
            rows = [jnp.where(second_core, p, o) for o, p in zip(own, peer)]
            rows += [jnp.where(second_core, o, p) for o, p in zip(own, peer)]
            for frame in range(2):
                far = far_ref[(2 * kind + frame) * tokens : (2 * kind + frame + 1) * tokens, at]
                rows.append(jnp.where(last, fresh[kind, frame, :, at], far))
            if kind:
                rows.append(far_ref[(5 + kind) * tokens : (6 + kind) * tokens, at])
            return rows

        queries, keys, values = frames_of(0), frames_of(1), frames_of(2)

        def mix(query, low):
            rows = lax.dot_general(
                jnp.concatenate(query, axis=0),
                jnp.concatenate(keys[low : low + 6], axis=0),
                (((1,), (1,)), ((), ())),
                preferred_element_type=F32,
            )
            part = [rows[:, i * tokens : (i + 1) * tokens] for i in range(6)]
            part[0] = jnp.where(first, -1e30, part[0])
            part[5] = jnp.where(last, -1e30, part[5])
            rows = jnp.concatenate(part, axis=1)
            top = jnp.max(rows, axis=1, keepdims=True)
            weights = jnp.exp2((rows - top) * factor)
            total = jnp.sum(weights, axis=1, keepdims=True)
            out = jnp.dot(
                weights.astype(BF16),
                jnp.concatenate(values[low : low + 6], axis=0),
                preferred_element_type=F32,
            )
            return (out * (1.0 / total)).astype(BF16)

        early = mix(queries[1:5], 0)
        send_ref[:, at] = early[:tokens]
        keep_ref[: 3 * tokens, at] = early[tokens:]
        keep_ref[3 * tokens :, at] = mix(queries[2:6], 1)

    group = 3 if heads % 3 == 0 else 1

    @pl.loop(0, heads // group)
    def _(step):
        for head in range(group):
            one(pl.ds(pl.multiple_of((step * group + head) * HD, HD), HD))


def attend(where, *operands):
    _, _, tokens, share = operands[0].shape
    return pl.pallas_call(
        attend_kernel,
        in_specs=[pl.BlockSpec(memory_space=pltpu.SMEM)] + [pl.BlockSpec(memory_space=pltpu.VMEM)] * len(operands),
        out_specs=[pl.BlockSpec(memory_space=pltpu.VMEM)] * 2,
        out_shape=[
            jax.ShapeDtypeStruct((tokens, share), BF16),
            jax.ShapeDtypeStruct((7 * tokens, share), BF16),
        ],
        compiler_params=params(),
        cost_estimate=COST,
        name="attend",
    )(where, *operands)


def project_kernel(half, place_ref, keep_ref, came_ref, peer_keep_ref, peer_came_ref, gate_ref, *refs):
    pieces, out_ref = refs[:-1], refs[-1]
    group, core, gate_at = place_ref[0], place_ref[1], place_ref[2]
    tokens, depth = came_ref.shape
    own = jnp.concatenate([keep_ref[...], came_ref[...]], axis=0)
    peer = jnp.concatenate([peer_keep_ref[...], peer_came_ref[...]], axis=0)
    if len(pieces) == 1:
        widths = [256] * (half // 256) + [half % 256] * (half % 256 > 0)
    else:
        widths = [piece.shape[1] for piece in pieces[::2]]
    low = 0
    for i, wide in enumerate(widths):
        if len(pieces) == 1:
            at = pl.ds(pl.multiple_of(core * half + low, HD), wide)
            near = pieces[0][pl.ds(pl.multiple_of(core * depth, HD), depth), at]
            far = pieces[0][pl.ds(pl.multiple_of((1 - core) * depth, HD), depth), at]
        else:
            here, there = pieces[2 * i][...], pieces[2 * i + 1][...]
            near = jnp.where(group == core, here, there)
            far = jnp.where(group == core, there, here)
        total = jnp.dot(own, near, preferred_element_type=F32)
        total = total + jnp.dot(peer, far, preferred_element_type=F32)
        at = pl.ds(pl.multiple_of(gate_at + low, HD), wide)
        row, crossing = gate_ref[0:1, at], gate_ref[1:2, at]
        order = (0, 1, 2, 7, 3, 4, 5, 6)
        parts = [total[n * tokens : (n + 1) * tokens] for n in order]
        for who in range(2):
            base = jnp.where(core == who, 0, 2 * tokens)
            for frame in range(2):
                n = 2 * who + frame
                gate = crossing if n == 3 else row
                result = (parts[n] * gate + parts[4 + n] * row).astype(BF16)
                out_ref[pl.ds(pl.multiple_of(base + frame * tokens, tokens), tokens), low : low + wide] = result
        low += wide


def project(group, core, half, gate_at, mix, pieces, gates):
    keep, came, peer_keep, peer_came = mix
    tokens, share = came.shape
    columns = half if len(pieces) == 1 else sum(piece.shape[1] for piece in pieces[::2])
    if 2 * share != pieces[0].shape[0] * (1 if len(pieces) == 1 else 2) or share % HD or half % HD:
        if len(pieces) == 1:
            weights = lax.dynamic_slice_in_dim(pieces[0], core * half, half, axis=1)
        else:
            weights = [
                jnp.where(group == 0, jnp.concatenate([own, other]), jnp.concatenate([other, own]))
                for own, other in zip(pieces[::2], pieces[1::2])
            ]
            weights = jnp.concatenate(weights, axis=1)
        rows = jnp.concatenate([keep, came], axis=0)
        if 2 * share == weights.shape[0]:
            peer = jnp.concatenate([peer_keep, peer_came], axis=0)
            rows = jnp.where(
                core == 0, jnp.concatenate([rows, peer], axis=1), jnp.concatenate([peer, rows], axis=1)
            )
        total = jnp.dot(rows, weights, preferred_element_type=F32).reshape(8, tokens, columns)
        gates = lax.dynamic_slice_in_dim(gates, gate_at, columns, axis=1)
        first = jnp.stack([total[0], total[1], total[2], total[7]])
        scale = jnp.stack([gates[0], gates[0], gates[0], gates[1]])[:, None, :]
        total = (first * scale + total[3:7] * gates[0]).reshape(2, 2 * tokens, columns)
        total = jnp.where(core == 0, total, total[::-1])
        return total.reshape(4 * tokens, columns).astype(BF16)

    place = jnp.stack([group, core, gate_at]).astype(jnp.int32)
    return pl.pallas_call(
        functools.partial(project_kernel, half),
        in_specs=[pl.BlockSpec(memory_space=pltpu.SMEM)]
        + [pl.BlockSpec(memory_space=pltpu.VMEM)] * (5 + len(pieces)),
        out_specs=pl.BlockSpec(memory_space=pltpu.VMEM),
        out_shape=jax.ShapeDtypeStruct((4 * tokens, columns), BF16),
        compiler_params=params(),
        cost_estimate=COST,
        name="project",
    )(place, *mix, gates, *pieces)


def arrivals(count):
    table = []
    for k in range(1, count):
        row = []
        for q in range(count):
            ahead, behind = count - 1 - q, q
            if q < count // 2:
                row.append(("down", k) if k <= ahead else ("up", k - ahead))
            else:
                row.append(("up", k) if k <= behind else ("down", k - behind))
        table.append(row)
    return table


def pick(place, row, held):
    value = None
    for source in sorted(set(row)):
        here = functools.reduce(jnp.logical_or, [place == q for q, r in enumerate(row) if r == source])
        value = held(source) if value is None else jnp.where(here, held(source), value)
    return value


def look_up(place, row):
    return sum(jnp.where(place == q, value, 0) for q, value in enumerate(row))


def after(value, *done):
    return lax.optimization_barrier((value, done))[0]


def local(
    latent,
    projections,
    frame_times,
    levels,
    gates,
    out_weight,
    incoming_latent,
    incoming_proj,
    incoming_times,
):
    place, count = lax.axis_index("queue"), lax.axis_size("queue")
    core, cores = lax.axis_index("seq"), lax.axis_size("seq")
    side, sides = lax.axis_index("heads"), lax.axis_size("heads")
    group, groups = lax.axis_index("groups"), lax.axis_size("groups")
    first, last = place == 0, place == count - 1
    frames, tokens, features = latent.shape
    channels = projections.shape[-1]
    assert cores == 2 and frames == 2 and groups == 2 and count % sides == 0
    columns = out_weight.shape[1]
    half = columns // 2
    swap = [(0, 1), (1, 0)]
    pair = ("queue", "seq")
    table = arrivals(count)
    block_of = [list(range(count))]
    for row in table:
        block_of.append([q + hops if way == "down" else q - hops for q, (way, hops) in enumerate(row)])

    depth = out_weight.shape[0] // 2
    cuts = [0, half]
    if half % HD == 0 and half > HD:
        cuts = [0, half - HD, half]
    chunks = list(zip(cuts[:-1], cuts[1:]))
    origin = lax.dynamic_slice(out_weight, (group * depth, core * half), (depth, half))
    whole = [(0, half)]
    held = {}

    def send_weights(name, block, low, hops, ends):
        for way, part, sign in (("up", block[0], 1), ("down", block[1], -1)):
            pairs = [(i, i + hops) for i in range(count - hops) if i >= ends]
            if sign < 0:
                pairs = [(count - 1 - i, count - 1 - j) for i, j in pairs]
            held[way, name, low] = lax.ppermute(part, "queue", pairs)

    gathered = {}

    def spread(k, low, high, *done):
        sources = {key: held[key + (0,)] for key in table[k - 1]}
        if done:
            sources = after(sources, *done)
        own = pick(place, table[k - 1], lambda key: sources[key][:, low:high])
        gathered[k, low] = (own, lax.ppermute(own, "groups", swap))
        return own

    send_weights(1, (origin, origin), 0, 1, 0)
    hop_1 = held["up", 1, 0], held["down", 1, 0]

    cos, sin = rotation_tables(jnp.concatenate([frame_times, incoming_times]))
    where = jnp.stack([core, first.astype(jnp.int32), last.astype(jnp.int32), levels[0]])
    mine, peer, peer_v, fresh = rotate_all(where, cos, sin, after(projections, origin), incoming_proj)
    got, got_v = lax.ppermute(peer, "seq", swap), lax.ppermute(peer_v, "seq", swap)
    back = [(i + 1, i) for i in range(count - 1)]
    far = lax.ppermute(after(bundle(where, mine, got, got_v), *hop_1), "queue", back)
    held["up", 1, 0], held["down", 1, 0] = hop_1
    spread(1, 0, half)
    if count > 2:
        send_weights(2, hop_1, 0, 1, 1)

    inputs = after((mine, got, got_v, fresh, far), gathered[1, 0][1])

    send, keep = attend(where, *inputs)
    came = lax.ppermute(send, "queue", back)
    next_level = after(far, came)[8 * tokens, :1].astype(jnp.int32)
    if count > 2:
        held["up", 2, 0], held["down", 2, 0] = after((held["up", 2, 0], held["down", 2, 0]), came)
    for hop in range(3, count):
        spread(hop - 1, 0, half)
        send_weights(hop, (held["up", hop - 1, 0], held["down", hop - 1, 0]), 0, 1, hop - 1)
    k = count - 1
    if keep.shape[1] < channels:
        peer_keep, peer_came = lax.ppermute(keep, "seq", swap), lax.ppermute(came, "seq", swap)
    else:
        peer_keep, peer_came = keep, came
    mix = keep, came, peer_keep, peer_came

    moved = lax.ppermute(after(latent, came), pair, [(i + 1, i) for i in range(2 * count - 1)])
    moved = jnp.where(jnp.logical_and(last, core == 1), incoming_latent, moved)
    moved = moved.reshape(frames * tokens, features)

    chosen = jnp.concatenate([levels, next_level])
    one_hot = (jnp.arange(gates.shape[0], dtype=jnp.int32)[None, :] == chosen[:, None]).astype(BF16)
    rows = jnp.dot(one_hot, gates, preferred_element_type=F32).astype(BF16)
    if sides == 2:
        other = lax.ppermute(rows, "heads", swap)
        rows = jnp.concatenate(
            [jnp.where(side == 0, rows, other), jnp.where(side == 0, other, rows)], axis=1
        )
    else:
        rows = lax.all_gather(rows, "heads", axis=1, tiled=True)
    rows = rows.astype(F32)
    crossing = jnp.where(last, 0.0, rows[1:2])
    gate_rows = jnp.concatenate([rows[:1], crossing], axis=0)

    per_side = count // sides
    flat = ("queue", "heads")

    def summed(k, pieces, low, *done):
        block = look_up(place, block_of[k])
        rows = after(mix, *done) if done else mix
        delta = project(group, core, half, block * columns + core * half + low, rows, pieces, gate_rows)
        if sides != 2:
            return block, delta, None
        pairs = [
            (q * 2 + 1 - block_of[k][q] // per_side, q * 2 + block_of[k][q] // per_side) for q in range(count)
        ]
        return block, delta, lax.ppermute(delta, flat, pairs)

    results, late, picked = [], [], []
    for n in range(k):
        pieces = [out_weight] if n == 0 else gathered[n, 0]
        if n == k - 1:
            for low, high in chunks:
                picked.append(spread(k, low, high, *picked, *[delta for _, delta, _ in results[-1:]]))
        results.append(summed(n, pieces, 0, *picked, *[delta for _, delta, _ in results[-1:]]))
    sums = [other for _, _, other in results if other is not None]
    for n, (low, _) in enumerate(chunks):
        done = [delta for _, delta, _ in results[-1:]] + [delta for _, (_, delta, _) in late]
        late.append((low, summed(k, gathered[k, low], low, *done, *(sums[2:] if n else sums[:2]))))
    if sides != 2:
        results += [result for _, result in late]
        change = jnp.zeros((2 * frames * tokens, count * half), BF16)
        for n, (block, delta, _) in enumerate(results):
            low = late[n - count + 1][0] if n >= count - 1 else 0
            change = lax.dynamic_update_slice_in_dim(change, delta, block * half + low, axis=1)
        early = lax.psum_scatter(change, "heads", scatter_dimension=1, tiled=True)
        late = []
    else:
        early = []
        for b in range(per_side):
            total = 0.0
            for block, delta, other in results:
                change = delta.astype(F32) + other.astype(F32)
                total = total + jnp.where(block == side * per_side + b, change, 0.0)
            early.append(total)
        early = jnp.concatenate(early, axis=1).astype(BF16)

    mine = frames * tokens
    early_back = lax.ppermute(early[mine:], "seq", swap)
    tail = []
    for low, (block, delta, other) in late:
        total = (delta.astype(F32) + other.astype(F32)).astype(BF16)
        tail.append((low, low + delta.shape[1], block, total[:mine], lax.ppermute(total[mine:], "seq", swap)))

    parts = []
    for b in range(per_side):
        for who in range(2):
            for low, high in chunks:
                at = b * half + low
                change = jnp.where(core == who, early[:mine, at : at + high - low], early_back[:, at : at + high - low])
                change = change.astype(F32)
                for start, _, block, own, back in tail:
                    if start == low:
                        last_part = jnp.where(core == who, own, back).astype(F32)
                        change = change + jnp.where(block == side * per_side + b, last_part, 0.0)
                at = b * columns + who * half + low
                parts.append((moved[:, at : at + high - low].astype(F32) + change).astype(BF16))
    return jnp.concatenate(parts, axis=1).reshape(frames, tokens, features)


def solution(mesh):
    return jax.shard_map(
        local,
        mesh=mesh,
        in_specs=(
            P(("groups", "queue", "seq"), None, "heads"),
            P(None, ("groups", "queue", "seq"), None, "heads"),
            P(("groups", "queue", "seq")),
            P(("groups", "queue")),
            P(None, "heads"),
            P("heads", "queue"),
            P("groups", None, "heads"),
            P("groups", None, None, "heads"),
            P("groups"),
        ),
        out_specs=P(("groups", "queue", "seq"), None, "heads"),
        check_vma=False,
    )
```

time: 182 us -> 169 us (0.929)
  waiting for transfers between devices: 66.5 us -> 53.1 us
  starting transfers between devices: 55.5 us -> 59.4 us
  Pallas kernels: 33.2 us -> 29.8 us
    ppermute x4, waiting for transfers between devices: 4.66 us -> 19.4 us  [spread(): gathered[k, low] = (own, lax.ppermute(own, 'groups', swap))]
    ppermute x6, waiting for transfers between devices: 25.5 us -> 11 us  [send_weights(): held[way, name, low] = lax.ppermute(part, 'queue', pairs)]
    ppermute x5, waiting for transfers between devices: 10.3 us -> 2.99 us  [summed(): return (block, delta, lax.ppermute(delta, flat, pairs))]
    ppermute x11 -> x7, waiting for transfers between devices: 24.8 us -> 18.7 us  [the longest x1 11.1 us: local(): lax.ppermute(after(bundle(where, mine, got, got_v), *hop_1), 'queue', back)]
    ppermute x2, starting transfers between devices: 0.85 us -> 5.78 us  [local(): lax.ppermute(total[mine:], 'seq', swap)]
    pallas_call x1, Pallas kernels: 12.9 us -> 8.58 us  [attend(): pl.pallas_call(attend_kernel, in_specs=[pl.BlockSpec(memory_space=pltpu.S...]
    ppermute x5, starting transfers between devices: 8.23 us -> 11.8 us  [summed(): return (block, delta, lax.ppermute(delta, flat, pairs))]
    ppermute x11 -> x7, starting transfers between devices: 23 us -> 19.5 us  [the longest x1 5.46 us: local(): lax.ppermute(keep, 'seq', swap)]
  transfers between devices with their start and end apart: 30 -> 26, of which waited for: 11 -> 12; matrix products, arithmetic and copies ran while one was open for 7% -> 8% of each run, Pallas kernels for 18% -> 18%
where the time goes in v3:
time: 169 us; the launch traced here: 168 us
  starting transfers between devices  59.4 us (35%)
  waiting for transfers between devices  53.1 us (31%)
  Pallas kernels  29.8 us (18%)
  other arithmetic  13.1 us (8%)
  local copies, waits for them, and re-layouts  10.4 us (6%)
  between operations  1.78 us (1%)
    ppermute x4, waiting for transfers between devices, spread(): gathered[k, low] = (own, lax.ppermute(own, 'groups', swap))  19.4 us
    pallas_call x5, Pallas kernels, project(): pl.pallas_call(functools.partial(project_kernel, half), in_specs=[pl.Bloc...  17.6 us
    ppermute x6, starting transfers between devices, send_weights(): held[way, name, low] = lax.ppermute(part, 'queue', pairs)  15.1 us
    ppermute x5, starting transfers between devices, summed(): return (block, delta, lax.ppermute(delta, flat, pairs))  11.8 us
    ppermute x1, waiting for transfers between devices, local(): lax.ppermute(after(bundle(where, mine, got, got_v), *hop_1), 'queue', back)  11.1 us
    ppermute x6, waiting for transfers between devices, send_weights(): held[way, name, low] = lax.ppermute(part, 'queue', pairs)  11 us
    pallas_call x1, Pallas kernels, attend(): pl.pallas_call(attend_kernel, in_specs=[pl.BlockSpec(memory_space=pltpu.S...  8.58 us
    unnamed x30, local copies, waits for them, and re-layouts  7.83 us
  transfers between devices with their start and end apart: 26, of which 12 were waited for; matrix products, arithmetic and copies ran while one was open for 8% of the time, Pallas kernels for 18%

profile of v3, /device:TPU:9, one launch (start us, length us, event | category | flops | bytes accessed | tf_op | source)
XLA Modules:
  0.0 167.8 jit_solution(3960323196110247314)
XLA Ops:
  1.4 3.2 %collective-permute-start.2 = (bf16[768,640]{1,0:T(8,128)(2,1)S(1)}, bf16[768,640]{1,0:T(8,128)(2,1)}, u32[]{:S(2)}, u32[]{:S(2)}) collective-permute-start(bf16[768,640]{1,0:T(8,128)(2,1)S(1)} %dynamic_slice.3), channel_id=1, source_target_pairs={{0,4},{4,8},{8,12},{1,5},{5,9},{9,13},{2,6},{6,10},{10,14},{3,7},{... | collective-permute-start | bytes 2949128 | tf_op jit(solution)/shard_map/ppermute | solution.py:334
  4.6 3.0 %collective-permute-start.3 = (bf16[768,640]{1,0:T(8,128)(2,1)S(1)}, bf16[768,640]{1,0:T(8,128)(2,1)}, u32[]{:S(2)}, u32[]{:S(2)}) collective-permute-start(bf16[768,640]{1,0:T(8,128)(2,1)S(1)} %dynamic_slice.3), channel_id=1, source_target_pairs={{12,8},{8,4},{4,0},{13,9},{9,5},{5,1},{14,10},{10,6},{6,2},{15,11}... | collective-permute-start | bytes 2949128 | tf_op jit(solution)/shard_map/ppermute | solution.py:334
  8.6 1.7 copy-done.6
  12.0 1.8 %rotate.1 = (bf16[3,2,128,768]{3,2,1,0:T(8,128)(2,1)S(1)}, bf16[2,2,128,768]{3,2,1,0:T(8,128)(2,1)S(1)}, bf16[2,128,768]{2,1,0:T(8,128)(2,1)S(1)}, bf16[3,2,128,768]{3,2,1,0:T(8,128)(2,1)S(1)}) custom-call(s32[4]{0:T(128)S(1)} %pad_add_fusion.core_ref.where_ref, f32[4,128]{1,0:T(4,128)S(1)} %get-tuple-element.102.cos_ref, ...), custom_call_target="tpu_custom_call" | custom-call | flops 1000 | bytes 1000 | tf_op jit(solution)/shard_map/rotate/pallas_call | solution.py:69
  15.2 2.4 %collective-permute-done.1.got_v = bf16[2,128,768]{2,1,0:T(8,128)(2,1)S(1)} collective-permute-done((bf16[2,128,768]{2,1,0:T(8,128)(2,1)S(1)}, bf16[2,128,768]{2,1,0:T(8,128)(2,1)S(1)}, u32[]{:S(2)}, u32[]{:S(2)}) %collective-permute-start.1) | collective-permute-done | bytes 393248 | tf_op jit(solution)/shard_map/ppermute | solution.py:352
  17.6 1.9 %bundle.1 = bf16[1040,768]{1,0:T(8,128)(2,1)} custom-call(s32[4]{0:T(128)S(1)} %pad_add_fusion.core_ref.where_ref, bf16[3,2,128,768]{3,2,1,0:T(8,128)(2,1)S(1)} %get-tuple-element.52.mine, bf16[2,2,128,768]{3,2,1,0:T(8,128)(2,1)S(1)} %collective-permute-done.got, bf16[2,128,768]{2,1,0:T(8,128)(2,1)S(1)} %collective-permute-done.1.got_v), custom_call_target="tpu_custom_call" | custom-call | flops 1000 | bytes 1000 | tf_op jit(solution)/shard_map/bundle/pallas_call | solution.py:102
  19.4 6.5 %collective-permute-done.2 = bf16[768,640]{1,0:T(8,128)(2,1)} collective-permute-done((bf16[768,640]{1,0:T(8,128)(2,1)S(1)}, bf16[768,640]{1,0:T(8,128)(2,1)}, u32[]{:S(2)}, u32[]{:S(2)}) %collective-permute-start.2) | collective-permute-done | bytes 983072 | tf_op jit(solution)/shard_map/ppermute | solution.py:334
  26.0 2.9 %collective-permute-done.3 = bf16[768,640]{1,0:T(8,128)(2,1)} collective-permute-done((bf16[768,640]{1,0:T(8,128)(2,1)S(1)}, bf16[768,640]{1,0:T(8,128)(2,1)}, u32[]{:S(2)}, u32[]{:S(2)}) %collective-permute-start.3) | collective-permute-done | bytes 983072 | tf_op jit(solution)/shard_map/ppermute | solution.py:334
  28.9 3.0 %collective-permute-start.4 = (bf16[1040,768]{1,0:T(8,128)(2,1)}, bf16[1040,768]{1,0:T(8,128)(2,1)}, u32[]{:S(2)}, u32[]{:S(2)}) collective-permute-start(bf16[1040,768]{1,0:T(8,128)(2,1)} %bundle.1), channel_id=1, source_target_pairs={{4,0},{8,4},{12,8},{5,1},{9,5},{13,9},{6,2},{10,6},{14,10},{7,3},{... | collective-permute-start | bytes 4792328 | tf_op jit(solution)/shard_map/ppermute | solution.py:354
  35.5 3.2 %collective-permute-start.13 = (bf16[768,640]{1,0:T(8,128)(2,1)}, bf16[768,640]{1,0:T(8,128)(2,1)}, u32[]{:S(2)}, u32[]{:S(2)}) collective-permute-start(bf16[768,640]{1,0:T(8,128)(2,1)} %collective-permute-done.2), channel_id=1, source_target_pairs={{4,8},{8,12},{5,9},{9,13},{6,10},{10,14},{7,11},{11,15},{20,24},{2... | collective-permute-start | bytes 2949128 | tf_op jit(solution)/shard_map/ppermute | solution.py:334
  38.8 1.9 %collective-permute-start.14 = (bf16[768,640]{1,0:T(8,128)(2,1)}, bf16[768,640]{1,0:T(8,128)(2,1)}, u32[]{:S(2)}, u32[]{:S(2)}) collective-permute-start(bf16[768,640]{1,0:T(8,128)(2,1)} %collective-permute-done.3), channel_id=1, source_target_pairs={{8,4},{4,0},{9,5},{5,1},{10,6},{6,2},{11,7},{7,3},{24,20},{20,16},... | collective-permute-start | bytes 2949128 | tf_op jit(solution)/shard_map/ppermute | solution.py:334
  40.8 13.7 %collective-permute-done.5.refs_1_ = bf16[768,640]{1,0:T(8,128)(2,1)} collective-permute-done((bf16[768,640]{1,0:T(8,128)(2,1)S(1)}, bf16[768,640]{1,0:T(8,128)(2,1)}, u32[]{:S(2)}, u32[]{:S(2)}) %collective-permute-start.5) | collective-permute-done | bytes 983072 | tf_op jit(solution)/shard_map/ppermute | solution.py:343
  54.5 11.1 %collective-permute-done.4.far_ref = bf16[1040,768]{1,0:T(8,128)(2,1)} collective-permute-done((bf16[1040,768]{1,0:T(8,128)(2,1)}, bf16[1040,768]{1,0:T(8,128)(2,1)}, u32[]{:S(2)}, u32[]{:S(2)}) %collective-permute-start.4) | collective-permute-done | bytes 1597472 | tf_op jit(solution)/shard_map/ppermute | solution.py:354
  68.0 8.6 %attend.1 = (bf16[128,768]{1,0:T(8,128)(2,1)S(1)}, bf16[896,768]{1,0:T(8,128)(2,1)S(1)}) custom-call(s32[4]{0:T(128)S(1)} %pad_add_fusion.core_ref.where_ref, bf16[3,2,128,768]{3,2,1,0:T(8,128)(2,1)S(1)} %get-tuple-element.52.mine, bf16[2,2,128,768]{3,2,1,0:T(8,128)(2,1)S(1)} %copy-done.5, bf16[2,128,768]{2,1,0:T(8,128)(2,1)S(1)} %collective-permute-done.1.got_v, ...), custom_call_target="tpu_custom_call" | custom-call | flops 1000 | bytes 1000 | tf_op jit(solution)/shard_map/attend/pallas_call | solution.py:172
  76.6 3.0 %collective-permute-start.6 = (bf16[128,768]{1,0:T(8,128)(2,1)S(1)}, bf16[128,768]{1,0:T(8,128)(2,1)S(1)}, u32[]{:S(2)}, u32[]{:S(2)}) collective-permute-start(bf16[128,768]{1,0:T(8,128)(2,1)S(1)} %get-tuple-element.57), channel_id=1, source_target_pairs={{4,0},{8,4},{12,8},{5,1},{9,5},{13,9},{6,2},{10,6},{14,10},{7,3},{... | collective-permute-start | bytes 589832 | tf_op jit(solution)/shard_map/ppermute | solution.py:363
  79.7 5.5 %collective-permute-start.8 = (bf16[896,768]{1,0:T(8,128)(2,1)S(1)}, bf16[896,768]{1,0:T(8,128)(2,1)S(1)}, u32[]{:S(2)}, u32[]{:S(2)}) collective-permute-start(bf16[896,768]{1,0:T(8,128)(2,1)S(1)} %get-tuple-element.83.keep_ref), channel_id=1, source_target_pairs={{0,1},{1,0},{2,3},{3,2},{4,5},{5,4},{6,7},{7,6},{8,9},{9,8},{10,11... | collective-permute-start | bytes 4128776 | tf_op jit(solution)/shard_map/ppermute | solution.py:372
  86.7 4.2 %collective-permute-done.6.came_ref = bf16[128,768]{1,0:T(8,128)(2,1)S(1)} collective-permute-done((bf16[128,768]{1,0:T(8,128)(2,1)S(1)}, bf16[128,768]{1,0:T(8,128)(2,1)S(1)}, u32[]{:S(2)}, u32[]{:S(2)}) %collective-permute-start.6) | collective-permute-done | bytes 196640 | tf_op jit(solution)/shard_map/ppermute | solution.py:363
  90.9 3.1 %collective-permute-start.15 = (bf16[768,640]{1,0:T(8,128)(2,1)}, bf16[768,640]{1,0:T(8,128)(2,1)S(1)}, u32[]{:S(2)}, u32[]{:S(2)}) collective-permute-start(bf16[768,640]{1,0:T(8,128)(2,1)} %collective-permute-done.14), channel_id=1, source_target_pairs={{4,0},{5,1},{6,2},{7,3},{20,16},{21,17},{22,18},{23,19}} | collective-permute-start | bytes 2949128 | tf_op jit(solution)/shard_map/ppermute | solution.py:334
  100.7 3.5 %collective-permute-start.9 = (bf16[128,768]{1,0:T(8,128)(2,1)S(1)}, bf16[128,768]{1,0:T(8,128)(2,1)S(1)}, u32[]{:S(2)}, u32[]{:S(2)}) collective-permute-start(bf16[128,768]{1,0:T(8,128)(2,1)S(1)} %collective-permute-done.6.came_ref), channel_id=1, source_target_pairs={{0,1},{1,0},{2,3},{3,2},{4,5},{5,4},{6,7},{7,6},{8,9},{9,8},{10,11... | collective-permute-start | bytes 589832 | tf_op jit(solution)/shard_map/ppermute | solution.py:372
  105.3 4.0 %project.5 = bf16[512,640]{1,0:T(8,128)(2,1)} custom-call(s32[3]{0:T(128)S(1)} %get-tuple-element.101.place_ref, bf16[896,768]{1,0:T(8,128)(2,1)S(1)} %get-tuple-element.83.keep_ref, bf16[128,768]{1,0:T(8,128)(2,1)S(1)} %collective-permute-done.6.came_ref, bf16[896,768]{1,0:T(8,128)(2,1)S(1)} %collective-permute-done.8.peer_keep_ref, ...), custom_call_target="tpu_custom_call" | custom-call | flops 1000 | bytes 1000 | tf_op jit(solution)/shard_map/project/pallas_call | solution.py:250
  110.7 4.8 %project.6 = bf16[512,640]{1,0:T(8,128)(2,1)} custom-call(s32[3]{0:T(128)S(1)} %get-tuple-element.100.place_ref, bf16[896,768]{1,0:T(8,128)(2,1)S(1)} %get-tuple-element.83.keep_ref, bf16[128,768]{1,0:T(8,128)(2,1)S(1)} %collective-permute-done.6.came_ref, bf16[896,768]{1,0:T(8,128)(2,1)S(1)} %collective-permute-done.8.peer_keep_ref, ...), custom_call_target="tpu_custom_call" | custom-call | flops 1000 | bytes 1000 | tf_op jit(solution)/shard_map/project/pallas_call | solution.py:250
  115.5 5.6 %collective-permute-start.12 = (bf16[512,640]{1,0:T(8,128)(2,1)}, bf16[512,640]{1,0:T(8,128)(2,1)}, u32[]{:S(2)}, u32[]{:S(2)}) collective-permute-start(bf16[512,640]{1,0:T(8,128)(2,1)} %project.6), channel_id=1, source_target_pairs={{2,0},{4,6},{10,8},{12,14},{3,1},{5,7},{11,9},{13,15},{18,16},{20,... | collective-permute-start | bytes 1966088 | tf_op jit(solution)/shard_map/ppermute | solution.py:407
  121.1 2.4 %select_select_fusion.refs_0_ = bf16[768,512]{1,0:T(8,128)(2,1)} fusion(bf16[768,640]{1,0:T(8,128)(2,1)} %collective-permute-done.3, bf16[768,640]{1,0:T(8,128)(2,1)S(1)} %collective-permute-done.15, bf16[768,640]{1,0:T(8,128)(2,1)} %collective-permute-done.2, bf16[768,640]{1,0:T(8,128)(2,1)S(1)} %collective-permute-done.16, pred[]{:T(512)S(6)} %eq.38, ...), kind=kLoop, calls=%fused_computation.10 | loop fusion | flops 1179648 | bytes 3932163 | tf_op jit(solution)/shard_map/jit(_where)/select_n | solution.py:280
  123.7 1.7 %select_select_fusion.1.refs_0_ = bf16[768,128]{1,0:T(8,128)(2,1)} fusion(bf16[768,640]{1,0:T(8,128)(2,1)} %collective-permute-done.3, bf16[768,640]{1,0:T(8,128)(2,1)S(1)} %collective-permute-done.15, bf16[768,640]{1,0:T(8,128)(2,1)} %collective-permute-done.2, bf16[768,640]{1,0:T(8,128)(2,1)S(1)} %collective-permute-done.16, pred[]{:T(512)S(6)} %eq.38, ...), kind=kLoop, calls=%fused_computation.35 | loop fusion | flops 294912 | bytes 983043 | tf_op jit(solution)/shard_map/jit(_where)/select_n | solution.py:280
  125.5 4.0 %project.7 = bf16[512,640]{1,0:T(8,128)(2,1)} custom-call(s32[3]{0:T(128)S(1)} %get-tuple-element.99.place_ref, bf16[896,768]{1,0:T(8,128)(2,1)S(1)} %get-tuple-element.83.keep_ref, bf16[128,768]{1,0:T(8,128)(2,1)S(1)} %collective-permute-done.6.came_ref, bf16[896,768]{1,0:T(8,128)(2,1)S(1)} %collective-permute-done.8.peer_keep_ref, ...), custom_call_target="tpu_custom_call" | custom-call | flops 1000 | bytes 1000 | tf_op jit(solution)/shard_map/project/pallas_call | solution.py:250
  129.5 2.2 %collective-permute-start.18 = (bf16[512,640]{1,0:T(8,128)(2,1)}, bf16[512,640]{1,0:T(8,128)(2,1)}, u32[]{:S(2)}, u32[]{:S(2)}) collective-permute-start(bf16[512,640]{1,0:T(8,128)(2,1)} %project.7), channel_id=1, source_target_pairs={{0,2},{4,6},{10,8},{14,12},{1,3},{5,7},{11,9},{15,13},{16,18},{20,... | collective-permute-start | bytes 1966088 | tf_op jit(solution)/shard_map/ppermute | solution.py:407
  131.7 3.1 %collective-permute-start.7 = (bf16[2,128,2560]{2,1,0:T(8,128)(2,1)}, bf16[2,128,2560]{2,1,0:T(8,128)(2,1)}, u32[]{:S(2)}, u32[]{:S(2)}) collective-permute-start(bf16[2,128,2560]{2,1,0:T(8,128)(2,1)} %param.9), channel_id=1, source_target_pairs={{1,0},{4,1},{5,4},{8,5},{9,8},{12,9},{13,12},{3,2},{6,3},{7,6},{10... | collective-permute-start | bytes 3932168 | tf_op jit(solution)/shard_map/ppermute | solution.py:377
  136.2 5.7 %collective-permute-done.20.refs_1_ = bf16[768,512]{1,0:T(8,128)(2,1)} collective-permute-done((bf16[768,512]{1,0:T(8,128)(2,1)}, bf16[768,512]{1,0:T(8,128)(2,1)}, u32[]{:S(2)}, u32[]{:S(2)}) %collective-permute-start.20) | collective-permute-done | bytes 786464 | tf_op jit(solution)/shard_map/ppermute | solution.py:343
  141.9 3.2 %project.8 = bf16[512,512]{1,0:T(8,128)(2,1)S(1)} custom-call(s32[3]{0:T(128)S(1)} %get-tuple-element.98.place_ref, bf16[896,768]{1,0:T(8,128)(2,1)S(1)} %get-tuple-element.83.keep_ref, bf16[128,768]{1,0:T(8,128)(2,1)S(1)} %collective-permute-done.6.came_ref, bf16[896,768]{1,0:T(8,128)(2,1)S(1)} %collective-permute-done.8.peer_keep_ref, ...), custom_call_target="tpu_custom_call" | custom-call | flops 1000 | bytes 1000 | tf_op jit(solution)/shard_map/project/pallas_call | solution.py:250
  148.0 2.9 %add_convert_fusion.1 = (bf16[512,640]{1,0:T(8,128)(2,1)S(1)}, bf16[512,640]{1,0:T(8,128)(2,1)S(1)}) fusion(bf16[512,640]{1,0:T(8,128)(2,1)} %collective-permute-done.11, bf16[512,640]{1,0:T(8,128)(2,1)} %project.5, bf16[512,640]{1,0:T(8,128)(2,1)} %collective-permute-done.12, bf16[512,640]{1,0:T(8,128)(2,1)} %project.6, ...), kind=kLoop, calls=%fused_computation.2 | loop fusion | flops 6881280 | bytes 5242886 | tf_op jit(solution)/shard_map/convert.3
  151.0 1.8 %collective-permute-start.19 = (bf16[256,1280]{1,0:T(8,128)(2,1)S(1)}, bf16[256,1280]{1,0:T(8,128)(2,1)S(1)}, u32[]{:S(2)}, u32[]{:S(2)}) collective-permute-start(bf16[256,1280]{1,0:T(8,128)(2,1)S(1)} %pad_maximum_fusion), channel_id=1, source_target_pairs={{0,1},{1,0},{2,3},{3,2},{4,5},{5,4},{6,7},{7,6},{8,9},{9,8},{10,11... | collective-permute-start | bytes 1966088 | tf_op jit(solution)/shard_map/ppermute | solution.py:439
  157.3 5.7 %collective-permute-start.22 = (bf16[256,512]{1,0:T(8,128)(2,1)S(1)}, bf16[256,512]{1,0:T(8,128)(2,1)S(1)}, u32[]{:S(2)}, u32[]{:S(2)}) collective-permute-start(bf16[256,512]{1,0:T(8,128)(2,1)S(1)} %slice.146), channel_id=1, source_target_pairs={{0,1},{1,0},{2,3},{3,2},{4,5},{5,4},{6,7},{7,6},{8,9},{9,8},{10,11... | collective-permute-start | bytes 786440 | tf_op jit(solution)/shard_map/ppermute | solution.py:443
  (92 shorter events, 34.6 us)
Async XLA Ops:
  0.0 95.9 %copy-start = (bf16[50,2560]{1,0:T(8,128)(2,1)S(1)}, bf16[50,2560]{1,0:T(8,128)(2,1)}, u32[]{:S(2)}) copy-start(bf16[50,2560]{1,0:T(8,128)(2,1)} %param.13) | copy-start | bytes 768004
  0.0 8.3 %copy-start.14 = (s32[2]{0:T(128)S(1)}, s32[2]{0:T(128)}, u32[]{:S(2)}) copy-start(s32[2]{0:T(128)} %param.11) | copy-start | bytes 28
  0.0 8.3 %copy-start.13 = (s32[2]{0:T(128)S(1)}, s32[2]{0:T(128)}, u32[]{:S(2)}) copy-start(s32[2]{0:T(128)} %param.17) | copy-start | bytes 28
  1.4 24.6 %collective-permute-start.2 = (bf16[768,640]{1,0:T(8,128)(2,1)S(1)}, bf16[768,640]{1,0:T(8,128)(2,1)}, u32[]{:S(2)}, u32[]{:S(2)}) collective-permute-start(bf16[768,640]{1,0:T(8,128)(2,1)S(1)} %dynamic_slice.3), channel_id=1, source_target_pairs={{0,4},{4,8},{8,12},{1,5},{5,9},{9,13},{2,6},{6,10},{10,14},{3,7},{... | collective-permute-start | bytes 2949128 | tf_op jit(solution)/shard_map/ppermute | solution.py:334
  4.6 24.3 %collective-permute-start.3 = (bf16[768,640]{1,0:T(8,128)(2,1)S(1)}, bf16[768,640]{1,0:T(8,128)(2,1)}, u32[]{:S(2)}, u32[]{:S(2)}) collective-permute-start(bf16[768,640]{1,0:T(8,128)(2,1)S(1)} %dynamic_slice.3), channel_id=1, source_target_pairs={{12,8},{8,4},{4,0},{13,9},{9,5},{5,1},{14,10},{10,6},{6,2},{15,11}... | collective-permute-start | bytes 2949128 | tf_op jit(solution)/shard_map/ppermute | solution.py:334
  13.8 5.6 %copy-start.8 = (bf16[3,2,128,768]{3,2,1,0:T(8,128)(2,1)}, bf16[3,2,128,768]{3,2,1,0:T(8,128)(2,1)S(1)}, u32[]{:S(2)}) copy-start(bf16[3,2,128,768]{3,2,1,0:T(8,128)(2,1)S(1)} %get-tuple-element.55.fresh) | copy-start | bytes 3538948
  13.8 3.8 %collective-permute-start = (bf16[2,2,128,768]{3,2,1,0:T(8,128)(2,1)S(1)}, bf16[2,2,128,768]{3,2,1,0:T(8,128)(2,1)S(1)}, u32[]{:S(2)}, u32[]{:S(2)}) collective-permute-start(bf16[2,2,128,768]{3,2,1,0:T(8,128)(2,1)S(1)} %get-tuple-element.48), channel_id=1, source_target_pairs={{0,1},{1,0},{2,3},{3,2},{4,5},{5,4},{6,7},{7,6},{8,9},{9,8},{10,11... | collective-permute-start | bytes 2359304 | tf_op jit(solution)/shard_map/ppermute | solution.py:352
  15.1 2.5 %collective-permute-start.1 = (bf16[2,128,768]{2,1,0:T(8,128)(2,1)S(1)}, bf16[2,128,768]{2,1,0:T(8,128)(2,1)S(1)}, u32[]{:S(2)}, u32[]{:S(2)}) collective-permute-start(bf16[2,128,768]{2,1,0:T(8,128)(2,1)S(1)} %get-tuple-element.49), channel_id=1, source_target_pairs={{0,1},{1,0},{2,3},{3,2},{4,5},{5,4},{6,7},{7,6},{8,9},{9,8},{10,11... | collective-permute-start | bytes 1179656 | tf_op jit(solution)/shard_map/ppermute | solution.py:352
  28.9 36.7 %collective-permute-start.4 = (bf16[1040,768]{1,0:T(8,128)(2,1)}, bf16[1040,768]{1,0:T(8,128)(2,1)}, u32[]{:S(2)}, u32[]{:S(2)}) collective-permute-start(bf16[1040,768]{1,0:T(8,128)(2,1)} %bundle.1), channel_id=1, source_target_pairs={{4,0},{8,4},{12,8},{5,1},{9,5},{13,9},{6,2},{10,6},{14,10},{7,3},{... | collective-permute-start | bytes 4792328 | tf_op jit(solution)/shard_map/ppermute | solution.py:354
  33.2 21.3 %collective-permute-start.5 = (bf16[768,640]{1,0:T(8,128)(2,1)S(1)}, bf16[768,640]{1,0:T(8,128)(2,1)}, u32[]{:S(2)}, u32[]{:S(2)}) collective-permute-start(bf16[768,640]{1,0:T(8,128)(2,1)S(1)} %broadcast_select_fusion.2.refs_0_), channel_id=1, source_target_pairs={{0,16},{16,0},{1,17},{17,1},{2,18},{18,2},{3,19},{19,3},{4,20},{20... | collective-permute-start | bytes 2949128 | tf_op jit(solution)/shard_map/ppermute | solution.py:343
  35.5 49.6 %collective-permute-start.13 = (bf16[768,640]{1,0:T(8,128)(2,1)}, bf16[768,640]{1,0:T(8,128)(2,1)}, u32[]{:S(2)}, u32[]{:S(2)}) collective-permute-start(bf16[768,640]{1,0:T(8,128)(2,1)} %collective-permute-done.2), channel_id=1, source_target_pairs={{4,8},{8,12},{5,9},{9,13},{6,10},{10,14},{7,11},{11,15},{20,24},{2... | collective-permute-start | bytes 2949128 | tf_op jit(solution)/shard_map/ppermute | solution.py:334
  38.8 47.9 %collective-permute-start.14 = (bf16[768,640]{1,0:T(8,128)(2,1)}, bf16[768,640]{1,0:T(8,128)(2,1)}, u32[]{:S(2)}, u32[]{:S(2)}) collective-permute-start(bf16[768,640]{1,0:T(8,128)(2,1)} %collective-permute-done.3), channel_id=1, source_target_pairs={{8,4},{4,0},{9,5},{5,1},{10,6},{6,2},{11,7},{7,3},{24,20},{20,16},... | collective-permute-start | bytes 2949128 | tf_op jit(solution)/shard_map/ppermute | solution.py:334
  68.0 37.3 %copy-start.1 = (bf16[1536,1280]{1,0:T(8,128)(2,1)S(1)}, bf16[1536,1280]{1,0:T(8,128)(2,1)}, u32[]{:S(2)}) copy-start(bf16[1536,1280]{1,0:T(8,128)(2,1)} %refs_0_.1) | copy-start | bytes 11796484
  76.6 14.3 %collective-permute-start.6 = (bf16[128,768]{1,0:T(8,128)(2,1)S(1)}, bf16[128,768]{1,0:T(8,128)(2,1)S(1)}, u32[]{:S(2)}, u32[]{:S(2)}) collective-permute-start(bf16[128,768]{1,0:T(8,128)(2,1)S(1)} %get-tuple-element.57), channel_id=1, source_target_pairs={{4,0},{8,4},{12,8},{5,1},{9,5},{13,9},{6,2},{10,6},{14,10},{7,3},{... | collective-permute-start | bytes 589832 | tf_op jit(solution)/shard_map/ppermute | solution.py:363
  79.7 25.6 %collective-permute-start.8 = (bf16[896,768]{1,0:T(8,128)(2,1)S(1)}, bf16[896,768]{1,0:T(8,128)(2,1)S(1)}, u32[]{:S(2)}, u32[]{:S(2)}) collective-permute-start(bf16[896,768]{1,0:T(8,128)(2,1)S(1)} %get-tuple-element.83.keep_ref), channel_id=1, source_target_pairs={{0,1},{1,0},{2,3},{3,2},{4,5},{5,4},{6,7},{7,6},{8,9},{9,8},{10,11... | collective-permute-start | bytes 4128776 | tf_op jit(solution)/shard_map/ppermute | solution.py:372
  90.9 30.2 %collective-permute-start.15 = (bf16[768,640]{1,0:T(8,128)(2,1)}, bf16[768,640]{1,0:T(8,128)(2,1)S(1)}, u32[]{:S(2)}, u32[]{:S(2)}) collective-permute-start(bf16[768,640]{1,0:T(8,128)(2,1)} %collective-permute-done.14), channel_id=1, source_target_pairs={{4,0},{5,1},{6,2},{7,3},{20,16},{21,17},{22,18},{23,19}} | collective-permute-start | bytes 2949128 | tf_op jit(solution)/shard_map/ppermute | solution.py:334
  96.1 4.6 %collective-permute-start.10 = (bf16[2,2560]{1,0:T(2,128)(2,1)S(1)}, bf16[2,2560]{1,0:T(2,128)(2,1)S(1)}, u32[]{:S(2)}, u32[]{:S(2)}) collective-permute-start(bf16[2,2560]{1,0:T(2,128)(2,1)S(1)} %convolution_convert_fusion), channel_id=1, source_target_pairs={{0,2},{2,0},{1,3},{3,1},{4,6},{6,4},{5,7},{7,5},{8,10},{10,8},{9,1... | collective-permute-start | bytes 30728 | tf_op jit(solution)/shard_map/ppermute | solution.py:385
  98.7 22.4 %collective-permute-start.16 = (bf16[768,640]{1,0:T(8,128)(2,1)}, bf16[768,640]{1,0:T(8,128)(2,1)S(1)}, u32[]{:S(2)}, u32[]{:S(2)}) collective-permute-start(bf16[768,640]{1,0:T(8,128)(2,1)} %collective-permute-done.13), channel_id=1, source_target_pairs={{8,12},{9,13},{10,14},{11,15},{24,28},{25,29},{26,30},{27,31}} | collective-permute-start | bytes 2949128 | tf_op jit(solution)/shard_map/ppermute | solution.py:334
  99.4 26.0 %collective-permute-start.17 = (bf16[768,640]{1,0:T(8,128)(2,1)S(1)}, bf16[768,640]{1,0:T(8,128)(2,1)S(1)}, u32[]{:S(2)}, u32[]{:S(2)}) collective-permute-start(bf16[768,640]{1,0:T(8,128)(2,1)S(1)} %broadcast_select_fusion.1.refs_0_), channel_id=1, source_target_pairs={{0,16},{16,0},{1,17},{17,1},{2,18},{18,2},{3,19},{19,3},{4,20},{20... | collective-permute-start | bytes 2949128 | tf_op jit(solution)/shard_map/ppermute | solution.py:343
  100.7 4.6 %collective-permute-start.9 = (bf16[128,768]{1,0:T(8,128)(2,1)S(1)}, bf16[128,768]{1,0:T(8,128)(2,1)S(1)}, u32[]{:S(2)}, u32[]{:S(2)}) collective-permute-start(bf16[128,768]{1,0:T(8,128)(2,1)S(1)} %collective-permute-done.6.came_ref), channel_id=1, source_target_pairs={{0,1},{1,0},{2,3},{3,2},{4,5},{5,4},{6,7},{7,6},{8,9},{9,8},{10,11... | collective-permute-start | bytes 589832 | tf_op jit(solution)/shard_map/ppermute | solution.py:372
  109.4 26.8 %collective-permute-start.11 = (bf16[512,640]{1,0:T(8,128)(2,1)}, bf16[512,640]{1,0:T(8,128)(2,1)}, u32[]{:S(2)}, u32[]{:S(2)}) collective-permute-start(bf16[512,640]{1,0:T(8,128)(2,1)} %project.5), channel_id=1, source_target_pairs={{2,0},{6,4},{8,10},{12,14},{3,1},{7,5},{9,11},{13,15},{18,16},{22,... | collective-permute-start | bytes 1966088 | tf_op jit(solution)/shard_map/ppermute | solution.py:407
  115.5 19.4 %collective-permute-start.12 = (bf16[512,640]{1,0:T(8,128)(2,1)}, bf16[512,640]{1,0:T(8,128)(2,1)}, u32[]{:S(2)}, u32[]{:S(2)}) collective-permute-start(bf16[512,640]{1,0:T(8,128)(2,1)} %project.6), channel_id=1, source_target_pairs={{2,0},{4,6},{10,8},{12,14},{3,1},{5,7},{11,9},{13,15},{18,16},{20,... | collective-permute-start | bytes 1966088 | tf_op jit(solution)/shard_map/ppermute | solution.py:407
  123.5 18.4 %collective-permute-start.20 = (bf16[768,512]{1,0:T(8,128)(2,1)}, bf16[768,512]{1,0:T(8,128)(2,1)}, u32[]{:S(2)}, u32[]{:S(2)}) collective-permute-start(bf16[768,512]{1,0:T(8,128)(2,1)} %select_select_fusion.refs_0_), channel_id=1, source_target_pairs={{0,16},{16,0},{1,17},{17,1},{2,18},{18,2},{3,19},{19,3},{4,20},{20... | collective-permute-start | bytes 2359304 | tf_op jit(solution)/shard_map/ppermute | solution.py:343
  129.5 18.5 %collective-permute-start.18 = (bf16[512,640]{1,0:T(8,128)(2,1)}, bf16[512,640]{1,0:T(8,128)(2,1)}, u32[]{:S(2)}, u32[]{:S(2)}) collective-permute-start(bf16[512,640]{1,0:T(8,128)(2,1)} %project.7), channel_id=1, source_target_pairs={{0,2},{4,6},{10,8},{14,12},{1,3},{5,7},{11,9},{15,13},{16,18},{20,... | collective-permute-start | bytes 1966088 | tf_op jit(solution)/shard_map/ppermute | solution.py:407
  131.7 31.3 %collective-permute-start.7 = (bf16[2,128,2560]{2,1,0:T(8,128)(2,1)}, bf16[2,128,2560]{2,1,0:T(8,128)(2,1)}, u32[]{:S(2)}, u32[]{:S(2)}) collective-permute-start(bf16[2,128,2560]{2,1,0:T(8,128)(2,1)} %param.9), channel_id=1, source_target_pairs={{1,0},{4,1},{5,4},{8,5},{9,8},{12,9},{13,12},{3,2},{6,3},{7,6},{10... | collective-permute-start | bytes 3932168 | tf_op jit(solution)/shard_map/ppermute | solution.py:377
  134.9 17.9 %collective-permute-start.23 = (bf16[768,128]{1,0:T(8,128)(2,1)}, bf16[768,128]{1,0:T(8,128)(2,1)S(1)}, u32[]{:S(2)}, u32[]{:S(2)}) collective-permute-start(bf16[768,128]{1,0:T(8,128)(2,1)} %select_select_fusion.1.refs_0_), channel_id=1, source_target_pairs={{0,16},{16,0},{1,17},{17,1},{2,18},{18,2},{3,19},{19,3},{4,20},{20... | collective-permute-start | bytes 589832 | tf_op jit(solution)/shard_map/ppermute | solution.py:343
  145.1 12.0 %collective-permute-start.21 = (bf16[512,512]{1,0:T(8,128)(2,1)S(1)}, bf16[512,512]{1,0:T(8,128)(2,1)S(1)}, u32[]{:S(2)}, u32[]{:S(2)}) collective-permute-start(bf16[512,512]{1,0:T(8,128)(2,1)S(1)} %project.8), channel_id=1, source_target_pairs={{0,2},{6,4},{8,10},{14,12},{1,3},{7,5},{9,11},{15,13},{16,18},{22,... | collective-permute-start | bytes 1572872 | tf_op jit(solution)/shard_map/ppermute | solution.py:407
  151.0 13.6 %collective-permute-start.19 = (bf16[256,1280]{1,0:T(8,128)(2,1)S(1)}, bf16[256,1280]{1,0:T(8,128)(2,1)S(1)}, u32[]{:S(2)}, u32[]{:S(2)}) collective-permute-start(bf16[256,1280]{1,0:T(8,128)(2,1)S(1)} %pad_maximum_fusion), channel_id=1, source_target_pairs={{0,1},{1,0},{2,3},{3,2},{4,5},{5,4},{6,7},{7,6},{8,9},{9,8},{10,11... | collective-permute-start | bytes 1966088 | tf_op jit(solution)/shard_map/ppermute | solution.py:439
  154.3 8.7 %copy-start.11 = (bf16[2,128,2560]{2,1,0:T(8,128)(2,1)S(1)}, bf16[2,128,2560]{2,1,0:T(8,128)(2,1)}, u32[]{:S(2)}) copy-start(bf16[2,128,2560]{2,1,0:T(8,128)(2,1)} %param.15) | copy-start | bytes 3932164
  154.3 10.1 %collective-permute-start.24 = (bf16[512,128]{1,0:T(8,128)(2,1)S(1)}, bf16[512,128]{1,0:T(8,128)(2,1)S(1)}, u32[]{:S(2)}, u32[]{:S(2)}) collective-permute-start(bf16[512,128]{1,0:T(8,128)(2,1)S(1)} %project.9), channel_id=1, source_target_pairs={{0,2},{6,4},{8,10},{14,12},{1,3},{7,5},{9,11},{15,13},{16,18},{22,... | collective-permute-start | bytes 393224 | tf_op jit(solution)/shard_map/ppermute | solution.py:407
  157.3 7.3 %collective-permute-start.22 = (bf16[256,512]{1,0:T(8,128)(2,1)S(1)}, bf16[256,512]{1,0:T(8,128)(2,1)S(1)}, u32[]{:S(2)}, u32[]{:S(2)}) collective-permute-start(bf16[256,512]{1,0:T(8,128)(2,1)S(1)} %slice.146), channel_id=1, source_target_pairs={{0,1},{1,0},{2,3},{3,2},{4,5},{5,4},{6,7},{7,6},{8,9},{9,8},{10,11... | collective-permute-start | bytes 786440 | tf_op jit(solution)/shard_map/ppermute | solution.py:443
  164.5 1.3 collective-permute-start.25
  (9 other events, 16.8 us)

commit v4 on v3

--- a/solution.py
+++ b/solution.py
@@ -327,7 +327,7 @@
     held = {}
 
     def send_weights(name, block, low, hops, ends):
-        for way, part, sign in (("up", block[0], 1), ("down", block[1], -1)):
+        for way, part, sign in (("down", block[1], -1), ("up", block[0], 1)):
             pairs = [(i, i + hops) for i in range(count - hops) if i >= ends]
             if sign < 0:
                 pairs = [(count - 1 - i, count - 1 - j) for i, j in pairs]
@@ -407,7 +407,7 @@
         return block, delta, lax.ppermute(delta, flat, pairs)
 
     results, late, picked = [], [], []
-    for n in range(k):
+    for n in [1, 0][2 - min(k, 2) :] + list(range(2, k)):
         pieces = [out_weight] if n == 0 else gathered[n, 0]
         if n == k - 1:
             for low, high in chunks:

time: 169 us -> 167 us (0.988)
  waiting for transfers between devices: 53.1 us -> 50.1 us
    ppermute x4, waiting for transfers between devices: 19.4 us -> 16.2 us  [spread(): gathered[k, low] = (own, lax.ppermute(own, 'groups', swap))]
where the time goes in v4:
time: 167 us; the launch traced here: 166 us
  starting transfers between devices  60.7 us (36%)
  waiting for transfers between devices  50.1 us (30%)
  Pallas kernels  29.8 us (18%)
  other arithmetic  13.2 us (8%)
  local copies, waits for them, and re-layouts  10.4 us (6%)
  between operations  1.79 us (1%)
    pallas_call x5, Pallas kernels, project(): pl.pallas_call(functools.partial(project_kernel, half), in_specs=[pl.Bloc...  17.7 us
    ppermute x4, waiting for transfers between devices, spread(): gathered[k, low] = (own, lax.ppermute(own, 'groups', swap))  16.2 us
    ppermute x6, starting transfers between devices, send_weights(): held[way, name, low] = lax.ppermute(part, 'queue', pairs)  15.1 us
    ppermute x5, starting transfers between devices, summed(): return (block, delta, lax.ppermute(delta, flat, pairs))  12.7 us
    ppermute x1, waiting for transfers between devices, local(): lax.ppermute(after(bundle(where, mine, got, got_v), *hop_1), 'queue', back)  11.1 us
    ppermute x6, waiting for transfers between devices, send_weights(): held[way, name, low] = lax.ppermute(part, 'queue', pairs)  11.1 us
    pallas_call x1, Pallas kernels, attend(): pl.pallas_call(attend_kernel, in_specs=[pl.BlockSpec(memory_space=pltpu.S...  8.41 us
    unnamed x30, local copies, waits for them, and re-layouts  7.83 us
  transfers between devices with their start and end apart: 26, of which 12 were waited for; matrix products, arithmetic and copies ran while one was open for 8% of the time, Pallas kernels for 18%

profile of v4, /device:TPU:9, one launch (start us, length us, event | category | flops | bytes accessed | tf_op | source)
XLA Modules:
  0.0 166.3 jit_solution(17721957143079628003)
XLA Ops:
  1.4 3.2 %collective-permute-start.2 = (bf16[768,640]{1,0:T(8,128)(2,1)S(1)}, bf16[768,640]{1,0:T(8,128)(2,1)}, u32[]{:S(2)}, u32[]{:S(2)}) collective-permute-start(bf16[768,640]{1,0:T(8,128)(2,1)S(1)} %dynamic_slice.3), channel_id=1, source_target_pairs={{0,4},{4,8},{8,12},{1,5},{5,9},{9,13},{2,6},{6,10},{10,14},{3,7},{... | collective-permute-start | bytes 2949128 | tf_op jit(solution)/shard_map/ppermute | solution.py:334
  4.6 3.0 %collective-permute-start.3 = (bf16[768,640]{1,0:T(8,128)(2,1)S(1)}, bf16[768,640]{1,0:T(8,128)(2,1)}, u32[]{:S(2)}, u32[]{:S(2)}) collective-permute-start(bf16[768,640]{1,0:T(8,128)(2,1)S(1)} %dynamic_slice.3), channel_id=1, source_target_pairs={{12,8},{8,4},{4,0},{13,9},{9,5},{5,1},{14,10},{10,6},{6,2},{15,11}... | collective-permute-start | bytes 2949128 | tf_op jit(solution)/shard_map/ppermute | solution.py:334
  12.0 1.8 %rotate.1 = (bf16[3,2,128,768]{3,2,1,0:T(8,128)(2,1)S(1)}, bf16[2,2,128,768]{3,2,1,0:T(8,128)(2,1)S(1)}, bf16[2,128,768]{2,1,0:T(8,128)(2,1)S(1)}, bf16[3,2,128,768]{3,2,1,0:T(8,128)(2,1)S(1)}) custom-call(s32[4]{0:T(128)S(1)} %pad_add_fusion.core_ref.where_ref, f32[4,128]{1,0:T(4,128)S(1)} %get-tuple-element.102.cos_ref, ...), custom_call_target="tpu_custom_call" | custom-call | flops 1000 | bytes 1000 | tf_op jit(solution)/shard_map/rotate/pallas_call | solution.py:69
  15.2 2.4 %collective-permute-done.1.got_v = bf16[2,128,768]{2,1,0:T(8,128)(2,1)S(1)} collective-permute-done((bf16[2,128,768]{2,1,0:T(8,128)(2,1)S(1)}, bf16[2,128,768]{2,1,0:T(8,128)(2,1)S(1)}, u32[]{:S(2)}, u32[]{:S(2)}) %collective-permute-start.1) | collective-permute-done | bytes 393248 | tf_op jit(solution)/shard_map/ppermute | solution.py:352
  17.6 1.9 %bundle.1 = bf16[1040,768]{1,0:T(8,128)(2,1)} custom-call(s32[4]{0:T(128)S(1)} %pad_add_fusion.core_ref.where_ref, bf16[3,2,128,768]{3,2,1,0:T(8,128)(2,1)S(1)} %get-tuple-element.52.mine, bf16[2,2,128,768]{3,2,1,0:T(8,128)(2,1)S(1)} %collective-permute-done.got, bf16[2,128,768]{2,1,0:T(8,128)(2,1)S(1)} %collective-permute-done.1.got_v), custom_call_target="tpu_custom_call" | custom-call | flops 1000 | bytes 1000 | tf_op jit(solution)/shard_map/bundle/pallas_call | solution.py:102
  19.4 6.5 %collective-permute-done.2 = bf16[768,640]{1,0:T(8,128)(2,1)} collective-permute-done((bf16[768,640]{1,0:T(8,128)(2,1)S(1)}, bf16[768,640]{1,0:T(8,128)(2,1)}, u32[]{:S(2)}, u32[]{:S(2)}) %collective-permute-start.2) | collective-permute-done | bytes 983072 | tf_op jit(solution)/shard_map/ppermute | solution.py:334
  26.0 2.9 %collective-permute-done.3 = bf16[768,640]{1,0:T(8,128)(2,1)} collective-permute-done((bf16[768,640]{1,0:T(8,128)(2,1)S(1)}, bf16[768,640]{1,0:T(8,128)(2,1)}, u32[]{:S(2)}, u32[]{:S(2)}) %collective-permute-start.3) | collective-permute-done | bytes 983072 | tf_op jit(solution)/shard_map/ppermute | solution.py:334
  28.9 3.0 %collective-permute-start.4 = (bf16[1040,768]{1,0:T(8,128)(2,1)}, bf16[1040,768]{1,0:T(8,128)(2,1)}, u32[]{:S(2)}, u32[]{:S(2)}) collective-permute-start(bf16[1040,768]{1,0:T(8,128)(2,1)} %bundle.1), channel_id=1, source_target_pairs={{4,0},{8,4},{12,8},{5,1},{9,5},{13,9},{6,2},{10,6},{14,10},{7,3},{... | collective-permute-start | bytes 4792328 | tf_op jit(solution)/shard_map/ppermute | solution.py:354
  35.5 3.2 %collective-permute-start.13 = (bf16[768,640]{1,0:T(8,128)(2,1)}, bf16[768,640]{1,0:T(8,128)(2,1)}, u32[]{:S(2)}, u32[]{:S(2)}) collective-permute-start(bf16[768,640]{1,0:T(8,128)(2,1)} %collective-permute-done.2), channel_id=1, source_target_pairs={{4,8},{8,12},{5,9},{9,13},{6,10},{10,14},{7,11},{11,15},{20,24},{2... | collective-permute-start | bytes 2949128 | tf_op jit(solution)/shard_map/ppermute | solution.py:334
  38.8 1.9 %collective-permute-start.14 = (bf16[768,640]{1,0:T(8,128)(2,1)}, bf16[768,640]{1,0:T(8,128)(2,1)}, u32[]{:S(2)}, u32[]{:S(2)}) collective-permute-start(bf16[768,640]{1,0:T(8,128)(2,1)} %collective-permute-done.3), channel_id=1, source_target_pairs={{8,4},{4,0},{9,5},{5,1},{10,6},{6,2},{11,7},{7,3},{24,20},{20,16},... | collective-permute-start | bytes 2949128 | tf_op jit(solution)/shard_map/ppermute | solution.py:334
  40.8 13.7 %collective-permute-done.5.refs_1_ = bf16[768,640]{1,0:T(8,128)(2,1)} collective-permute-done((bf16[768,640]{1,0:T(8,128)(2,1)S(1)}, bf16[768,640]{1,0:T(8,128)(2,1)}, u32[]{:S(2)}, u32[]{:S(2)}) %collective-permute-start.5) | collective-permute-done | bytes 983072 | tf_op jit(solution)/shard_map/ppermute | solution.py:343
  54.5 11.1 %collective-permute-done.4.far_ref = bf16[1040,768]{1,0:T(8,128)(2,1)} collective-permute-done((bf16[1040,768]{1,0:T(8,128)(2,1)}, bf16[1040,768]{1,0:T(8,128)(2,1)}, u32[]{:S(2)}, u32[]{:S(2)}) %collective-permute-start.4) | collective-permute-done | bytes 1597472 | tf_op jit(solution)/shard_map/ppermute | solution.py:354
  68.0 8.4 %attend.1 = (bf16[128,768]{1,0:T(8,128)(2,1)S(1)}, bf16[896,768]{1,0:T(8,128)(2,1)S(1)}) custom-call(s32[4]{0:T(128)S(1)} %pad_add_fusion.core_ref.where_ref, bf16[3,2,128,768]{3,2,1,0:T(8,128)(2,1)S(1)} %get-tuple-element.52.mine, bf16[2,2,128,768]{3,2,1,0:T(8,128)(2,1)S(1)} %copy-done.5, bf16[2,128,768]{2,1,0:T(8,128)(2,1)S(1)} %collective-permute-done.1.got_v, ...), custom_call_target="tpu_custom_call" | custom-call | flops 1000 | bytes 1000 | tf_op jit(solution)/shard_map/attend/pallas_call | solution.py:172
  76.4 3.0 %collective-permute-start.6 = (bf16[128,768]{1,0:T(8,128)(2,1)S(1)}, bf16[128,768]{1,0:T(8,128)(2,1)S(1)}, u32[]{:S(2)}, u32[]{:S(2)}) collective-permute-start(bf16[128,768]{1,0:T(8,128)(2,1)S(1)} %get-tuple-element.57), channel_id=1, source_target_pairs={{4,0},{8,4},{12,8},{5,1},{9,5},{13,9},{6,2},{10,6},{14,10},{7,3},{... | collective-permute-start | bytes 589832 | tf_op jit(solution)/shard_map/ppermute | solution.py:363
  79.5 5.5 %collective-permute-start.8 = (bf16[896,768]{1,0:T(8,128)(2,1)S(1)}, bf16[896,768]{1,0:T(8,128)(2,1)S(1)}, u32[]{:S(2)}, u32[]{:S(2)}) collective-permute-start(bf16[896,768]{1,0:T(8,128)(2,1)S(1)} %get-tuple-element.83.keep_ref), channel_id=1, source_target_pairs={{0,1},{1,0},{2,3},{3,2},{4,5},{5,4},{6,7},{7,6},{8,9},{9,8},{10,11... | collective-permute-start | bytes 4128776 | tf_op jit(solution)/shard_map/ppermute | solution.py:372
  86.7 4.2 %collective-permute-done.6.came_ref = bf16[128,768]{1,0:T(8,128)(2,1)S(1)} collective-permute-done((bf16[128,768]{1,0:T(8,128)(2,1)S(1)}, bf16[128,768]{1,0:T(8,128)(2,1)S(1)}, u32[]{:S(2)}, u32[]{:S(2)}) %collective-permute-start.6) | collective-permute-done | bytes 196640 | tf_op jit(solution)/shard_map/ppermute | solution.py:363
  90.9 3.1 %collective-permute-start.15 = (bf16[768,640]{1,0:T(8,128)(2,1)}, bf16[768,640]{1,0:T(8,128)(2,1)S(1)}, u32[]{:S(2)}, u32[]{:S(2)}) collective-permute-start(bf16[768,640]{1,0:T(8,128)(2,1)} %collective-permute-done.14), channel_id=1, source_target_pairs={{4,0},{5,1},{6,2},{7,3},{20,16},{21,17},{22,18},{23,19}} | collective-permute-start | bytes 2949128 | tf_op jit(solution)/shard_map/ppermute | solution.py:334
  100.7 3.5 %collective-permute-start.9 = (bf16[128,768]{1,0:T(8,128)(2,1)S(1)}, bf16[128,768]{1,0:T(8,128)(2,1)S(1)}, u32[]{:S(2)}, u32[]{:S(2)}) collective-permute-start(bf16[128,768]{1,0:T(8,128)(2,1)S(1)} %collective-permute-done.6.came_ref), channel_id=1, source_target_pairs={{0,1},{1,0},{2,3},{3,2},{4,5},{5,4},{6,7},{7,6},{8,9},{9,8},{10,11... | collective-permute-start | bytes 589832 | tf_op jit(solution)/shard_map/ppermute | solution.py:372
  105.3 4.9 %project.5 = bf16[512,640]{1,0:T(8,128)(2,1)} custom-call(s32[3]{0:T(128)S(1)} %get-tuple-element.101.place_ref, bf16[896,768]{1,0:T(8,128)(2,1)S(1)} %get-tuple-element.83.keep_ref, bf16[128,768]{1,0:T(8,128)(2,1)S(1)} %collective-permute-done.6.came_ref, bf16[896,768]{1,0:T(8,128)(2,1)S(1)} %collective-permute-done.8.peer_keep_ref, ...), custom_call_target="tpu_custom_call" | custom-call | flops 1000 | bytes 1000 | tf_op jit(solution)/shard_map/project/pallas_call | solution.py:250
  110.2 3.0 %collective-permute-start.11 = (bf16[512,640]{1,0:T(8,128)(2,1)}, bf16[512,640]{1,0:T(8,128)(2,1)}, u32[]{:S(2)}, u32[]{:S(2)}) collective-permute-start(bf16[512,640]{1,0:T(8,128)(2,1)} %project.5), channel_id=1, source_target_pairs={{2,0},{4,6},{10,8},{12,14},{3,1},{5,7},{11,9},{13,15},{18,16},{20,... | collective-permute-start | bytes 1966088 | tf_op jit(solution)/shard_map/ppermute | solution.py:407
  113.3 4.1 %project.6 = bf16[512,640]{1,0:T(8,128)(2,1)} custom-call(s32[3]{0:T(128)S(1)} %get-tuple-element.100.place_ref, bf16[896,768]{1,0:T(8,128)(2,1)S(1)} %get-tuple-element.83.keep_ref, bf16[128,768]{1,0:T(8,128)(2,1)S(1)} %collective-permute-done.6.came_ref, bf16[896,768]{1,0:T(8,128)(2,1)S(1)} %collective-permute-done.8.peer_keep_ref, ...), custom_call_target="tpu_custom_call" | custom-call | flops 1000 | bytes 1000 | tf_op jit(solution)/shard_map/project/pallas_call | solution.py:250
  118.8 2.5 %select_select_fusion.refs_0_ = bf16[768,512]{1,0:T(8,128)(2,1)} fusion(bf16[768,640]{1,0:T(8,128)(2,1)} %collective-permute-done.3, bf16[768,640]{1,0:T(8,128)(2,1)S(1)} %collective-permute-done.15, bf16[768,640]{1,0:T(8,128)(2,1)} %collective-permute-done.2, bf16[768,640]{1,0:T(8,128)(2,1)S(1)} %collective-permute-done.16, pred[]{:T(512)S(6)} %eq.38, ...), kind=kLoop, calls=%fused_computation.10 | loop fusion | flops 1179648 | bytes 3932163 | tf_op jit(solution)/shard_map/jit(_where)/select_n | solution.py:280
  122.1 1.8 %select_select_fusion.1.refs_0_ = bf16[768,128]{1,0:T(8,128)(2,1)} fusion(bf16[768,640]{1,0:T(8,128)(2,1)} %collective-permute-done.3, bf16[768,640]{1,0:T(8,128)(2,1)S(1)} %collective-permute-done.15, bf16[768,640]{1,0:T(8,128)(2,1)} %collective-permute-done.2, bf16[768,640]{1,0:T(8,128)(2,1)S(1)} %collective-permute-done.16, pred[]{:T(512)S(6)} %eq.38, ...), kind=kLoop, calls=%fused_computation.35 | loop fusion | flops 294912 | bytes 983043 | tf_op jit(solution)/shard_map/jit(_where)/select_n | solution.py:280
  123.8 4.1 %project.7 = bf16[512,640]{1,0:T(8,128)(2,1)} custom-call(s32[3]{0:T(128)S(1)} %get-tuple-element.99.place_ref, bf16[896,768]{1,0:T(8,128)(2,1)S(1)} %get-tuple-element.83.keep_ref, bf16[128,768]{1,0:T(8,128)(2,1)S(1)} %collective-permute-done.6.came_ref, bf16[896,768]{1,0:T(8,128)(2,1)S(1)} %collective-permute-done.8.peer_keep_ref, ...), custom_call_target="tpu_custom_call" | custom-call | flops 1000 | bytes 1000 | tf_op jit(solution)/shard_map/project/pallas_call | solution.py:250
  127.9 5.5 %collective-permute-start.18 = (bf16[512,640]{1,0:T(8,128)(2,1)}, bf16[512,640]{1,0:T(8,128)(2,1)}, u32[]{:S(2)}, u32[]{:S(2)}) collective-permute-start(bf16[512,640]{1,0:T(8,128)(2,1)} %project.7), channel_id=1, source_target_pairs={{0,2},{4,6},{10,8},{14,12},{1,3},{5,7},{11,9},{15,13},{16,18},{20,... | collective-permute-start | bytes 1966088 | tf_op jit(solution)/shard_map/ppermute | solution.py:407
  133.4 3.4 %collective-permute-start.7 = (bf16[2,128,2560]{2,1,0:T(8,128)(2,1)}, bf16[2,128,2560]{2,1,0:T(8,128)(2,1)}, u32[]{:S(2)}, u32[]{:S(2)}) collective-permute-start(bf16[2,128,2560]{2,1,0:T(8,128)(2,1)} %param.9), channel_id=1, source_target_pairs={{1,0},{4,1},{5,4},{8,5},{9,8},{12,9},{13,12},{3,2},{6,3},{7,6},{10... | collective-permute-start | bytes 3932168 | tf_op jit(solution)/shard_map/ppermute | solution.py:377
  137.6 2.5 %collective-permute-done.20.refs_1_ = bf16[768,512]{1,0:T(8,128)(2,1)} collective-permute-done((bf16[768,512]{1,0:T(8,128)(2,1)}, bf16[768,512]{1,0:T(8,128)(2,1)}, u32[]{:S(2)}, u32[]{:S(2)}) %collective-permute-start.20) | collective-permute-done | bytes 786464 | tf_op jit(solution)/shard_map/ppermute | solution.py:343
  140.1 3.2 %project.8 = bf16[512,512]{1,0:T(8,128)(2,1)S(1)} custom-call(s32[3]{0:T(128)S(1)} %get-tuple-element.98.place_ref, bf16[896,768]{1,0:T(8,128)(2,1)S(1)} %get-tuple-element.83.keep_ref, bf16[128,768]{1,0:T(8,128)(2,1)S(1)} %collective-permute-done.6.came_ref, bf16[896,768]{1,0:T(8,128)(2,1)S(1)} %collective-permute-done.8.peer_keep_ref, ...), custom_call_target="tpu_custom_call" | custom-call | flops 1000 | bytes 1000 | tf_op jit(solution)/shard_map/project/pallas_call | solution.py:250
  145.6 2.9 %add_convert_fusion.1 = (bf16[512,640]{1,0:T(8,128)(2,1)S(1)}, bf16[512,640]{1,0:T(8,128)(2,1)S(1)}) fusion(bf16[512,640]{1,0:T(8,128)(2,1)} %collective-permute-done.11, bf16[512,640]{1,0:T(8,128)(2,1)} %project.5, bf16[512,640]{1,0:T(8,128)(2,1)} %collective-permute-done.12, bf16[512,640]{1,0:T(8,128)(2,1)} %project.6, ...), kind=kLoop, calls=%fused_computation.2 | loop fusion | flops 6881280 | bytes 5242886 | tf_op jit(solution)/shard_map/convert.3
  148.6 2.2 %collective-permute-start.19 = (bf16[256,1280]{1,0:T(8,128)(2,1)S(1)}, bf16[256,1280]{1,0:T(8,128)(2,1)S(1)}, u32[]{:S(2)}, u32[]{:S(2)}) collective-permute-start(bf16[256,1280]{1,0:T(8,128)(2,1)S(1)} %pad_maximum_fusion), channel_id=1, source_target_pairs={{0,1},{1,0},{2,3},{3,2},{4,5},{5,4},{6,7},{7,6},{8,9},{9,8},{10,11... | collective-permute-start | bytes 1966088 | tf_op jit(solution)/shard_map/ppermute | solution.py:439
  153.8 2.1 %collective-permute-done.21 = bf16[512,512]{1,0:T(8,128)(2,1)S(1)} collective-permute-done((bf16[512,512]{1,0:T(8,128)(2,1)S(1)}, bf16[512,512]{1,0:T(8,128)(2,1)S(1)}, u32[]{:S(2)}, u32[]{:S(2)}) %collective-permute-start.21) | collective-permute-done | bytes 524320 | tf_op jit(solution)/shard_map/ppermute | solution.py:407
  156.1 5.4 %collective-permute-start.22 = (bf16[256,512]{1,0:T(8,128)(2,1)S(1)}, bf16[256,512]{1,0:T(8,128)(2,1)S(1)}, u32[]{:S(2)}, u32[]{:S(2)}) collective-permute-start(bf16[256,512]{1,0:T(8,128)(2,1)S(1)} %slice.146), channel_id=1, source_target_pairs={{0,1},{1,0},{2,3},{3,2},{4,5},{5,4},{6,7},{7,6},{8,9},{9,8},{10,11... | collective-permute-start | bytes 786440 | tf_op jit(solution)/shard_map/ppermute | solution.py:443
  (92 shorter events, 34.7 us)
Async XLA Ops:
  0.0 95.9 %copy-start = (bf16[50,2560]{1,0:T(8,128)(2,1)S(1)}, bf16[50,2560]{1,0:T(8,128)(2,1)}, u32[]{:S(2)}) copy-start(bf16[50,2560]{1,0:T(8,128)(2,1)} %param.13) | copy-start | bytes 768004
  0.0 8.3 %copy-start.14 = (s32[2]{0:T(128)S(1)}, s32[2]{0:T(128)}, u32[]{:S(2)}) copy-start(s32[2]{0:T(128)} %param.11) | copy-start | bytes 28
  0.0 8.3 %copy-start.13 = (s32[2]{0:T(128)S(1)}, s32[2]{0:T(128)}, u32[]{:S(2)}) copy-start(s32[2]{0:T(128)} %param.17) | copy-start | bytes 28
  1.4 24.6 %collective-permute-start.2 = (bf16[768,640]{1,0:T(8,128)(2,1)S(1)}, bf16[768,640]{1,0:T(8,128)(2,1)}, u32[]{:S(2)}, u32[]{:S(2)}) collective-permute-start(bf16[768,640]{1,0:T(8,128)(2,1)S(1)} %dynamic_slice.3), channel_id=1, source_target_pairs={{0,4},{4,8},{8,12},{1,5},{5,9},{9,13},{2,6},{6,10},{10,14},{3,7},{... | collective-permute-start | bytes 2949128 | tf_op jit(solution)/shard_map/ppermute | solution.py:334
  4.6 24.3 %collective-permute-start.3 = (bf16[768,640]{1,0:T(8,128)(2,1)S(1)}, bf16[768,640]{1,0:T(8,128)(2,1)}, u32[]{:S(2)}, u32[]{:S(2)}) collective-permute-start(bf16[768,640]{1,0:T(8,128)(2,1)S(1)} %dynamic_slice.3), channel_id=1, source_target_pairs={{12,8},{8,4},{4,0},{13,9},{9,5},{5,1},{14,10},{10,6},{6,2},{15,11}... | collective-permute-start | bytes 2949128 | tf_op jit(solution)/shard_map/ppermute | solution.py:334
  13.8 3.8 %collective-permute-start = (bf16[2,2,128,768]{3,2,1,0:T(8,128)(2,1)S(1)}, bf16[2,2,128,768]{3,2,1,0:T(8,128)(2,1)S(1)}, u32[]{:S(2)}, u32[]{:S(2)}) collective-permute-start(bf16[2,2,128,768]{3,2,1,0:T(8,128)(2,1)S(1)} %get-tuple-element.48), channel_id=1, source_target_pairs={{0,1},{1,0},{2,3},{3,2},{4,5},{5,4},{6,7},{7,6},{8,9},{9,8},{10,11... | collective-permute-start | bytes 2359304 | tf_op jit(solution)/shard_map/ppermute | solution.py:352
  15.1 2.5 %collective-permute-start.1 = (bf16[2,128,768]{2,1,0:T(8,128)(2,1)S(1)}, bf16[2,128,768]{2,1,0:T(8,128)(2,1)S(1)}, u32[]{:S(2)}, u32[]{:S(2)}) collective-permute-start(bf16[2,128,768]{2,1,0:T(8,128)(2,1)S(1)} %get-tuple-element.49), channel_id=1, source_target_pairs={{0,1},{1,0},{2,3},{3,2},{4,5},{5,4},{6,7},{7,6},{8,9},{9,8},{10,11... | collective-permute-start | bytes 1179656 | tf_op jit(solution)/shard_map/ppermute | solution.py:352
  28.9 36.7 %collective-permute-start.4 = (bf16[1040,768]{1,0:T(8,128)(2,1)}, bf16[1040,768]{1,0:T(8,128)(2,1)}, u32[]{:S(2)}, u32[]{:S(2)}) collective-permute-start(bf16[1040,768]{1,0:T(8,128)(2,1)} %bundle.1), channel_id=1, source_target_pairs={{4,0},{8,4},{12,8},{5,1},{9,5},{13,9},{6,2},{10,6},{14,10},{7,3},{... | collective-permute-start | bytes 4792328 | tf_op jit(solution)/shard_map/ppermute | solution.py:354
  33.2 21.3 %collective-permute-start.5 = (bf16[768,640]{1,0:T(8,128)(2,1)S(1)}, bf16[768,640]{1,0:T(8,128)(2,1)}, u32[]{:S(2)}, u32[]{:S(2)}) collective-permute-start(bf16[768,640]{1,0:T(8,128)(2,1)S(1)} %broadcast_select_fusion.2.refs_0_), channel_id=1, source_target_pairs={{0,16},{16,0},{1,17},{17,1},{2,18},{18,2},{3,19},{19,3},{4,20},{20... | collective-permute-start | bytes 2949128 | tf_op jit(solution)/shard_map/ppermute | solution.py:343
  35.5 49.5 %collective-permute-start.13 = (bf16[768,640]{1,0:T(8,128)(2,1)}, bf16[768,640]{1,0:T(8,128)(2,1)}, u32[]{:S(2)}, u32[]{:S(2)}) collective-permute-start(bf16[768,640]{1,0:T(8,128)(2,1)} %collective-permute-done.2), channel_id=1, source_target_pairs={{4,8},{8,12},{5,9},{9,13},{6,10},{10,14},{7,11},{11,15},{20,24},{2... | collective-permute-start | bytes 2949128 | tf_op jit(solution)/shard_map/ppermute | solution.py:334
  38.8 47.9 %collective-permute-start.14 = (bf16[768,640]{1,0:T(8,128)(2,1)}, bf16[768,640]{1,0:T(8,128)(2,1)}, u32[]{:S(2)}, u32[]{:S(2)}) collective-permute-start(bf16[768,640]{1,0:T(8,128)(2,1)} %collective-permute-done.3), channel_id=1, source_target_pairs={{8,4},{4,0},{9,5},{5,1},{10,6},{6,2},{11,7},{7,3},{24,20},{20,16},... | collective-permute-start | bytes 2949128 | tf_op jit(solution)/shard_map/ppermute | solution.py:334
  76.4 14.5 %collective-permute-start.6 = (bf16[128,768]{1,0:T(8,128)(2,1)S(1)}, bf16[128,768]{1,0:T(8,128)(2,1)S(1)}, u32[]{:S(2)}, u32[]{:S(2)}) collective-permute-start(bf16[128,768]{1,0:T(8,128)(2,1)S(1)} %get-tuple-element.57), channel_id=1, source_target_pairs={{4,0},{8,4},{12,8},{5,1},{9,5},{13,9},{6,2},{10,6},{14,10},{7,3},{... | collective-permute-start | bytes 589832 | tf_op jit(solution)/shard_map/ppermute | solution.py:363
  79.5 25.8 %collective-permute-start.8 = (bf16[896,768]{1,0:T(8,128)(2,1)S(1)}, bf16[896,768]{1,0:T(8,128)(2,1)S(1)}, u32[]{:S(2)}, u32[]{:S(2)}) collective-permute-start(bf16[896,768]{1,0:T(8,128)(2,1)S(1)} %get-tuple-element.83.keep_ref), channel_id=1, source_target_pairs={{0,1},{1,0},{2,3},{3,2},{4,5},{5,4},{6,7},{7,6},{8,9},{9,8},{10,11... | collective-permute-start | bytes 4128776 | tf_op jit(solution)/shard_map/ppermute | solution.py:372
  90.9 27.9 %collective-permute-start.15 = (bf16[768,640]{1,0:T(8,128)(2,1)}, bf16[768,640]{1,0:T(8,128)(2,1)S(1)}, u32[]{:S(2)}, u32[]{:S(2)}) collective-permute-start(bf16[768,640]{1,0:T(8,128)(2,1)} %collective-permute-done.14), channel_id=1, source_target_pairs={{4,0},{5,1},{6,2},{7,3},{20,16},{21,17},{22,18},{23,19}} | collective-permute-start | bytes 2949128 | tf_op jit(solution)/shard_map/ppermute | solution.py:334
  96.1 9.2 %copy-start.3 = (bf16[768,640]{1,0:T(8,128)(2,1)S(1)}, bf16[768,640]{1,0:T(8,128)(2,1)}, u32[]{:S(2)}) copy-start(bf16[768,640]{1,0:T(8,128)(2,1)} %copy-done.2) | copy-start | bytes 2949124
  96.1 4.6 %collective-permute-start.10 = (bf16[2,2560]{1,0:T(2,128)(2,1)S(1)}, bf16[2,2560]{1,0:T(2,128)(2,1)S(1)}, u32[]{:S(2)}, u32[]{:S(2)}) collective-permute-start(bf16[2,2560]{1,0:T(2,128)(2,1)S(1)} %convolution_convert_fusion), channel_id=1, source_target_pairs={{0,2},{2,0},{1,3},{3,1},{4,6},{6,4},{5,7},{7,5},{8,10},{10,8},{9,1... | collective-permute-start | bytes 30728 | tf_op jit(solution)/shard_map/ppermute | solution.py:385
  98.7 20.1 %collective-permute-start.16 = (bf16[768,640]{1,0:T(8,128)(2,1)}, bf16[768,640]{1,0:T(8,128)(2,1)S(1)}, u32[]{:S(2)}, u32[]{:S(2)}) collective-permute-start(bf16[768,640]{1,0:T(8,128)(2,1)} %collective-permute-done.13), channel_id=1, source_target_pairs={{8,12},{9,13},{10,14},{11,15},{24,28},{25,29},{26,30},{27,31}} | collective-permute-start | bytes 2949128 | tf_op jit(solution)/shard_map/ppermute | solution.py:334
  99.4 24.4 %collective-permute-start.17 = (bf16[768,640]{1,0:T(8,128)(2,1)S(1)}, bf16[768,640]{1,0:T(8,128)(2,1)S(1)}, u32[]{:S(2)}, u32[]{:S(2)}) collective-permute-start(bf16[768,640]{1,0:T(8,128)(2,1)S(1)} %broadcast_select_fusion.1.refs_0_), channel_id=1, source_target_pairs={{0,16},{16,0},{1,17},{17,1},{2,18},{18,2},{3,19},{19,3},{4,20},{20... | collective-permute-start | bytes 2949128 | tf_op jit(solution)/shard_map/ppermute | solution.py:343
  100.7 4.6 %collective-permute-start.9 = (bf16[128,768]{1,0:T(8,128)(2,1)S(1)}, bf16[128,768]{1,0:T(8,128)(2,1)S(1)}, u32[]{:S(2)}, u32[]{:S(2)}) collective-permute-start(bf16[128,768]{1,0:T(8,128)(2,1)S(1)} %collective-permute-done.6.came_ref), channel_id=1, source_target_pairs={{0,1},{1,0},{2,3},{3,2},{4,5},{5,4},{6,7},{7,6},{8,9},{9,8},{10,11... | collective-permute-start | bytes 589832 | tf_op jit(solution)/shard_map/ppermute | solution.py:372
  105.3 8.0 %copy-start.1 = (bf16[1536,1280]{1,0:T(8,128)(2,1)S(1)}, bf16[1536,1280]{1,0:T(8,128)(2,1)}, u32[]{:S(2)}) copy-start(bf16[1536,1280]{1,0:T(8,128)(2,1)} %refs_0_.1) | copy-start | bytes 11796484
  110.2 27.3 %collective-permute-start.11 = (bf16[512,640]{1,0:T(8,128)(2,1)}, bf16[512,640]{1,0:T(8,128)(2,1)}, u32[]{:S(2)}, u32[]{:S(2)}) collective-permute-start(bf16[512,640]{1,0:T(8,128)(2,1)} %project.5), channel_id=1, source_target_pairs={{2,0},{4,6},{10,8},{12,14},{3,1},{5,7},{11,9},{13,15},{18,16},{20,... | collective-permute-start | bytes 1966088 | tf_op jit(solution)/shard_map/ppermute | solution.py:407
  117.4 19.4 %collective-permute-start.12 = (bf16[512,640]{1,0:T(8,128)(2,1)}, bf16[512,640]{1,0:T(8,128)(2,1)}, u32[]{:S(2)}, u32[]{:S(2)}) collective-permute-start(bf16[512,640]{1,0:T(8,128)(2,1)} %project.6), channel_id=1, source_target_pairs={{2,0},{6,4},{8,10},{12,14},{3,1},{7,5},{9,11},{13,15},{18,16},{22,... | collective-permute-start | bytes 1966088 | tf_op jit(solution)/shard_map/ppermute | solution.py:407
  121.3 18.8 %collective-permute-start.20 = (bf16[768,512]{1,0:T(8,128)(2,1)}, bf16[768,512]{1,0:T(8,128)(2,1)}, u32[]{:S(2)}, u32[]{:S(2)}) collective-permute-start(bf16[768,512]{1,0:T(8,128)(2,1)} %select_select_fusion.refs_0_), channel_id=1, source_target_pairs={{0,16},{16,0},{1,17},{17,1},{2,18},{18,2},{3,19},{19,3},{4,20},{20... | collective-permute-start | bytes 2359304 | tf_op jit(solution)/shard_map/ppermute | solution.py:343
  127.9 17.7 %collective-permute-start.18 = (bf16[512,640]{1,0:T(8,128)(2,1)}, bf16[512,640]{1,0:T(8,128)(2,1)}, u32[]{:S(2)}, u32[]{:S(2)}) collective-permute-start(bf16[512,640]{1,0:T(8,128)(2,1)} %project.7), channel_id=1, source_target_pairs={{0,2},{4,6},{10,8},{14,12},{1,3},{5,7},{11,9},{15,13},{16,18},{20,... | collective-permute-start | bytes 1966088 | tf_op jit(solution)/shard_map/ppermute | solution.py:407
  133.4 28.1 %collective-permute-start.7 = (bf16[2,128,2560]{2,1,0:T(8,128)(2,1)}, bf16[2,128,2560]{2,1,0:T(8,128)(2,1)}, u32[]{:S(2)}, u32[]{:S(2)}) collective-permute-start(bf16[2,128,2560]{2,1,0:T(8,128)(2,1)} %param.9), channel_id=1, source_target_pairs={{1,0},{4,1},{5,4},{8,5},{9,8},{12,9},{13,12},{3,2},{6,3},{7,6},{10... | collective-permute-start | bytes 3932168 | tf_op jit(solution)/shard_map/ppermute | solution.py:377
  136.8 14.0 %collective-permute-start.23 = (bf16[768,128]{1,0:T(8,128)(2,1)}, bf16[768,128]{1,0:T(8,128)(2,1)S(1)}, u32[]{:S(2)}, u32[]{:S(2)}) collective-permute-start(bf16[768,128]{1,0:T(8,128)(2,1)} %select_select_fusion.1.refs_0_), channel_id=1, source_target_pairs={{0,16},{16,0},{1,17},{17,1},{2,18},{18,2},{3,19},{19,3},{4,20},{20... | collective-permute-start | bytes 589832 | tf_op jit(solution)/shard_map/ppermute | solution.py:343
  143.3 12.6 %collective-permute-start.21 = (bf16[512,512]{1,0:T(8,128)(2,1)S(1)}, bf16[512,512]{1,0:T(8,128)(2,1)S(1)}, u32[]{:S(2)}, u32[]{:S(2)}) collective-permute-start(bf16[512,512]{1,0:T(8,128)(2,1)S(1)} %project.8), channel_id=1, source_target_pairs={{0,2},{6,4},{8,10},{14,12},{1,3},{7,5},{9,11},{15,13},{16,18},{22,... | collective-permute-start | bytes 1572872 | tf_op jit(solution)/shard_map/ppermute | solution.py:407
  148.6 14.5 %collective-permute-start.19 = (bf16[256,1280]{1,0:T(8,128)(2,1)S(1)}, bf16[256,1280]{1,0:T(8,128)(2,1)S(1)}, u32[]{:S(2)}, u32[]{:S(2)}) collective-permute-start(bf16[256,1280]{1,0:T(8,128)(2,1)S(1)} %pad_maximum_fusion), channel_id=1, source_target_pairs={{0,1},{1,0},{2,3},{3,2},{4,5},{5,4},{6,7},{7,6},{8,9},{9,8},{10,11... | collective-permute-start | bytes 1966088 | tf_op jit(solution)/shard_map/ppermute | solution.py:439
  152.3 9.1 %copy-start.11 = (bf16[2,128,2560]{2,1,0:T(8,128)(2,1)S(1)}, bf16[2,128,2560]{2,1,0:T(8,128)(2,1)}, u32[]{:S(2)}) copy-start(bf16[2,128,2560]{2,1,0:T(8,128)(2,1)} %param.15) | copy-start | bytes 3932164
  152.4 10.6 %collective-permute-start.24 = (bf16[512,128]{1,0:T(8,128)(2,1)S(1)}, bf16[512,128]{1,0:T(8,128)(2,1)S(1)}, u32[]{:S(2)}, u32[]{:S(2)}) collective-permute-start(bf16[512,128]{1,0:T(8,128)(2,1)S(1)} %project.9), channel_id=1, source_target_pairs={{0,2},{6,4},{8,10},{14,12},{1,3},{7,5},{9,11},{15,13},{16,18},{22,... | collective-permute-start | bytes 393224 | tf_op jit(solution)/shard_map/ppermute | solution.py:407
  156.1 7.0 %collective-permute-start.22 = (bf16[256,512]{1,0:T(8,128)(2,1)S(1)}, bf16[256,512]{1,0:T(8,128)(2,1)S(1)}, u32[]{:S(2)}, u32[]{:S(2)}) collective-permute-start(bf16[256,512]{1,0:T(8,128)(2,1)S(1)} %slice.146), channel_id=1, source_target_pairs={{0,1},{1,0},{2,3},{3,2},{4,5},{5,4},{6,7},{7,6},{8,9},{9,8},{10,11... | collective-permute-start | bytes 786440 | tf_op jit(solution)/shard_map/ppermute | solution.py:443
  163.0 1.3 collective-permute-start.25
  (9 other events, 17.6 us)

commit v5 on v4

--- a/solution.py
+++ b/solution.py
@@ -110,7 +110,7 @@
     )(where, mine, got, got_v)
 
 
-def attend_kernel(where_ref, mine, got, got_v, fresh, far_ref, send_ref, keep_ref):
+def attend_kernel(where_ref, mine, got, got_v, fresh, far_ref, gate_ref, send_ref, keep_ref, row_ref):
     theirs = got.at[0], got.at[1], got_v
     tokens = mine.shape[2]
     heads = mine.shape[-1] // HD
@@ -159,6 +159,12 @@
         keep_ref[: 3 * tokens, at] = early[tokens:]
         keep_ref[3 * tokens :, at] = mix(queries[2:6], 1)
 
+    level = far_ref[8 * tokens : 8 * tokens + SPARE, :HD].astype(F32)[0:1]
+    for at in range(0, gate_ref.shape[1], HD):
+        rows = gate_ref[:, at : at + HD]
+        chosen = lax.broadcasted_iota(jnp.int32, rows.shape, 0).astype(F32) == level
+        row_ref[:, at : at + HD] = jnp.sum(jnp.where(chosen, rows, 0.0), axis=0, keepdims=True)
+
     group = 3 if heads % 3 == 0 else 1
 
     @pl.loop(0, heads // group)
@@ -172,10 +178,11 @@
     return pl.pallas_call(
         attend_kernel,
         in_specs=[pl.BlockSpec(memory_space=pltpu.SMEM)] + [pl.BlockSpec(memory_space=pltpu.VMEM)] * len(operands),
-        out_specs=[pl.BlockSpec(memory_space=pltpu.VMEM)] * 2,
+        out_specs=[pl.BlockSpec(memory_space=pltpu.VMEM)] * 3,
         out_shape=[
             jax.ShapeDtypeStruct((tokens, share), BF16),
             jax.ShapeDtypeStruct((7 * tokens, share), BF16),
+            jax.ShapeDtypeStruct((1, operands[-1].shape[1]), F32),
         ],
         compiler_params=params(),
         cost_estimate=COST,
@@ -359,9 +366,9 @@
 
     inputs = after((mine, got, got_v, fresh, far), gathered[1, 0][1])
 
-    send, keep = attend(where, *inputs)
+    table_of_gates = jnp.pad(gates.astype(F32), ((0, -gates.shape[0] % 8), (0, 0)))
+    send, keep, next_row = attend(where, *inputs, table_of_gates)
     came = lax.ppermute(send, "queue", back)
-    next_level = after(far, came)[8 * tokens, :1].astype(jnp.int32)
     if count > 2:
         held["up", 2, 0], held["down", 2, 0] = after((held["up", 2, 0], held["down", 2, 0]), came)
     for hop in range(3, count):
@@ -378,17 +385,16 @@
     moved = jnp.where(jnp.logical_and(last, core == 1), incoming_latent, moved)
     moved = moved.reshape(frames * tokens, features)
 
-    chosen = jnp.concatenate([levels, next_level])
-    one_hot = (jnp.arange(gates.shape[0], dtype=jnp.int32)[None, :] == chosen[:, None]).astype(BF16)
-    rows = jnp.dot(one_hot, gates, preferred_element_type=F32).astype(BF16)
-    if sides == 2:
-        other = lax.ppermute(rows, "heads", swap)
-        rows = jnp.concatenate(
-            [jnp.where(side == 0, rows, other), jnp.where(side == 0, other, rows)], axis=1
-        )
-    else:
-        rows = lax.all_gather(rows, "heads", axis=1, tiled=True)
-    rows = rows.astype(F32)
+    one_hot = (jnp.arange(gates.shape[0], dtype=jnp.int32) == levels[0]).astype(BF16)[None, :]
+    own_row = jnp.dot(one_hot, gates, preferred_element_type=F32)
+
+    def both_sides(row):
+        if sides != 2:
+            return lax.all_gather(row, "heads", axis=1, tiled=True)
+        other = lax.ppermute(row, "heads", swap)
+        return jnp.concatenate([jnp.where(side == 0, row, other), jnp.where(side == 0, other, row)], axis=1)
+
+    rows = jnp.concatenate([both_sides(own_row), both_sides(next_row)], axis=0)
     crossing = jnp.where(last, 0.0, rows[1:2])
     gate_rows = jnp.concatenate([rows[:1], crossing], axis=0)
 

time: 167 us -> 164 us (0.982)
  waiting for transfers between devices: 50.1 us -> 47.1 us
  starting transfers between devices: 60.7 us -> 63 us
    select_n x4, other arithmetic: 6.87 us -> 5.02 us  [pick(): jnp.where(here, held(source), value)]
  transfers between devices with their start and end apart: 26 -> 27, of which waited for: 12 -> 11; matrix products, arithmetic and copies ran while one was open for 8% -> 7% of each run, Pallas kernels for 18% -> 18%
where the time goes in v5:
time: 164 us; the launch traced here: 163 us
  starting transfers between devices  63 us (38%)
  waiting for transfers between devices  47.1 us (29%)
  Pallas kernels  29.9 us (18%)
  other arithmetic  12.2 us (7%)
  local copies, waits for them, and re-layouts  10.1 us (6%)
    pallas_call x5, Pallas kernels, project(): pl.pallas_call(functools.partial(project_kernel, half), in_specs=[pl.Bloc...  17.7 us
    ppermute x4, waiting for transfers between devices, spread(): gathered[k, low] = (own, lax.ppermute(own, 'groups', swap))  16.2 us
    ppermute x6, starting transfers between devices, send_weights(): held[way, name, low] = lax.ppermute(part, 'queue', pairs)  14.2 us
    ppermute x5, starting transfers between devices, summed(): return (block, delta, lax.ppermute(delta, flat, pairs))  13.6 us
    ppermute x1, waiting for transfers between devices, local(): lax.ppermute(after(bundle(where, mine, got, got_v), *hop_1), 'queue', back)  11.1 us
    ppermute x6, waiting for transfers between devices, send_weights(): held[way, name, low] = lax.ppermute(part, 'queue', pairs)  9.64 us
    pallas_call x1, Pallas kernels, attend(): pl.pallas_call(attend_kernel, in_specs=[pl.BlockSpec(memory_space=pltpu.S...  8.51 us
    unnamed x30, local copies, waits for them, and re-layouts  7.75 us
  transfers between devices with their start and end apart: 27, of which 11 were waited for; matrix products, arithmetic and copies ran while one was open for 7% of the time, Pallas kernels for 18%

profile of v5, /device:TPU:9, one launch (start us, length us, event | category | flops | bytes accessed | tf_op | source)
XLA Modules:
  0.0 163.5 jit_solution(17166782091836372626)
XLA Ops:
  0.0 2.3 %dynamic_slice.3 = bf16[768,640]{1,0:T(8,128)(2,1)} dynamic-slice(bf16[1536,1280]{1,0:T(8,128)(2,1)} %refs_0_.1, s32[]{:T(128)S(6)} %select_n.298, s32[]{:T(128)S(6)} %select_n.299), dynamic_slice_sizes={768,640} | dynamic-slice | bytes 1966084 | tf_op jit(solution)/shard_map/dynamic_slice | solution.py:332
  2.3 3.2 %collective-permute-start.2 = (bf16[768,640]{1,0:T(8,128)(2,1)}, bf16[768,640]{1,0:T(8,128)(2,1)}, u32[]{:S(2)}, u32[]{:S(2)}) collective-permute-start(bf16[768,640]{1,0:T(8,128)(2,1)} %dynamic_slice.3), channel_id=1, source_target_pairs={{0,4},{4,8},{8,12},{1,5},{5,9},{9,13},{2,6},{6,10},{10,14},{3,7},{... | collective-permute-start | bytes 2949128 | tf_op jit(solution)/shard_map/ppermute | solution.py:341
  5.5 3.0 %collective-permute-start.3 = (bf16[768,640]{1,0:T(8,128)(2,1)}, bf16[768,640]{1,0:T(8,128)(2,1)}, u32[]{:S(2)}, u32[]{:S(2)}) collective-permute-start(bf16[768,640]{1,0:T(8,128)(2,1)} %dynamic_slice.3), channel_id=1, source_target_pairs={{12,8},{8,4},{4,0},{13,9},{9,5},{5,1},{14,10},{10,6},{6,2},{15,11}... | collective-permute-start | bytes 2949128 | tf_op jit(solution)/shard_map/ppermute | solution.py:341
  12.9 1.8 %rotate.1 = (bf16[3,2,128,768]{3,2,1,0:T(8,128)(2,1)S(1)}, bf16[2,2,128,768]{3,2,1,0:T(8,128)(2,1)S(1)}, bf16[2,128,768]{2,1,0:T(8,128)(2,1)S(1)}, bf16[3,2,128,768]{3,2,1,0:T(8,128)(2,1)S(1)}) custom-call(s32[4]{0:T(128)S(1)} %pad_add_fusion.core_ref.where_ref, f32[4,128]{1,0:T(4,128)S(1)} %get-tuple-element.102.cos_ref, ...), custom_call_target="tpu_custom_call" | custom-call | flops 1000 | bytes 1000 | tf_op jit(solution)/shard_map/rotate/pallas_call | solution.py:69
  16.1 2.4 %collective-permute-done.1.got_v = bf16[2,128,768]{2,1,0:T(8,128)(2,1)S(1)} collective-permute-done((bf16[2,128,768]{2,1,0:T(8,128)(2,1)S(1)}, bf16[2,128,768]{2,1,0:T(8,128)(2,1)S(1)}, u32[]{:S(2)}, u32[]{:S(2)}) %collective-permute-start.1) | collective-permute-done | bytes 393248 | tf_op jit(solution)/shard_map/ppermute | solution.py:359
  18.5 1.9 %bundle.1 = bf16[1040,768]{1,0:T(8,128)(2,1)} custom-call(s32[4]{0:T(128)S(1)} %pad_add_fusion.core_ref.where_ref, bf16[3,2,128,768]{3,2,1,0:T(8,128)(2,1)S(1)} %get-tuple-element.52.mine, bf16[2,2,128,768]{3,2,1,0:T(8,128)(2,1)S(1)} %collective-permute-done.got, bf16[2,128,768]{2,1,0:T(8,128)(2,1)S(1)} %collective-permute-done.1.got_v), custom_call_target="tpu_custom_call" | custom-call | flops 1000 | bytes 1000 | tf_op jit(solution)/shard_map/bundle/pallas_call | solution.py:102
  20.4 6.7 %collective-permute-done.2 = bf16[768,640]{1,0:T(8,128)(2,1)} collective-permute-done((bf16[768,640]{1,0:T(8,128)(2,1)}, bf16[768,640]{1,0:T(8,128)(2,1)}, u32[]{:S(2)}, u32[]{:S(2)}) %collective-permute-start.2) | collective-permute-done | bytes 983072 | tf_op jit(solution)/shard_map/ppermute | solution.py:341
  27.1 2.9 %collective-permute-done.3 = bf16[768,640]{1,0:T(8,128)(2,1)} collective-permute-done((bf16[768,640]{1,0:T(8,128)(2,1)}, bf16[768,640]{1,0:T(8,128)(2,1)}, u32[]{:S(2)}, u32[]{:S(2)}) %collective-permute-start.3) | collective-permute-done | bytes 983072 | tf_op jit(solution)/shard_map/ppermute | solution.py:341
  30.0 3.0 %collective-permute-start.4 = (bf16[1040,768]{1,0:T(8,128)(2,1)}, bf16[1040,768]{1,0:T(8,128)(2,1)}, u32[]{:S(2)}, u32[]{:S(2)}) collective-permute-start(bf16[1040,768]{1,0:T(8,128)(2,1)} %bundle.1), channel_id=1, source_target_pairs={{4,0},{8,4},{12,8},{5,1},{9,5},{13,9},{6,2},{10,6},{14,10},{7,3},{... | collective-permute-start | bytes 4792328 | tf_op jit(solution)/shard_map/ppermute | solution.py:361
  38.2 2.3 %collective-permute-start.14 = (bf16[768,640]{1,0:T(8,128)(2,1)}, bf16[768,640]{1,0:T(8,128)(2,1)S(1)}, u32[]{:S(2)}, u32[]{:S(2)}) collective-permute-start(bf16[768,640]{1,0:T(8,128)(2,1)} %collective-permute-done.2), channel_id=1, source_target_pairs={{4,8},{8,12},{5,9},{9,13},{6,10},{10,14},{7,11},{11,15},{20,24},{2... | collective-permute-start | bytes 2949128 | tf_op jit(solution)/shard_map/ppermute | solution.py:341
  40.5 1.9 %collective-permute-start.15 = (bf16[768,640]{1,0:T(8,128)(2,1)}, bf16[768,640]{1,0:T(8,128)(2,1)S(1)}, u32[]{:S(2)}, u32[]{:S(2)}) collective-permute-start(bf16[768,640]{1,0:T(8,128)(2,1)} %collective-permute-done.3), channel_id=1, source_target_pairs={{8,4},{4,0},{9,5},{5,1},{10,6},{6,2},{11,7},{7,3},{24,20},{20,16},... | collective-permute-start | bytes 2949128 | tf_op jit(solution)/shard_map/ppermute | solution.py:341
  42.4 13.3 %collective-permute-done.5.refs_1_ = bf16[768,640]{1,0:T(8,128)(2,1)} collective-permute-done((bf16[768,640]{1,0:T(8,128)(2,1)S(1)}, bf16[768,640]{1,0:T(8,128)(2,1)}, u32[]{:S(2)}, u32[]{:S(2)}) %collective-permute-start.5) | collective-permute-done | bytes 983072 | tf_op jit(solution)/shard_map/ppermute | solution.py:350
  55.7 11.1 %collective-permute-done.4.far_ref = bf16[1040,768]{1,0:T(8,128)(2,1)} collective-permute-done((bf16[1040,768]{1,0:T(8,128)(2,1)}, bf16[1040,768]{1,0:T(8,128)(2,1)}, u32[]{:S(2)}, u32[]{:S(2)}) %collective-permute-start.4) | collective-permute-done | bytes 1597472 | tf_op jit(solution)/shard_map/ppermute | solution.py:361
  70.1 8.5 %attend.1 = (bf16[128,768]{1,0:T(8,128)(2,1)S(1)}, bf16[896,768]{1,0:T(8,128)(2,1)S(1)}, f32[1,2560]{1,0:T(1,128)S(1)}) custom-call(s32[4]{0:T(128)S(1)} %pad_add_fusion.core_ref.where_ref, bf16[3,2,128,768]{3,2,1,0:T(8,128)(2,1)S(1)} %get-tuple-element.52.mine, bf16[2,2,128,768]{3,2,1,0:T(8,128)(2,1)S(1)} %collective-permute-done.got, ...), custom_call_target="tpu_custom_call" | custom-call | flops 1000 | bytes 1000 | tf_op jit(solution)/shard_map/attend/pallas_call | solution.py:178
  79.9 3.0 %collective-permute-start.6 = (bf16[128,768]{1,0:T(8,128)(2,1)S(1)}, bf16[128,768]{1,0:T(8,128)(2,1)S(1)}, u32[]{:S(2)}, u32[]{:S(2)}) collective-permute-start(bf16[128,768]{1,0:T(8,128)(2,1)S(1)} %get-tuple-element.57), channel_id=1, source_target_pairs={{4,0},{8,4},{12,8},{5,1},{9,5},{13,9},{6,2},{10,6},{14,10},{7,3},{... | collective-permute-start | bytes 589832 | tf_op jit(solution)/shard_map/ppermute | solution.py:371
  82.9 5.8 %collective-permute-start.8 = (bf16[896,768]{1,0:T(8,128)(2,1)S(1)}, bf16[896,768]{1,0:T(8,128)(2,1)S(1)}, u32[]{:S(2)}, u32[]{:S(2)}) collective-permute-start(bf16[896,768]{1,0:T(8,128)(2,1)S(1)} %get-tuple-element.83.keep_ref), channel_id=1, source_target_pairs={{0,1},{1,0},{2,3},{3,2},{4,5},{5,4},{6,7},{7,6},{8,9},{9,8},{10,11... | collective-permute-start | bytes 4128776 | tf_op jit(solution)/shard_map/ppermute | solution.py:379
  88.8 3.2 %collective-permute-done.6.came_ref = bf16[128,768]{1,0:T(8,128)(2,1)S(1)} collective-permute-done((bf16[128,768]{1,0:T(8,128)(2,1)S(1)}, bf16[128,768]{1,0:T(8,128)(2,1)S(1)}, u32[]{:S(2)}, u32[]{:S(2)}) %collective-permute-start.6) | collective-permute-done | bytes 196640 | tf_op jit(solution)/shard_map/ppermute | solution.py:371
  92.0 3.1 %collective-permute-start.16 = (bf16[768,640]{1,0:T(8,128)(2,1)S(1)}, bf16[768,640]{1,0:T(8,128)(2,1)S(1)}, u32[]{:S(2)}, u32[]{:S(2)}) collective-permute-start(bf16[768,640]{1,0:T(8,128)(2,1)S(1)} %collective-permute-done.15), channel_id=1, source_target_pairs={{4,0},{5,1},{6,2},{7,3},{20,16},{21,17},{22,18},{23,19}} | collective-permute-start | bytes 2949128 | tf_op jit(solution)/shard_map/ppermute | solution.py:341
  97.2 3.3 %collective-permute-start.9 = (bf16[128,768]{1,0:T(8,128)(2,1)S(1)}, bf16[128,768]{1,0:T(8,128)(2,1)S(1)}, u32[]{:S(2)}, u32[]{:S(2)}) collective-permute-start(bf16[128,768]{1,0:T(8,128)(2,1)S(1)} %collective-permute-done.6.came_ref), channel_id=1, source_target_pairs={{0,1},{1,0},{2,3},{3,2},{4,5},{5,4},{6,7},{7,6},{8,9},{9,8},{10,11... | collective-permute-start | bytes 589832 | tf_op jit(solution)/shard_map/ppermute | solution.py:379
  101.6 4.9 %project.5 = bf16[512,640]{1,0:T(8,128)(2,1)} custom-call(s32[3]{0:T(128)S(1)} %get-tuple-element.101.place_ref, bf16[896,768]{1,0:T(8,128)(2,1)S(1)} %get-tuple-element.83.keep_ref, bf16[128,768]{1,0:T(8,128)(2,1)S(1)} %collective-permute-done.6.came_ref, bf16[896,768]{1,0:T(8,128)(2,1)S(1)} %collective-permute-done.8.peer_keep_ref, ...), custom_call_target="tpu_custom_call" | custom-call | flops 1000 | bytes 1000 | tf_op jit(solution)/shard_map/project/pallas_call | solution.py:257
  106.5 4.0 %collective-permute-start.12 = (bf16[512,640]{1,0:T(8,128)(2,1)}, bf16[512,640]{1,0:T(8,128)(2,1)}, u32[]{:S(2)}, u32[]{:S(2)}) collective-permute-start(bf16[512,640]{1,0:T(8,128)(2,1)} %project.5), channel_id=1, source_target_pairs={{2,0},{4,6},{10,8},{12,14},{3,1},{5,7},{11,9},{13,15},{18,16},{20,... | collective-permute-start | bytes 1966088 | tf_op jit(solution)/shard_map/ppermute | solution.py:413
  110.5 4.0 %project.6 = bf16[512,640]{1,0:T(8,128)(2,1)} custom-call(s32[3]{0:T(128)S(1)} %get-tuple-element.100.place_ref, bf16[896,768]{1,0:T(8,128)(2,1)S(1)} %get-tuple-element.83.keep_ref, bf16[128,768]{1,0:T(8,128)(2,1)S(1)} %collective-permute-done.6.came_ref, bf16[896,768]{1,0:T(8,128)(2,1)S(1)} %collective-permute-done.8.peer_keep_ref, ...), custom_call_target="tpu_custom_call" | custom-call | flops 1000 | bytes 1000 | tf_op jit(solution)/shard_map/project/pallas_call | solution.py:257
  116.0 2.5 %select_select_fusion.refs_0_ = bf16[768,512]{1,0:T(8,128)(2,1)} fusion(bf16[768,640]{1,0:T(8,128)(2,1)} %collective-permute-done.3, bf16[768,640]{1,0:T(8,128)(2,1)S(1)} %collective-permute-done.16, bf16[768,640]{1,0:T(8,128)(2,1)} %collective-permute-done.2, bf16[768,640]{1,0:T(8,128)(2,1)S(1)} %collective-permute-done.17, pred[]{:T(512)S(6)} %eq.37, ...), kind=kLoop, calls=%fused_computation.9 | loop fusion | flops 1179648 | bytes 3932163 | tf_op jit(solution)/shard_map/jit(_where)/select_n | solution.py:287
  119.8 4.0 %project.7 = bf16[512,640]{1,0:T(8,128)(2,1)} custom-call(s32[3]{0:T(128)S(1)} %get-tuple-element.99.place_ref, bf16[896,768]{1,0:T(8,128)(2,1)S(1)} %get-tuple-element.83.keep_ref, bf16[128,768]{1,0:T(8,128)(2,1)S(1)} %collective-permute-done.6.came_ref, bf16[896,768]{1,0:T(8,128)(2,1)S(1)} %collective-permute-done.8.peer_keep_ref, ...), custom_call_target="tpu_custom_call" | custom-call | flops 1000 | bytes 1000 | tf_op jit(solution)/shard_map/project/pallas_call | solution.py:257
  123.8 5.5 %collective-permute-start.19 = (bf16[512,640]{1,0:T(8,128)(2,1)}, bf16[512,640]{1,0:T(8,128)(2,1)}, u32[]{:S(2)}, u32[]{:S(2)}) collective-permute-start(bf16[512,640]{1,0:T(8,128)(2,1)} %project.7), channel_id=1, source_target_pairs={{0,2},{4,6},{10,8},{14,12},{1,3},{5,7},{11,9},{15,13},{16,18},{20,... | collective-permute-start | bytes 1966088 | tf_op jit(solution)/shard_map/ppermute | solution.py:413
  129.3 3.4 %collective-permute-start.7 = (bf16[2,128,2560]{2,1,0:T(8,128)(2,1)}, bf16[2,128,2560]{2,1,0:T(8,128)(2,1)}, u32[]{:S(2)}, u32[]{:S(2)}) collective-permute-start(bf16[2,128,2560]{2,1,0:T(8,128)(2,1)} %param.9), channel_id=1, source_target_pairs={{1,0},{4,1},{5,4},{8,5},{9,8},{12,9},{13,12},{3,2},{6,3},{7,6},{10... | collective-permute-start | bytes 3932168 | tf_op jit(solution)/shard_map/ppermute | solution.py:384
  134.0 2.9 %collective-permute-done.21.refs_1_ = bf16[768,512]{1,0:T(8,128)(2,1)} collective-permute-done((bf16[768,512]{1,0:T(8,128)(2,1)}, bf16[768,512]{1,0:T(8,128)(2,1)}, u32[]{:S(2)}, u32[]{:S(2)}) %collective-permute-start.21) | collective-permute-done | bytes 786464 | tf_op jit(solution)/shard_map/ppermute | solution.py:350
  137.0 3.2 %project.8 = bf16[512,512]{1,0:T(8,128)(2,1)S(1)} custom-call(s32[3]{0:T(128)S(1)} %get-tuple-element.98.place_ref, bf16[896,768]{1,0:T(8,128)(2,1)S(1)} %get-tuple-element.83.keep_ref, bf16[128,768]{1,0:T(8,128)(2,1)S(1)} %collective-permute-done.6.came_ref, bf16[896,768]{1,0:T(8,128)(2,1)S(1)} %collective-permute-done.8.peer_keep_ref, ...), custom_call_target="tpu_custom_call" | custom-call | flops 1000 | bytes 1000 | tf_op jit(solution)/shard_map/project/pallas_call | solution.py:257
  141.6 2.9 %add_convert_fusion.1 = (bf16[512,640]{1,0:T(8,128)(2,1)S(1)}, bf16[512,640]{1,0:T(8,128)(2,1)S(1)}) fusion(bf16[512,640]{1,0:T(8,128)(2,1)} %collective-permute-done.12, bf16[512,640]{1,0:T(8,128)(2,1)} %project.5, bf16[512,640]{1,0:T(8,128)(2,1)} %collective-permute-done.13, bf16[512,640]{1,0:T(8,128)(2,1)} %project.6, ...), kind=kLoop, calls=%fused_computation.1 | loop fusion | flops 6881280 | bytes 5242886 | tf_op jit(solution)/shard_map/convert.4
  144.6 3.2 %collective-permute-start.20 = (bf16[256,1280]{1,0:T(8,128)(2,1)S(1)}, bf16[256,1280]{1,0:T(8,128)(2,1)S(1)}, u32[]{:S(2)}, u32[]{:S(2)}) collective-permute-start(bf16[256,1280]{1,0:T(8,128)(2,1)S(1)} %pad_maximum_fusion), channel_id=1, source_target_pairs={{0,1},{1,0},{2,3},{3,2},{4,5},{5,4},{6,7},{7,6},{8,9},{9,8},{10,11... | collective-permute-start | bytes 1966088 | tf_op jit(solution)/shard_map/ppermute | solution.py:445
  150.7 2.4 %collective-permute-done.22 = bf16[512,512]{1,0:T(8,128)(2,1)S(1)} collective-permute-done((bf16[512,512]{1,0:T(8,128)(2,1)S(1)}, bf16[512,512]{1,0:T(8,128)(2,1)S(1)}, u32[]{:S(2)}, u32[]{:S(2)}) %collective-permute-start.22) | collective-permute-done | bytes 524320 | tf_op jit(solution)/shard_map/ppermute | solution.py:413
  153.3 5.4 %collective-permute-start.23 = (bf16[256,512]{1,0:T(8,128)(2,1)S(1)}, bf16[256,512]{1,0:T(8,128)(2,1)S(1)}, u32[]{:S(2)}, u32[]{:S(2)}) collective-permute-start(bf16[256,512]{1,0:T(8,128)(2,1)S(1)} %slice.132), channel_id=1, source_target_pairs={{0,1},{1,0},{2,3},{3,2},{4,5},{5,4},{6,7},{7,6},{8,9},{9,8},{10,11... | collective-permute-start | bytes 786440 | tf_op jit(solution)/shard_map/ppermute | solution.py:449
  (93 shorter events, 31.5 us)
Async XLA Ops:
  0.0 9.2 %copy-start.14 = (s32[2]{0:T(128)S(1)}, s32[2]{0:T(128)}, u32[]{:S(2)}) copy-start(s32[2]{0:T(128)} %param.11) | copy-start | bytes 28
  0.0 9.2 %copy-start.13 = (s32[2]{0:T(128)S(1)}, s32[2]{0:T(128)}, u32[]{:S(2)}) copy-start(s32[2]{0:T(128)} %param.17) | copy-start | bytes 28
  2.3 24.8 %collective-permute-start.2 = (bf16[768,640]{1,0:T(8,128)(2,1)}, bf16[768,640]{1,0:T(8,128)(2,1)}, u32[]{:S(2)}, u32[]{:S(2)}) collective-permute-start(bf16[768,640]{1,0:T(8,128)(2,1)} %dynamic_slice.3), channel_id=1, source_target_pairs={{0,4},{4,8},{8,12},{1,5},{5,9},{9,13},{2,6},{6,10},{10,14},{3,7},{... | collective-permute-start | bytes 2949128 | tf_op jit(solution)/shard_map/ppermute | solution.py:341
  5.5 24.5 %collective-permute-start.3 = (bf16[768,640]{1,0:T(8,128)(2,1)}, bf16[768,640]{1,0:T(8,128)(2,1)}, u32[]{:S(2)}, u32[]{:S(2)}) collective-permute-start(bf16[768,640]{1,0:T(8,128)(2,1)} %dynamic_slice.3), channel_id=1, source_target_pairs={{12,8},{8,4},{4,0},{13,9},{9,5},{5,1},{14,10},{10,6},{6,2},{15,11}... | collective-permute-start | bytes 2949128 | tf_op jit(solution)/shard_map/ppermute | solution.py:341
  14.7 3.8 %collective-permute-start = (bf16[2,2,128,768]{3,2,1,0:T(8,128)(2,1)S(1)}, bf16[2,2,128,768]{3,2,1,0:T(8,128)(2,1)S(1)}, u32[]{:S(2)}, u32[]{:S(2)}) collective-permute-start(bf16[2,2,128,768]{3,2,1,0:T(8,128)(2,1)S(1)} %get-tuple-element.48), channel_id=1, source_target_pairs={{0,1},{1,0},{2,3},{3,2},{4,5},{5,4},{6,7},{7,6},{8,9},{9,8},{10,11... | collective-permute-start | bytes 2359304 | tf_op jit(solution)/shard_map/ppermute | solution.py:359
  16.0 2.5 %collective-permute-start.1 = (bf16[2,128,768]{2,1,0:T(8,128)(2,1)S(1)}, bf16[2,128,768]{2,1,0:T(8,128)(2,1)S(1)}, u32[]{:S(2)}, u32[]{:S(2)}) collective-permute-start(bf16[2,128,768]{2,1,0:T(8,128)(2,1)S(1)} %get-tuple-element.49), channel_id=1, source_target_pairs={{0,1},{1,0},{2,3},{3,2},{4,5},{5,4},{6,7},{7,6},{8,9},{9,8},{10,11... | collective-permute-start | bytes 1179656 | tf_op jit(solution)/shard_map/ppermute | solution.py:359
  30.0 36.7 %collective-permute-start.4 = (bf16[1040,768]{1,0:T(8,128)(2,1)}, bf16[1040,768]{1,0:T(8,128)(2,1)}, u32[]{:S(2)}, u32[]{:S(2)}) collective-permute-start(bf16[1040,768]{1,0:T(8,128)(2,1)} %bundle.1), channel_id=1, source_target_pairs={{4,0},{8,4},{12,8},{5,1},{9,5},{13,9},{6,2},{10,6},{14,10},{7,3},{... | collective-permute-start | bytes 4792328 | tf_op jit(solution)/shard_map/ppermute | solution.py:361
  34.4 32.4 %copy-start.1 = (bf16[768,640]{1,0:T(8,128)(2,1)}, bf16[768,640]{1,0:T(8,128)(2,1)S(1)}, u32[]{:S(2)}) copy-start(bf16[768,640]{1,0:T(8,128)(2,1)S(1)} %broadcast_select_fusion.2.refs_0_) | copy-start | bytes 2949124
  34.4 21.3 %collective-permute-start.5 = (bf16[768,640]{1,0:T(8,128)(2,1)S(1)}, bf16[768,640]{1,0:T(8,128)(2,1)}, u32[]{:S(2)}, u32[]{:S(2)}) collective-permute-start(bf16[768,640]{1,0:T(8,128)(2,1)S(1)} %broadcast_select_fusion.2.refs_0_), channel_id=1, source_target_pairs={{0,16},{16,0},{1,17},{17,1},{2,18},{18,2},{3,19},{19,3},{4,20},{20... | collective-permute-start | bytes 2949128 | tf_op jit(solution)/shard_map/ppermute | solution.py:350
  35.9 44.0 %collective-permute-start.10 = (f32[1,2560]{1,0:T(1,128)S(1)}, f32[1,2560]{1,0:T(1,128)S(1)}, u32[]{:S(2)}, u32[]{:S(2)}) collective-permute-start(f32[1,2560]{1,0:T(1,128)S(1)} %fusion.32), channel_id=1, source_target_pairs={{0,2},{2,0},{1,3},{3,1},{4,6},{6,4},{5,7},{7,5},{8,10},{10,8},{9,1... | collective-permute-start | bytes 30728 | tf_op jit(solution)/shard_map/ppermute | solution.py:394
  38.2 50.6 %collective-permute-start.14 = (bf16[768,640]{1,0:T(8,128)(2,1)}, bf16[768,640]{1,0:T(8,128)(2,1)S(1)}, u32[]{:S(2)}, u32[]{:S(2)}) collective-permute-start(bf16[768,640]{1,0:T(8,128)(2,1)} %collective-permute-done.2), channel_id=1, source_target_pairs={{4,8},{8,12},{5,9},{9,13},{6,10},{10,14},{7,11},{11,15},{20,24},{2... | collective-permute-start | bytes 2949128 | tf_op jit(solution)/shard_map/ppermute | solution.py:341
  40.5 48.3 %collective-permute-start.15 = (bf16[768,640]{1,0:T(8,128)(2,1)}, bf16[768,640]{1,0:T(8,128)(2,1)S(1)}, u32[]{:S(2)}, u32[]{:S(2)}) collective-permute-start(bf16[768,640]{1,0:T(8,128)(2,1)} %collective-permute-done.3), channel_id=1, source_target_pairs={{8,4},{4,0},{9,5},{5,1},{10,6},{6,2},{11,7},{7,3},{24,20},{20,16},... | collective-permute-start | bytes 2949128 | tf_op jit(solution)/shard_map/ppermute | solution.py:341
  78.6 10.1 %collective-permute-start.11 = (f32[1,2560]{1,0:T(1,128)S(1)}, f32[1,2560]{1,0:T(1,128)S(1)}, u32[]{:S(2)}, u32[]{:S(2)}) collective-permute-start(f32[1,2560]{1,0:T(1,128)S(1)} %get-tuple-element.60), channel_id=1, source_target_pairs={{0,2},{2,0},{1,3},{3,1},{4,6},{6,4},{5,7},{7,5},{8,10},{10,8},{9,1... | collective-permute-start | bytes 30728 | tf_op jit(solution)/shard_map/ppermute | solution.py:394
  79.9 12.0 %collective-permute-start.6 = (bf16[128,768]{1,0:T(8,128)(2,1)S(1)}, bf16[128,768]{1,0:T(8,128)(2,1)S(1)}, u32[]{:S(2)}, u32[]{:S(2)}) collective-permute-start(bf16[128,768]{1,0:T(8,128)(2,1)S(1)} %get-tuple-element.57), channel_id=1, source_target_pairs={{4,0},{8,4},{12,8},{5,1},{9,5},{13,9},{6,2},{10,6},{14,10},{7,3},{... | collective-permute-start | bytes 589832 | tf_op jit(solution)/shard_map/ppermute | solution.py:371
  82.9 18.7 %collective-permute-start.8 = (bf16[896,768]{1,0:T(8,128)(2,1)S(1)}, bf16[896,768]{1,0:T(8,128)(2,1)S(1)}, u32[]{:S(2)}, u32[]{:S(2)}) collective-permute-start(bf16[896,768]{1,0:T(8,128)(2,1)S(1)} %get-tuple-element.83.keep_ref), channel_id=1, source_target_pairs={{0,1},{1,0},{2,3},{3,2},{4,5},{5,4},{6,7},{7,6},{8,9},{9,8},{10,11... | collective-permute-start | bytes 4128776 | tf_op jit(solution)/shard_map/ppermute | solution.py:379
  92.0 24.1 %collective-permute-start.16 = (bf16[768,640]{1,0:T(8,128)(2,1)S(1)}, bf16[768,640]{1,0:T(8,128)(2,1)S(1)}, u32[]{:S(2)}, u32[]{:S(2)}) collective-permute-start(bf16[768,640]{1,0:T(8,128)(2,1)S(1)} %collective-permute-done.15), channel_id=1, source_target_pairs={{4,0},{5,1},{6,2},{7,3},{20,16},{21,17},{22,18},{23,19}} | collective-permute-start | bytes 2949128 | tf_op jit(solution)/shard_map/ppermute | solution.py:341
  95.0 21.0 %collective-permute-start.17 = (bf16[768,640]{1,0:T(8,128)(2,1)S(1)}, bf16[768,640]{1,0:T(8,128)(2,1)S(1)}, u32[]{:S(2)}, u32[]{:S(2)}) collective-permute-start(bf16[768,640]{1,0:T(8,128)(2,1)S(1)} %collective-permute-done.14), channel_id=1, source_target_pairs={{8,12},{9,13},{10,14},{11,15},{24,28},{25,29},{26,30},{27,31}} | collective-permute-start | bytes 2949128 | tf_op jit(solution)/shard_map/ppermute | solution.py:341
  95.9 23.9 %collective-permute-start.18 = (bf16[768,640]{1,0:T(8,128)(2,1)S(1)}, bf16[768,640]{1,0:T(8,128)(2,1)S(1)}, u32[]{:S(2)}, u32[]{:S(2)}) collective-permute-start(bf16[768,640]{1,0:T(8,128)(2,1)S(1)} %broadcast_select_fusion.1.refs_0_), channel_id=1, source_target_pairs={{0,16},{16,0},{1,17},{17,1},{2,18},{18,2},{3,19},{19,3},{4,20},{20... | collective-permute-start | bytes 2949128 | tf_op jit(solution)/shard_map/ppermute | solution.py:350
  97.2 4.4 %collective-permute-start.9 = (bf16[128,768]{1,0:T(8,128)(2,1)S(1)}, bf16[128,768]{1,0:T(8,128)(2,1)S(1)}, u32[]{:S(2)}, u32[]{:S(2)}) collective-permute-start(bf16[128,768]{1,0:T(8,128)(2,1)S(1)} %collective-permute-done.6.came_ref), channel_id=1, source_target_pairs={{0,1},{1,0},{2,3},{3,2},{4,5},{5,4},{6,7},{7,6},{8,9},{9,8},{10,11... | collective-permute-start | bytes 589832 | tf_op jit(solution)/shard_map/ppermute | solution.py:379
  101.6 8.9 %copy-start = (bf16[1536,1280]{1,0:T(8,128)(2,1)S(1)}, bf16[1536,1280]{1,0:T(8,128)(2,1)}, u32[]{:S(2)}) copy-start(bf16[1536,1280]{1,0:T(8,128)(2,1)} %refs_0_.1) | copy-start | bytes 11796484
  106.5 27.5 %collective-permute-start.12 = (bf16[512,640]{1,0:T(8,128)(2,1)}, bf16[512,640]{1,0:T(8,128)(2,1)}, u32[]{:S(2)}, u32[]{:S(2)}) collective-permute-start(bf16[512,640]{1,0:T(8,128)(2,1)} %project.5), channel_id=1, source_target_pairs={{2,0},{4,6},{10,8},{12,14},{3,1},{5,7},{11,9},{13,15},{18,16},{20,... | collective-permute-start | bytes 1966088 | tf_op jit(solution)/shard_map/ppermute | solution.py:413
  114.5 18.2 %collective-permute-start.13 = (bf16[512,640]{1,0:T(8,128)(2,1)}, bf16[512,640]{1,0:T(8,128)(2,1)}, u32[]{:S(2)}, u32[]{:S(2)}) collective-permute-start(bf16[512,640]{1,0:T(8,128)(2,1)} %project.6), channel_id=1, source_target_pairs={{2,0},{6,4},{8,10},{12,14},{3,1},{7,5},{9,11},{13,15},{18,16},{22,... | collective-permute-start | bytes 1966088 | tf_op jit(solution)/shard_map/ppermute | solution.py:413
  118.5 18.5 %collective-permute-start.21 = (bf16[768,512]{1,0:T(8,128)(2,1)}, bf16[768,512]{1,0:T(8,128)(2,1)}, u32[]{:S(2)}, u32[]{:S(2)}) collective-permute-start(bf16[768,512]{1,0:T(8,128)(2,1)} %select_select_fusion.refs_0_), channel_id=1, source_target_pairs={{0,16},{16,0},{1,17},{17,1},{2,18},{18,2},{3,19},{19,3},{4,20},{20... | collective-permute-start | bytes 2359304 | tf_op jit(solution)/shard_map/ppermute | solution.py:350
  123.8 17.7 %collective-permute-start.19 = (bf16[512,640]{1,0:T(8,128)(2,1)}, bf16[512,640]{1,0:T(8,128)(2,1)}, u32[]{:S(2)}, u32[]{:S(2)}) collective-permute-start(bf16[512,640]{1,0:T(8,128)(2,1)} %project.7), channel_id=1, source_target_pairs={{0,2},{4,6},{10,8},{14,12},{1,3},{5,7},{11,9},{15,13},{16,18},{20,... | collective-permute-start | bytes 1966088 | tf_op jit(solution)/shard_map/ppermute | solution.py:413
  129.3 29.3 %collective-permute-start.7 = (bf16[2,128,2560]{2,1,0:T(8,128)(2,1)}, bf16[2,128,2560]{2,1,0:T(8,128)(2,1)}, u32[]{:S(2)}, u32[]{:S(2)}) collective-permute-start(bf16[2,128,2560]{2,1,0:T(8,128)(2,1)} %param.9), channel_id=1, source_target_pairs={{1,0},{4,1},{5,4},{8,5},{9,8},{12,9},{13,12},{3,2},{6,3},{7,6},{10... | collective-permute-start | bytes 3932168 | tf_op jit(solution)/shard_map/ppermute | solution.py:384
  132.7 15.0 %collective-permute-start.24 = (bf16[768,128]{1,0:T(8,128)(2,1)S(1)}, bf16[768,128]{1,0:T(8,128)(2,1)S(1)}, u32[]{:S(2)}, u32[]{:S(2)}) collective-permute-start(bf16[768,128]{1,0:T(8,128)(2,1)S(1)} %select_select_fusion.1.refs_0_), channel_id=1, source_target_pairs={{0,16},{16,0},{1,17},{17,1},{2,18},{18,2},{3,19},{19,3},{4,20},{20... | collective-permute-start | bytes 589832 | tf_op jit(solution)/shard_map/ppermute | solution.py:350
  140.2 12.9 %collective-permute-start.22 = (bf16[512,512]{1,0:T(8,128)(2,1)S(1)}, bf16[512,512]{1,0:T(8,128)(2,1)S(1)}, u32[]{:S(2)}, u32[]{:S(2)}) collective-permute-start(bf16[512,512]{1,0:T(8,128)(2,1)S(1)} %project.8), channel_id=1, source_target_pairs={{0,2},{6,4},{8,10},{14,12},{1,3},{7,5},{9,11},{15,13},{16,18},{22,... | collective-permute-start | bytes 1572872 | tf_op jit(solution)/shard_map/ppermute | solution.py:413
  144.6 15.7 %collective-permute-start.20 = (bf16[256,1280]{1,0:T(8,128)(2,1)S(1)}, bf16[256,1280]{1,0:T(8,128)(2,1)S(1)}, u32[]{:S(2)}, u32[]{:S(2)}) collective-permute-start(bf16[256,1280]{1,0:T(8,128)(2,1)S(1)} %pad_maximum_fusion), channel_id=1, source_target_pairs={{0,1},{1,0},{2,3},{3,2},{4,5},{5,4},{6,7},{7,6},{8,9},{9,8},{10,11... | collective-permute-start | bytes 1966088 | tf_op jit(solution)/shard_map/ppermute | solution.py:445
  149.2 9.4 %copy-start.10 = (bf16[2,128,2560]{2,1,0:T(8,128)(2,1)S(1)}, bf16[2,128,2560]{2,1,0:T(8,128)(2,1)}, u32[]{:S(2)}) copy-start(bf16[2,128,2560]{2,1,0:T(8,128)(2,1)} %param.15) | copy-start | bytes 3932164
  149.3 10.9 %collective-permute-start.25 = (bf16[512,128]{1,0:T(8,128)(2,1)S(1)}, bf16[512,128]{1,0:T(8,128)(2,1)S(1)}, u32[]{:S(2)}, u32[]{:S(2)}) collective-permute-start(bf16[512,128]{1,0:T(8,128)(2,1)S(1)} %project.9), channel_id=1, source_target_pairs={{0,2},{6,4},{8,10},{14,12},{1,3},{7,5},{9,11},{15,13},{16,18},{22,... | collective-permute-start | bytes 393224 | tf_op jit(solution)/shard_map/ppermute | solution.py:413
  153.3 7.0 %collective-permute-start.23 = (bf16[256,512]{1,0:T(8,128)(2,1)S(1)}, bf16[256,512]{1,0:T(8,128)(2,1)S(1)}, u32[]{:S(2)}, u32[]{:S(2)}) collective-permute-start(bf16[256,512]{1,0:T(8,128)(2,1)S(1)} %slice.132), channel_id=1, source_target_pairs={{0,1},{1,0},{2,3},{3,2},{4,5},{5,4},{6,7},{7,6},{8,9},{9,8},{10,11... | collective-permute-start | bytes 786440 | tf_op jit(solution)/shard_map/ppermute | solution.py:449
  160.2 1.3 collective-permute-start.26
  (10 other events, 23.8 us)
